TPU v7x, 256 devices: a whole 4x4x8 slice. The times are simulated.
256 devices in a mesh: seq: 64 (over y, z_lo, x), chan: 4 (over z_hi, core).
Axes of the slice: x: 4, y: 4, z: 8 (z_hi: 2, z_lo: 4; z = z_hi * 4 + z_lo), core: 2. Of those that a mesh axis runs over, the one named last changes fastest.
Arguments:
- query_input: bfloat16 [16384, 4096], P('seq', 'chan'), may hold values from -6 to 6
- key_input: bfloat16 [16384, 4096], P('seq', 'chan'), may hold values from -6 to 6
- value_input: bfloat16 [16384, 4096], P('seq', 'chan'), may hold values from -6 to 6
- spectra: float32 [2, 128, 256, 4096], P(None, 'seq', None, 'chan'), may hold values from -4 to 4
- skip_gain: float32 [4096], P('chan'), may hold values from 0.5 to 1.5
- proj_weight: bfloat16 [4096, 4096], P(('chan', 'seq')), may hold values from -0.09375 to 0.09375
Outputs:
- mixed: bfloat16 [16384, 4096], P('seq', 'chan')
All inputs are finite; a program needn't handle non-finite values.
Results may differ from a plain program's by a relative error of at most 0.0049.
Values may be sent and summed in bfloat16 or wider, within the bound.
No kernel may reach another device: no remote copies, remote signals or barrier semaphores. Data moves between devices by JAX's collectives and lax.ppermute only.
A program may use at most 128 MiB of HBM per device.

v0:
```python
import math

import jax
import jax.numpy as jnp
from jax import lax
from jax.sharding import PartitionSpec as P

precise = lax.Precision.HIGHEST


def phase_tables(row_ids, col_ids, modulus):
    turn_count = row_ids[:, None] * col_ids[None, :] % modulus
    phase_angle = turn_count.astype(jnp.float32) * (2.0 * math.pi / modulus)
    return (jnp.cos(phase_angle), jnp.sin(phase_angle))


def rotate(real_part, imag_part, cos_table, sin_table, sign_value):
    return (
        real_part * cos_table - sign_value * imag_part * sin_table,
        imag_part * cos_table + sign_value * real_part * sin_table,
    )


def contract(matrix, operand):
    return jnp.einsum("qr,crh->cqh", matrix, operand, precision=precise)


def row_section(real_part, imag_part, cos_table, sin_table, sign_value):
    new_real = contract(cos_table, real_part) - sign_value * contract(sin_table, imag_part)
    new_imag = contract(cos_table, imag_part) + sign_value * contract(sin_table, real_part)
    return (new_real, new_imag)


def filter_spectrum(real_part, imag_part, spectra):
    return (
        real_part * spectra[0] - imag_part * spectra[1],
        real_part * spectra[1] + imag_part * spectra[0],
    )


def first_section(blocks, block_count):
    used_count = blocks.shape[0]
    cos_table, sin_table = phase_tables(
        jnp.arange(block_count, dtype=jnp.int32),
        jnp.arange(used_count, dtype=jnp.int32),
        block_count,
    )
    flattened = blocks.reshape(used_count, -1)
    tail_shape = (block_count,) + blocks.shape[1:]
    real_part = jnp.dot(cos_table, flattened, precision=precise).reshape(tail_shape)
    imag_part = -jnp.dot(sin_table, flattened, precision=precise).reshape(tail_shape)
    return (real_part, imag_part)


def last_section(real_part, imag_part, used_count, inverse_scale):
    block_count = real_part.shape[0]
    cos_table, sin_table = phase_tables(
        jnp.arange(used_count, dtype=jnp.int32),
        jnp.arange(block_count, dtype=jnp.int32),
        block_count,
    )
    tail_shape = (used_count,) + real_part.shape[1:]
    result = jnp.dot(cos_table, real_part.reshape(block_count, -1), precision=precise)
    result = result - jnp.dot(sin_table, imag_part.reshape(block_count, -1), precision=precise)
    return (result * inverse_scale).reshape(tail_shape)


def split_positions(conv_input, spectra):
    tok_rows = conv_input.shape[0]
    seq_count = lax.axis_size("seq")
    block_count = 2 * seq_count
    slab_rows = tok_rows // seq_count
    full_len = block_count * tok_rows
    seq_index = lax.axis_index("seq")
    all_rows = jnp.arange(tok_rows, dtype=jnp.int32)
    block_ids = jnp.arange(block_count, dtype=jnp.int32)
    blocks = lax.all_to_all(conv_input[None], "seq", split_axis=1, concat_axis=0, tiled=True)
    real_part, imag_part = first_section(blocks, block_count)
    here_rows = seq_index * slab_rows + jnp.arange(slab_rows, dtype=jnp.int32)
    cos_table, sin_table = phase_tables(block_ids, here_rows, full_len)
    real_part, imag_part = rotate(
        real_part, imag_part, cos_table[:, :, None], sin_table[:, :, None], -1.0
    )
    spread = lax.all_to_all(
        jnp.stack([real_part, imag_part]), "seq", split_axis=1, concat_axis=2, tiled=True
    )
    cos_rows, sin_rows = phase_tables(all_rows, all_rows, tok_rows)
    real_part, imag_part = row_section(spread[0], spread[1], cos_rows, sin_rows, -1.0)
    real_part, imag_part = filter_spectrum(real_part, imag_part, spectra)
    real_part, imag_part = row_section(real_part, imag_part, cos_rows, sin_rows, 1.0)
    here_blocks = seq_index * 2 + jnp.arange(2, dtype=jnp.int32)
    cos_table, sin_table = phase_tables(here_blocks, all_rows, full_len)
    real_part, imag_part = rotate(
        real_part, imag_part, cos_table[:, :, None], sin_table[:, :, None], 1.0
    )
    gathered = lax.all_to_all(
        jnp.stack([real_part, imag_part]), "seq", split_axis=2, concat_axis=1, tiled=True
    )
    filtered = last_section(gathered[0], gathered[1], seq_count, 1.0 / full_len)
    return lax.all_to_all(filtered, "seq", split_axis=0, concat_axis=1, tiled=True)[0]


def local(query_input, key_input, value_input, spectra, skip_gain, proj_weight):
    tok_rows = query_input.shape[0]
    conv_input = key_input.astype(jnp.float32) * value_input.astype(jnp.float32)
    filtered = split_positions(conv_input, spectra)
    gated = (query_input.astype(jnp.float32) * (filtered + skip_gain[None, :] * conv_input)).astype(
        jnp.bfloat16
    )
    contract_dims = (((1,), (1,)), ((), ()))
    local_cols = lax.all_to_all(proj_weight, "chan", split_axis=1, concat_axis=0, tiled=True)
    partials = lax.dot_general(
        gated,
        lax.all_gather(local_cols, "seq", axis=0, tiled=True),
        contract_dims,
        preferred_element_type=jnp.float32,
    )
    seq_count = lax.axis_size("seq")
    chan_count = lax.axis_size("chan")
    col_width = proj_weight.shape[0]
    ordered = partials.reshape(tok_rows, seq_count, chan_count, col_width)
    ordered = ordered.transpose(0, 2, 1, 3).reshape(tok_rows, seq_count * chan_count * col_width)
    mixed = lax.psum_scatter(ordered, "chan", scatter_dimension=1, tiled=True)
    return mixed.astype(jnp.bfloat16)


def solution(mesh):
    return jax.shard_map(
        local,
        mesh=mesh,
        in_specs=(
            P("seq", "chan"),
            P("seq", "chan"),
            P("seq", "chan"),
            P(None, "seq", None, "chan"),
            P("chan"),
            P(("chan", "seq"), None),
        ),
        out_specs=P("seq", "chan"),
        check_vma=False,
    )
```

profile of v0, /device:TPU:1, one launch (start us, length us, event | category | flops | bytes accessed | tf_op | source)
XLA Modules:
  0.0 560.8 jit_solution(14219284940023856415)
XLA Ops:
  6.5 1.4 convert_multiply_fusion
  8.0 1.7 broadcast_in_dim.2
  9.7 12.6 %all-to-all-start = ((f32[1,256,1024]{2,0,1:T(1,128)}), f32[1,256,1024]{2,0,1:T(1,128)S(1)}, u32[]{:S(2)}, u32[]{:S(2)}) async-start(f32[1,256,1024]{2,0,1:T(1,128)} %broadcast_in_dim.2), calls=%async_computation | async-start | bytes 2097152 | tf_op jit(solution)/shard_map/all_to_all | solution.py:77
  22.3 0.7 copy.81
  23.0 27.3 %all-to-all-done = f32[1,256,1024]{2,0,1:T(1,128)S(1)} async-done(((f32[1,256,1024]{2,0,1:T(1,128)}), f32[1,256,1024]{2,0,1:T(1,128)S(1)}, u32[]{:S(2)}, u32[]{:S(2)}) %all-to-all-start) | async-done | bytes 1048608 | tf_op jit(solution)/shard_map/all_to_all | solution.py:77
  50.3 8.0 %all-to-all-start.4 = ((bf16[16,4,1024]{2,0,1:T(8,128)(2,1)}), bf16[16,4,1024]{2,0,1:T(8,128)(2,1)S(1)}, u32[]{:S(2)}, u32[]{:S(2)}) async-start(bf16[16,4,1024]{2,0,1:T(8,128)(2,1)} %bitcast.107), calls=%async_computation.4 | async-start | bytes 262144 | tf_op jit(solution)/shard_map/all_to_all | solution.py:111
  58.3 2.5 reduce
  60.8 0.5 reshape.148
  61.3 2.0 fusion.3
  63.3 2.4 subtract_bitcast_fusion.1
  66.0 4.6 copy.45
  70.6 0.7 copy-done.5
  71.3 5.7 %all-to-all-start.1 = ((f32[2,128,4,1024]{3,2,0,1:T(4,128)}), f32[2,128,4,1024]{3,2,0,1:T(4,128)}, u32[]{:S(2)}, u32[]{:S(2)}) async-start(f32[2,128,4,1024]{3,2,0,1:T(4,128)} %copy.45), calls=%async_computation.1 | async-start | bytes 8388608 | tf_op jit(solution)/shard_map/all_to_all | solution.py:84
  77.0 0.7 all-gather.2.cloned.1.call-update
  78.0 4.0 fusion.120
  81.9 2.9 copy.62
  84.8 1.8 copy.63
  86.8 103.7 %all-to-all-done.1 = f32[2,128,4,1024]{3,2,0,1:T(4,128)} async-done(((f32[2,128,4,1024]{3,2,0,1:T(4,128)}), f32[2,128,4,1024]{3,2,0,1:T(4,128)}, u32[]{:S(2)}, u32[]{:S(2)}) %all-to-all-start.1) | async-done | bytes 4194336 | tf_op jit(solution)/shard_map/all_to_all | solution.py:84
  190.5 6.3 %copy.80 = f32[2,64,2,4,1024]{4,2,3,1,0:T(2,128)S(1)} copy(f32[2,64,2,4,1024]{4,3,0,2,1:T(4,128)} %bitcast.5) | data formatting | bytes 8388608 | tf_op jit(solution)/shard_map/all_to_all | solution.py:84
  196.8 3.7 fusion.121
  200.4 2.7 copy.47
  203.2 4.5 copy.48
  207.7 2.8 fusion.24
  210.6 2.8 fusion.22
  213.4 2.8 multiply_subtract_fusion
  216.2 3.1 fusion.2
  219.4 3.0 fusion.18
  222.4 2.8 fusion.20
  225.2 3.0 convolution_add_fusion
  228.1 3.1 subtract_bitcast_fusion
  231.3 2.5 pad_maximum_fusion.1
  233.7 7.4 %copy.53 = f32[2,2,256,1024]{3,1,0,2:T(2,128)} copy(f32[2,2,256,1024]{2,3,1,0:T(8,128)} %pad_maximum_fusion.1) | data formatting | bytes 8388608 | tf_op jit(solution)/shard_map/stack | solution.py:97
  241.1 137.4 %all_to_all.67 = f32[2,2,256,1024]{3,1,0,2:T(2,128)S(1)} all-to-all(f32[2,2,256,1024]{3,1,0,2:T(2,128)} %copy.53), channel_id=1, replica_groups=mesh['seq'=64,'chan'=4] {'seq'}, dimensions={2} | all-to-all | bytes 8388608 | tf_op jit(solution)/shard_map/all_to_all | solution.py:96
  378.5 1.5 copy.54
  380.1 1.6 fusion.119
  381.7 1.0 copy.55
  382.7 1.6 copy.66
  384.3 1.0 copy.56
  385.3 1.6 copy.67
  386.9 1.3 fusion.52
  388.3 1.4 fusion
  389.7 1.0 reshape.149
  390.7 45.3 %all_to_all.68 = f32[64,4,1024]{2,1,0:T(4,128)S(1)} all-to-all(f32[64,4,1024]{2,1,0:T(4,128)S(1)} %reshape.149), channel_id=1, replica_groups=mesh['seq'=64,'chan'=4] {'seq'}, dimensions={0} | all-to-all | bytes 2097152 | tf_op jit(solution)/shard_map/all_to_all | solution.py:100
  436.4 6.1 %fusion.9 = f32[256,4096]{0,1:T(8,128)S(1)} fusion(bf16[4096,1024]{1,0:T(8,128)(2,1)} %all-gather.2.cloned.1.call-done, f32[256,1024]{1,0:T(8,128)S(1)} %squeeze.21, bf16[256,1024]{1,0:T(8,128)(2,1)} %param.6, f32[1024]{0:T(1024)S(1)} %copy-done.6, bf16[256,1024]{1,0:T(8,128)(2,1)S(1)} %copy-done.3, bf16[256,1024]{1,0:T(8,128)(2,1)S(1)} %copy-done.4), kind=kOutput, calls=%fused_computation.27 | convolution fusion | flops 2149580800 | bytes 15208448 | tf_op jit(solution)/shard_map/dot_general | solution.py:112
  442.5 2.4 copy.59
  444.9 106.3 %reduce-scatter.2.cloned.1.call-done = f32[256,1024]{0,1:T(8,128)} async-done(((f32[256,4096]{0,1:T(8,128)}), f32[256,1024]{0,1:T(8,128)}) %reduce-scatter.2.cloned.1.call-update) | async-done | bytes 1048592 | tf_op jit(solution)/shard_map/reduce_scatter | solution.py:123
  551.2 1.3 convert_element_type.71
  552.5 1.0 copy.60
  (26 shorter events, 1.3 us)
Async XLA Ops:
  8.0 14.3 %copy-start.7 = (bf16[16,4096]{1,0:T(8,128)(2,1)S(1)}, bf16[16,4096]{1,0:T(8,128)(2,1)}, u32[]{:S(2)}) copy-start(bf16[16,4096]{1,0:T(8,128)(2,1)} %param.11) | copy-start | bytes 393220
  9.7 40.7 %all-to-all-start = ((f32[1,256,1024]{2,0,1:T(1,128)}), f32[1,256,1024]{2,0,1:T(1,128)S(1)}, u32[]{:S(2)}, u32[]{:S(2)}) async-start(f32[1,256,1024]{2,0,1:T(1,128)} %broadcast_in_dim.2), calls=%async_computation | async-start | bytes 2097152 | tf_op jit(solution)/shard_map/all_to_all | solution.py:77
  50.3 20.3 %all-to-all-start.4 = ((bf16[16,4,1024]{2,0,1:T(8,128)(2,1)}), bf16[16,4,1024]{2,0,1:T(8,128)(2,1)S(1)}, u32[]{:S(2)}, u32[]{:S(2)}) async-start(bf16[16,4,1024]{2,0,1:T(8,128)(2,1)} %bitcast.107), calls=%async_computation.4 | async-start | bytes 262144 | tf_op jit(solution)/shard_map/all_to_all | solution.py:111
  70.6 0.7 copy-start.5
  71.3 119.2 %all-to-all-start.1 = ((f32[2,128,4,1024]{3,2,0,1:T(4,128)}), f32[2,128,4,1024]{3,2,0,1:T(4,128)}, u32[]{:S(2)}, u32[]{:S(2)}) async-start(f32[2,128,4,1024]{3,2,0,1:T(4,128)} %copy.45), calls=%async_computation.1 | async-start | bytes 8388608 | tf_op jit(solution)/shard_map/all_to_all | solution.py:84
  77.0 359.4 %all-gather.2.cloned.1.call-start = ((), (), s32[]{:S(2)}) async-start(), calls=%async_computation.6 | async-start | bytes 8519680 | tf_op jit(solution)/shard_map/all_gather | solution.py:114
  77.7 473.5 %reduce-scatter.2.cloned.1.call-start = ((), (), s32[]{:S(2)}) async-start(), calls=%async_computation.7 | async-start | bytes 5242880 | tf_op jit(solution)/shard_map/reduce_scatter | solution.py:123
  207.7 2.9 copy-start
  213.4 2.8 copy-start.1
  213.4 2.8 copy-start.2
  390.6 45.7 %copy-start.3 = (bf16[256,1024]{1,0:T(8,128)(2,1)S(1)}, bf16[256,1024]{1,0:T(8,128)(2,1)}, u32[]{:S(2)}) copy-start(bf16[256,1024]{1,0:T(8,128)(2,1)} %param.8) | copy-start | bytes 1572868
  390.6 45.7 %copy-start.4 = (bf16[256,1024]{1,0:T(8,128)(2,1)S(1)}, bf16[256,1024]{1,0:T(8,128)(2,1)}, u32[]{:S(2)}) copy-start(bf16[256,1024]{1,0:T(8,128)(2,1)} %param.7) | copy-start | bytes 1572868
  390.7 45.7 %copy-start.6 = (f32[1024]{0:T(1024)S(1)}, f32[1024]{0:T(1024)}, u32[]{:S(2)}) copy-start(f32[1024]{0:T(1024)} %param.10) | copy-start | bytes 12292
Sparse Core Ops, SparseCore 0:
  79.6 347.5 all-gather.1
  445.0 106.1 reduce-scatter.1
where the time goes:
time: 571 us; the launch traced here: 561 us
  waiting for transfers between devices  238 us (42%)
  blocking collectives  183 us (32%)
  local copies, waits for them, and re-layouts  54.6 us (10%)
  matrix products  36.6 us (6%)
  starting transfers between devices  26.5 us (5%)
  between operations  14.2 us (2%)
  other arithmetic  8.2 us (1%)
    all_to_all x1, blocking collectives, split_positions(): lax.all_to_all(jnp.stack([real_part, imag_part]), 'seq', split_axis=2, co...  137 us
    reduce_scatter x1, waiting for transfers between devices, local(): mixed = lax.psum_scatter(ordered, 'chan', scatter_dimension=1, tiled=True)  106 us
    all_to_all x1, waiting for transfers between devices, split_positions(): lax.all_to_all(jnp.stack([real_part, imag_part]), 'seq', split_axis=1, co...  104 us
    all_to_all x1, blocking collectives, split_positions(): lax.all_to_all(filtered, 'seq', split_axis=0, concat_axis=1, tiled=True)[0]  45.3 us
    all_to_all x1, waiting for transfers between devices, split_positions(): lax.all_to_all(conv_input[None], 'seq', split_axis=1, concat_axis=0, tile...  27.3 us
    dot_general x8, matrix products, contract(): return jnp.einsum('qr,crh->cqh', matrix, operand, precision=precise)  23.4 us
    all_to_all x1, starting transfers between devices, split_positions(): lax.all_to_all(conv_input[None], 'seq', split_axis=1, concat_axis=0, tile...  12.6 us
    another operation x2, local copies, waits for them, and re-layouts, split_positions(): jnp.stack([real_part, imag_part])  12 us
  transfers between devices with their start and end apart: 5, of which 3 were waited for; matrix products, arithmetic and copies ran while one was open for 15% of the time, Pallas kernels for 0%

commit v1 on v0

v1 whole, which is shorter than its diff:
```python
import numpy as np

import jax
import jax.numpy as jnp
import ml_dtypes
from jax import lax
from jax.experimental import pallas as pl
from jax.experimental.pallas import tpu as pltpu
from jax.sharding import Mesh, PartitionSpec as P

BF, F32 = jnp.bfloat16, jnp.float32
SEQ = ("y", "z", "x")
TOK, NSEQ, CLASSES = 256, 64, 128
FULL = CLASSES * TOK


def split(table):
    hi = table.astype(ml_dtypes.bfloat16)
    lo = (table - hi.astype(np.float64)).astype(ml_dtypes.bfloat16)
    return hi, lo


def tables():
    classes = np.concatenate([np.arange(0, CLASSES, 2), np.arange(1, CLASSES, 2)])
    blocks, rows = np.arange(NSEQ), np.arange(TOK)
    turn = 2 * np.pi * (classes[:, None] * blocks[None, :] % CLASSES) / CLASSES
    fwd_hi, fwd_lo = split(np.concatenate([np.cos(turn), -np.sin(turn)], 0))
    first = np.concatenate([fwd_hi, fwd_lo], 1)
    inv = np.concatenate([np.cos(turn.T), -np.sin(turn.T)], 1) / FULL
    last = np.concatenate(split(inv), 0)
    turn = 2 * np.pi * (rows[:, None] * rows[None, :] % TOK) / TOK
    row_hi, row_lo = split(np.concatenate([np.cos(turn), np.sin(turn)], 0))
    turn = 2 * np.pi * (classes[:, None] * rows[None, :]) / FULL
    return first, last, row_hi, row_lo, np.cos(turn).astype(np.float32), np.sin(turn).astype(np.float32)


def dot(a, b):
    return lax.dot_general(a, b, (((1,), (0,)), ((), ())), preferred_element_type=F32)


def parts(value):
    hi = value.astype(BF)
    return hi, (value - hi.astype(F32)).astype(BF)


def prep_kernel(k_ref, v_ref, s_ref, o_ref):
    conv = k_ref[...].astype(F32) * v_ref[...].astype(F32)
    o_ref[:, :TOK] = conv.T.astype(BF)
    for j in range(4):
        o_ref[:, TOK * (j + 1) : TOK * (j + 2)] = s_ref[j].T.astype(BF)


def prep(key, value, spectra):
    width = key.shape[1]
    blk = 128
    return pl.pallas_call(
        prep_kernel,
        grid=(width // blk,),
        in_specs=[
            pl.BlockSpec((TOK, blk), lambda i: (0, i)),
            pl.BlockSpec((TOK, blk), lambda i: (0, i)),
            pl.BlockSpec((4, TOK, blk), lambda i: (0, 0, i)),
        ],
        out_specs=pl.BlockSpec((blk, 5 * TOK), lambda i: (i, 0)),
        out_shape=jax.ShapeDtypeStruct((width, 5 * TOK), BF),
        compiler_params=pltpu.CompilerParams(vmem_limit_bytes=32 << 20),
        name="prep",
    )(key, value, spectra)


GROUP = 2


def fft_kernel(r_ref, first_ref, last_ref, hi_ref, lo_ref, tc_ref, ts_ref, o_ref, xs, ys):
    chans = r_ref.shape[0] // NSEQ

    def widen(i, _):
        rows = pl.ds(pl.multiple_of(i * 64, 64), 64)
        for c in range(10):
            xs[c, rows, :] = r_ref[rows, c * 128 : c * 128 + 128].astype(F32)
        return 0

    lax.fori_loop(0, r_ref.shape[0] // 64, widen, 0)
    first, last = first_ref[...], last_ref[...]
    hi_table, lo_table = hi_ref[...], lo_ref[...]
    tc, ts = tc_ref[...], ts_ref[...]

    def rows_of(h, col):
        rows = pl.ds(h, NSEQ, stride=chans)
        return jnp.concatenate([xs[2 * col, rows, :], xs[2 * col + 1, rows, :]], 1)

    def row_section(stacked):
        hi, lo = parts(stacked)
        return dot(hi, hi_table) + dot(lo, hi_table) + dot(hi, lo_table)

    def step(g, _):
        stacked = []
        for j in range(GROUP):
            x = rows_of(g * GROUP + j, 0).astype(BF)
            a = dot(first, jnp.concatenate([x, x], 0))
            ar, ai = a[:CLASSES], a[CLASSES:]
            ar, ai = ar * tc + ai * ts, ai * tc - ar * ts
            stacked += [jnp.concatenate([ar, ai], 1), jnp.concatenate([ai, -ar], 1)]
        freq = row_section(jnp.concatenate(stacked, 0))
        stacked = []
        for j in range(GROUP):
            h = g * GROUP + j
            rr = jnp.concatenate([rows_of(h, 1), rows_of(h, 2)], 0)
            ri = jnp.concatenate([rows_of(h, 3), rows_of(h, 4)], 0)
            base = 2 * CLASSES * j
            xr, xi = freq[base : base + CLASSES], freq[base + CLASSES : base + 2 * CLASSES]
            pr, pi = rr * xr - ri * xi, rr * xi + ri * xr
            stacked += [jnp.concatenate([pr, -pi], 1), jnp.concatenate([pi, pr], 1)]
        back = row_section(jnp.concatenate(stacked, 0))
        for j in range(GROUP):
            h = g * GROUP + j
            base = 2 * CLASSES * j
            br, bi = back[base : base + CLASSES], back[base + CLASSES : base + 2 * CLASSES]
            br, bi = br * tc - bi * ts, bi * tc + br * ts
            hi, lo = parts(jnp.concatenate([br, bi], 0))
            both = dot(last, hi)
            y = both[:NSEQ] + both[NSEQ:] + dot(last[:NSEQ], lo)
            for c in range(2):
                ys[c, pl.ds(h, NSEQ, stride=chans), :] = y[:, c * 128 : c * 128 + 128]
        return 0

    lax.fori_loop(0, chans // GROUP, step, 0)
    for c in range(2):
        o_ref[:, c * 128 : c * 128 + 128] = ys[c].astype(BF)


def convolve(received):
    rows = received.shape[0]
    consts = [jnp.asarray(t) for t in tables()]
    return pl.pallas_call(
        fft_kernel,
        in_specs=[pl.BlockSpec(memory_space=pltpu.VMEM)] * 7,
        out_specs=pl.BlockSpec(memory_space=pltpu.VMEM),
        out_shape=jax.ShapeDtypeStruct((rows, TOK), BF),
        scratch_shapes=[pltpu.VMEM((10, rows, 128), F32), pltpu.VMEM((2, rows, 128), F32)],
        compiler_params=pltpu.CompilerParams(vmem_limit_bytes=40 << 20),
        name="convolve",
    )(received, *consts)


def gate_kernel(y_ref, q_ref, k_ref, v_ref, s_ref, o_ref):
    conv = k_ref[...].astype(F32) * v_ref[...].astype(F32)
    filtered = y_ref[...].astype(F32).T
    o_ref[...] = (q_ref[...].astype(F32) * (filtered + s_ref[...] * conv)).astype(BF)


def gate(y, query, key, value, gain):
    width = key.shape[1]
    blk = 128
    tok = pl.BlockSpec((TOK, blk), lambda i: (0, i))
    return pl.pallas_call(
        gate_kernel,
        grid=(width // blk,),
        in_specs=[pl.BlockSpec((blk, TOK), lambda i: (i, 0)), tok, tok, tok, pl.BlockSpec((1, blk), lambda i: (0, i))],
        out_specs=tok,
        out_shape=jax.ShapeDtypeStruct((TOK, width), BF),
        compiler_params=pltpu.CompilerParams(vmem_limit_bytes=32 << 20),
        name="gate",
    )(y, query, key, value, gain)


def project_kernel(order_ref, g0, g1, g2, g3, w_ref, o_ref, acc):
    i = pl.program_id(0)
    for j, g_ref in enumerate((g0, g1, g2, g3)):

        @pl.when(i == j)
        def _():
            g = g_ref[...]
            for y in range(4):
                w = jnp.concatenate([w_ref[y, x, z] for z in range(4) for x in range(4)], 0)
                cols = slice(y * 256, y * 256 + 256)
                term = lax.dot_general(g, w, (((1,), (1,)), ((), ())), preferred_element_type=F32)
                total = term if j == 0 else acc[:, cols] + term
                if j == 3:
                    o_ref[:, cols] = total.astype(BF)
                else:
                    acc[:, cols] = total


def project(order, pieces, weight):
    width = pieces[0].shape[1]
    outs = weight.shape[0] * weight.shape[1] * weight.shape[2] * weight.shape[3]
    whole = pl.BlockSpec((TOK, width), lambda i, order: (0, 0))
    return pl.pallas_call(
        project_kernel,
        grid_spec=pltpu.PrefetchScalarGridSpec(
            num_scalar_prefetch=1,
            grid=(4,),
            in_specs=[whole] * 4
            + [pl.BlockSpec(weight.shape[:4] + (width,), lambda i, order: (0, 0, 0, 0, order[i]))],
            out_specs=pl.BlockSpec((TOK, outs), lambda i, order: (0, 0)),
            scratch_shapes=[pltpu.VMEM((TOK, outs), F32)],
        ),
        out_shape=jax.ShapeDtypeStruct((TOK, outs), BF),
        compiler_params=pltpu.CompilerParams(vmem_limit_bytes=32 << 20),
        name="project",
    )(order, *pieces, weight)


def gather_weight(weight):
    z = lax.axis_index("z")
    from_z = [weight] + [
        lax.ppermute(weight, "z", [(a, (a + d) % 4) for a in range(4)]) for d in (1, 2, 3)
    ]
    stacked = jnp.stack(from_z)
    ordered = jnp.stack([lax.dynamic_index_in_dim(stacked, (z - a) % 4, 0, False) for a in range(4)])
    return lax.all_gather(ordered[None], ("y", "x"), axis=0, tiled=True).reshape(
        (4, 4, 4) + weight.shape
    )


def local(query, key, value, spectra, gain, weight):
    swap = [(0, 1), (1, 0)]
    full_weight = gather_weight(weight)
    send = prep(key, value, spectra.reshape((4,) + spectra.shape[2:]))
    send = send.reshape(NSEQ, -1, send.shape[1])
    received = lax.all_to_all(send, SEQ, split_axis=0, concat_axis=0, tiled=True)
    y = convolve(received.reshape(-1, received.shape[2]))
    y = lax.all_to_all(y.reshape(NSEQ, -1, TOK), SEQ, split_axis=0, concat_axis=0, tiled=True)
    gated = gate(y.reshape(-1, TOK), query, key, value, gain[None, :])
    over_h = lax.ppermute(gated, "h", swap)
    over_k = lax.ppermute(gated, "k", swap)
    over_hk = lax.ppermute(over_h, "k", swap)
    h, k = lax.axis_index("h"), lax.axis_index("k")
    order = jnp.stack([h * 2 + k, h * 2 + 1 - k, (1 - h) * 2 + k, (1 - h) * 2 + 1 - k])
    return project(order.astype(jnp.int32), (gated, over_k, over_h, over_hk), full_weight)


def solution(mesh):
    fine = Mesh(mesh.devices.reshape(4, 4, 4, 2, 2), ("y", "z", "x", "h", "k"))
    chan = ("h", "k")
    return jax.shard_map(
        local,
        mesh=fine,
        in_specs=(
            P(SEQ, chan),
            P(SEQ, chan),
            P(SEQ, chan),
            P(None, SEQ, None, chan),
            P(chan),
            P(chan + SEQ, None),
        ),
        out_specs=P(SEQ, chan),
        check_vma=False,
    )
```

time: 571 us -> 191 us (0.33); the launches traced: 561 us -> 188 us
  waiting for transfers between devices: 238 us -> 23.4 us
  blocking collectives: 183 us -> 93.7 us
  local copies, waits for them, and re-layouts: 54.6 us -> 7.76 us
  matrix products: 36.6 us -> 0 us
  Pallas kernels: 0 us -> 28.5 us
  starting transfers between devices: 26.5 us -> 18.7 us
  other arithmetic: 8.2 us -> 1.91 us
    all_to_all x3 -> x0, waiting for transfers between devices: 131 us -> none  [the longest x1 104 us: split_positions(): lax.all_to_all(jnp.stack([real_part, imag_part]), 'seq', split_axis=1, co...]
    reduce_scatter x1 -> x0, waiting for transfers between devices: 106 us -> none  [local(): mixed = lax.psum_scatter(ordered, 'chan', scatter_dimension=1, tiled=True)]
    all_to_all x2, blocking collectives: 183 us -> 93.7 us  [the longest x1 71 us: local(): lax.all_to_all(send, SEQ, split_axis=0, concat_axis=0, tiled=True)]
    dot_general x13 -> x0, matrix products: 36.6 us -> none  [the longest x8 23.4 us: contract(): return jnp.einsum('qr,crh->cqh', matrix, operand, precision=precise)]
    pallas_call x0 -> x4, Pallas kernels: none -> 28.5 us  [the longest x1 19.7 us: convolve(): pl.pallas_call(fft_kernel, in_specs=[pl.BlockSpec(memory_space=pltpu.VMEM...]
    all_to_all x3 -> x0, starting transfers between devices: 26.2 us -> none  [the longest x1 12.6 us: split_positions(): lax.all_to_all(conv_input[None], 'seq', split_axis=1, concat_axis=0, tile...]
    ppermute x0 -> x6, waiting for transfers between devices: none -> 23.3 us  [the longest x3 10.9 us: gather_weight(): lax.ppermute(weight, 'z', [(a, (a + d) % 4) for a in range(4)])]
    ppermute x0 -> x6, starting transfers between devices: none -> 18.7 us  [the longest x1 5.91 us: local(): over_h = lax.ppermute(gated, 'h', swap)]
  transfers between devices with their start and end apart: 5 -> 7, of which waited for: 3 -> 4; matrix products, arithmetic and copies ran while one was open for 15% -> 0% of each run, Pallas kernels for 0% -> 13%
where the time goes in v1:
time: 191 us; the launch traced here: 188 us
  blocking collectives  93.7 us (49%)
  Pallas kernels  28.5 us (15%)
  waiting for transfers between devices  23.4 us (12%)
  starting transfers between devices  18.7 us (10%)
  between operations  13.6 us (7%)
  local copies, waits for them, and re-layouts  7.76 us (4%)
    all_to_all x1, blocking collectives, local(): lax.all_to_all(send, SEQ, split_axis=0, concat_axis=0, tiled=True)  71 us
    all_to_all x1, blocking collectives, local(): lax.all_to_all(y.reshape(NSEQ, -1, TOK), SEQ, split_axis=0, concat_axis=0...  22.7 us
    pallas_call x1, Pallas kernels, convolve(): pl.pallas_call(fft_kernel, in_specs=[pl.BlockSpec(memory_space=pltpu.VMEM...  19.7 us
    ppermute x3, waiting for transfers between devices, gather_weight(): lax.ppermute(weight, 'z', [(a, (a + d) % 4) for a in range(4)])  10.9 us
    ppermute x1, waiting for transfers between devices, local(): over_h = lax.ppermute(gated, 'h', swap)  10.9 us
    unnamed x28, local copies, waits for them, and re-layouts  7.71 us
    ppermute x1, starting transfers between devices, local(): over_h = lax.ppermute(gated, 'h', swap)  5.91 us
    ppermute x3, starting transfers between devices, gather_weight(): lax.ppermute(weight, 'z', [(a, (a + d) % 4) for a in range(4)])  5.46 us
  transfers between devices with their start and end apart: 7, of which 4 were waited for; matrix products, arithmetic and copies ran while one was open for 0% of the time, Pallas kernels for 13%

profile of v1, /device:TPU:1, one launch (start us, length us, event | category | flops | bytes accessed | tf_op | source)
XLA Modules:
  0.0 187.5 jit_solution(15638489782210625811)
XLA Ops:
  6.5 0.0 all-gather.3.cloned.1.call-start
  6.5 5.2 %collective-permute-start.5 = (bf16[16,4096]{1,0:T(8,128)(2,1)}, bf16[16,4096]{1,0:T(8,128)(2,1)S(1)}, u32[]{:S(2)}, u32[]{:S(2)}) collective-permute-start(bf16[16,4096]{1,0:T(8,128)(2,1)} %param.17), channel_id=1, source_target_pairs={{0,48},{16,0},{32,16},{48,32},{1,49},{17,1},{33,17},{49,33},{2,50}... | collective-permute-start | bytes 393224 | tf_op jit(solution)/shard_map/ppermute | solution.py:208
  11.7 0.0 collective-permute-start.4
  11.7 0.3 collective-permute-start.3
  12.0 2.3 %collective-permute-done.5 = bf16[16,4096]{1,0:T(8,128)(2,1)S(1)} collective-permute-done((bf16[16,4096]{1,0:T(8,128)(2,1)}, bf16[16,4096]{1,0:T(8,128)(2,1)S(1)}, u32[]{:S(2)}, u32[]{:S(2)}) %collective-permute-start.5) | collective-permute-done | bytes 131104 | tf_op jit(solution)/shard_map/ppermute | solution.py:208
  14.3 8.7 %collective-permute-done.4 = bf16[16,4096]{1,0:T(8,128)(2,1)S(1)} collective-permute-done((bf16[16,4096]{1,0:T(8,128)(2,1)}, bf16[16,4096]{1,0:T(8,128)(2,1)S(1)}, u32[]{:S(2)}, u32[]{:S(2)}) %collective-permute-start.4) | collective-permute-done | bytes 131104 | tf_op jit(solution)/shard_map/ppermute | solution.py:208
  22.9 0.0 collective-permute-done.3
  22.9 1.0 pad_maximum_fusion
  24.0 0.9 pad_maximum_fusion.1
  24.8 0.0 all-gather.3.cloned.1.call-update
  24.9 0.0 copy-start.1
  24.9 2.2 %copy-done.1 = f32[2,2,256,1024]{3,2,1,0:T(8,128)S(1)} copy-done((f32[2,2,256,1024]{3,2,1,0:T(8,128)S(1)}, f32[2,2,256,1024]{3,2,1,0:T(8,128)}, u32[]{:S(2)}) %copy-start.1) | copy-done | bytes 4194328
  27.1 1.0 copy-done.2
  28.1 1.0 copy-done.4
  29.1 2.3 %prep.1 = bf16[1024,1280]{1,0:T(8,128)(2,1)S(1)} custom-call(bf16[256,1024]{1,0:T(8,128)(2,1)S(1)} %copy-done.2, bf16[256,1024]{1,0:T(8,128)(2,1)S(1)} %copy-done.4, f32[4,256,1024]{2,1,0:T(8,128)S(1)} %bitcast.18), custom_call_target="tpu_custom_call" | custom-call | tf_op jit(solution)/shard_map/prep/pallas_call | solution.py:56
  31.5 0.0 copy-start.7
  31.5 0.0 copy-start.8
  31.5 0.0 copy-start.9
  31.5 0.0 copy-start.10
  31.5 0.0 copy-start.11
  31.5 0.0 copy-start.12
  31.6 0.0 copy-start.3
  31.6 0.0 copy-start.5
  31.6 0.0 copy-start.6
  31.6 0.0 copy-start.13
  31.6 71.0 %all_to_all.10 = bf16[64,16,1280]{2,1,0:T(8,128)(2,1)S(1)} all-to-all(bf16[64,16,1280]{2,1,0:T(8,128)(2,1)S(1)} %bitcast.16), channel_id=1, replica_groups=mesh['y'=4,'z'=4,'x'=4,'h'=2,'k'=2] {'y','z','x'}, dimensions={0} | all-to-all | bytes 5242880 | tf_op jit(solution)/shard_map/all_to_all | solution.py:222
  102.6 0.0 copy-done.7
  102.6 0.0 copy-done.8
  102.6 0.0 copy-done.9
  102.6 0.0 copy-done.10
  102.6 0.0 copy-done.11
  102.6 0.0 copy-done.12
  102.6 19.7 %convolve.1 = bf16[1024,256]{1,0:T(8,128)(2,1)S(1)} custom-call(bf16[1024,1280]{1,0:T(8,128)(2,1)S(1)} %bitcast.15, bf16[256,128]{1,0:T(8,128)(2,1)S(1)} %copy-done.11, bf16[128,256]{1,0:T(8,128)(2,1)S(1)} %copy-done.12, bf16[512,256]{1,0:T(8,128)(2,1)S(1)} %copy-done.7, bf16[512,256]{1,0:T(8,128)(2,1)S(1)} %copy-done.8, f32[128,256]{1,0:T(8,128)S(1)} %copy-done.9, ...), custom_call_target="tpu_custom_call" | custom-call | tf_op jit(solution)/shard_map/convolve/pallas_call | solution.py:135
  122.4 22.7 %all_to_all.11 = bf16[64,16,256]{2,1,0:T(8,128)(2,1)S(1)} all-to-all(bf16[64,16,256]{2,1,0:T(8,128)(2,1)S(1)} %bitcast.20), channel_id=1, replica_groups=mesh['y'=4,'z'=4,'x'=4,'h'=2,'k'=2] {'y','z','x'}, dimensions={0} | all-to-all | bytes 1048576 | tf_op jit(solution)/shard_map/all_to_all | solution.py:224
  145.0 0.0 copy-done.3
  145.0 0.0 copy-done.5
  145.0 0.0 copy-done.6
  145.0 0.0 copy-done.13
  145.0 1.5 gate.1.g0
  146.5 5.9 %collective-permute-start.1 = (bf16[256,1024]{1,0:T(8,128)(2,1)S(1)}, bf16[256,1024]{1,0:T(8,128)(2,1)S(1)}, u32[]{:S(2)}, u32[]{:S(2)}) collective-permute-start(bf16[256,1024]{1,0:T(8,128)(2,1)S(1)} %gate.1.g0), channel_id=1, source_target_pairs={{0,2},{2,0},{1,3},{3,1},{4,6},{6,4},{5,7},{7,5},{8,10},{10,8},{9,1... | collective-permute-start | bytes 1572872 | tf_op jit(solution)/shard_map/ppermute | solution.py:226
  152.5 2.5 %collective-permute-start = (bf16[256,1024]{1,0:T(8,128)(2,1)S(1)}, bf16[256,1024]{1,0:T(8,128)(2,1)S(1)}, u32[]{:S(2)}, u32[]{:S(2)}) collective-permute-start(bf16[256,1024]{1,0:T(8,128)(2,1)S(1)} %gate.1.g0), channel_id=1, source_target_pairs={{0,1},{1,0},{2,3},{3,2},{4,5},{5,4},{6,7},{7,6},{8,9},{9,8},{10,11... | collective-permute-start | bytes 1572872 | tf_op jit(solution)/shard_map/ppermute | solution.py:227
  154.9 10.9 %collective-permute-done.1.g2 = bf16[256,1024]{1,0:T(8,128)(2,1)S(1)} collective-permute-done((bf16[256,1024]{1,0:T(8,128)(2,1)S(1)}, bf16[256,1024]{1,0:T(8,128)(2,1)S(1)}, u32[]{:S(2)}, u32[]{:S(2)}) %collective-permute-start.1) | collective-permute-done | bytes 524320 | tf_op jit(solution)/shard_map/ppermute | solution.py:226
  165.9 4.9 %collective-permute-start.2 = (bf16[256,1024]{1,0:T(8,128)(2,1)S(1)}, bf16[256,1024]{1,0:T(8,128)(2,1)S(1)}, u32[]{:S(2)}, u32[]{:S(2)}) collective-permute-start(bf16[256,1024]{1,0:T(8,128)(2,1)S(1)} %collective-permute-done.1.g2), channel_id=1, source_target_pairs={{0,1},{1,0},{2,3},{3,2},{4,5},{5,4},{6,7},{7,6},{8,9},{9,8},{10,11... | collective-permute-start | bytes 1572872 | tf_op jit(solution)/shard_map/ppermute | solution.py:228
  170.7 0.1 pad_add_fusion.order_ref
  170.8 0.0 collective-permute-done.g1
  170.8 1.5 collective-permute-done.2.g3
  172.3 3.4 %copy-done = bf16[64,16,4096]{2,1,0:T(8,128)(2,1)S(1)} copy-done((bf16[64,16,4096]{2,1,0:T(8,128)(2,1)S(1)}, bf16[64,16,4096]{2,1,0:T(8,128)(2,1)}, u32[]{:S(2)}) %copy-start) | copy-done | bytes 8388632
  175.7 5.0 %project.1 = bf16[256,1024]{1,0:T(8,128)(2,1)} custom-call(s32[4]{0:T(128)S(1)} %pad_add_fusion.order_ref, bf16[256,1024]{1,0:T(8,128)(2,1)S(1)} %gate.1.g0, bf16[256,1024]{1,0:T(8,128)(2,1)S(1)} %collective-permute-done.g1, bf16[256,1024]{1,0:T(8,128)(2,1)S(1)} %collective-permute-done.1.g2, bf16[256,1024]{1,0:T(8,128)(2,1)S(1)} %collective-permute-done.2.g3, ...), custom_call_target="tpu_custom_call" | custom-call | tf_op jit(solution)/shard_map/project/pallas_call | solution.py:189
  (5 shorter events, 0.1 us)
Async XLA Ops:
  6.5 165.8 %all-gather.3.cloned.1.call-start = ((), (), s32[]{:S(2)}) async-start(), calls=%async_computation.2 | async-start | bytes 8912896 | tf_op jit(solution)/shard_map/all_gather | solution.py:212
  6.5 7.7 %collective-permute-start.5 = (bf16[16,4096]{1,0:T(8,128)(2,1)}, bf16[16,4096]{1,0:T(8,128)(2,1)S(1)}, u32[]{:S(2)}, u32[]{:S(2)}) collective-permute-start(bf16[16,4096]{1,0:T(8,128)(2,1)} %param.17), channel_id=1, source_target_pairs={{0,48},{16,0},{32,16},{48,32},{1,49},{17,1},{33,17},{49,33},{2,50}... | collective-permute-start | bytes 393224 | tf_op jit(solution)/shard_map/ppermute | solution.py:208
  11.7 11.2 %collective-permute-start.4 = (bf16[16,4096]{1,0:T(8,128)(2,1)}, bf16[16,4096]{1,0:T(8,128)(2,1)S(1)}, u32[]{:S(2)}, u32[]{:S(2)}) collective-permute-start(bf16[16,4096]{1,0:T(8,128)(2,1)} %param.17), channel_id=1, source_target_pairs={{0,32},{16,48},{32,0},{48,16},{1,33},{17,49},{33,1},{49,17},{2,34}... | collective-permute-start | bytes 393224 | tf_op jit(solution)/shard_map/ppermute | solution.py:208
  11.7 11.2 %collective-permute-start.3 = (bf16[16,4096]{1,0:T(8,128)(2,1)}, bf16[16,4096]{1,0:T(8,128)(2,1)S(1)}, u32[]{:S(2)}, u32[]{:S(2)}) collective-permute-start(bf16[16,4096]{1,0:T(8,128)(2,1)} %param.17), channel_id=1, source_target_pairs={{0,16},{16,32},{32,48},{48,0},{1,17},{17,33},{33,49},{49,1},{2,18}... | collective-permute-start | bytes 393224 | tf_op jit(solution)/shard_map/ppermute | solution.py:208
  24.9 2.2 %copy-start.1 = (f32[2,2,256,1024]{3,2,1,0:T(8,128)S(1)}, f32[2,2,256,1024]{3,2,1,0:T(8,128)}, u32[]{:S(2)}) copy-start(f32[2,2,256,1024]{3,2,1,0:T(8,128)} %param.15) | copy-start | bytes 12582916
  27.1 1.0 copy-start.2
  28.1 1.0 copy-start.4
  31.5 71.1 %copy-start.7 = (bf16[512,256]{1,0:T(8,128)(2,1)S(1)}, bf16[512,256]{1,0:T(8,128)(2,1)}, u32[]{:S(2)}) copy-start(bf16[512,256]{1,0:T(8,128)(2,1)} %constant.72.clone.hi_ref) | copy-start | bytes 786436
  31.5 71.1 %copy-start.8 = (bf16[512,256]{1,0:T(8,128)(2,1)S(1)}, bf16[512,256]{1,0:T(8,128)(2,1)}, u32[]{:S(2)}) copy-start(bf16[512,256]{1,0:T(8,128)(2,1)} %constant.73.clone.lo_ref) | copy-start | bytes 786436
  31.5 71.1 %copy-start.9 = (f32[128,256]{1,0:T(8,128)S(1)}, f32[128,256]{1,0:T(8,128)}, u32[]{:S(2)}) copy-start(f32[128,256]{1,0:T(8,128)} %constant.74.clone.tc_ref) | copy-start | bytes 393220
  31.5 71.1 %copy-start.10 = (f32[128,256]{1,0:T(8,128)S(1)}, f32[128,256]{1,0:T(8,128)}, u32[]{:S(2)}) copy-start(f32[128,256]{1,0:T(8,128)} %constant.75.clone.ts_ref) | copy-start | bytes 393220
  31.5 71.1 %copy-start.11 = (bf16[256,128]{1,0:T(8,128)(2,1)S(1)}, bf16[256,128]{1,0:T(8,128)(2,1)}, u32[]{:S(2)}) copy-start(bf16[256,128]{1,0:T(8,128)(2,1)} %constant.70.clone.first_ref) | copy-start | bytes 196612
  31.5 71.1 %copy-start.12 = (bf16[128,256]{1,0:T(8,128)(2,1)S(1)}, bf16[128,256]{1,0:T(8,128)(2,1)}, u32[]{:S(2)}) copy-start(bf16[128,256]{1,0:T(8,128)(2,1)} %constant.71.clone.last_ref) | copy-start | bytes 196612
  31.6 113.5 %copy-start.3 = (bf16[256,1024]{1,0:T(8,128)(2,1)S(1)}, bf16[256,1024]{1,0:T(8,128)(2,1)}, u32[]{:S(2)}) copy-start(bf16[256,1024]{1,0:T(8,128)(2,1)} %k_ref.3) | copy-start | bytes 1572868
  31.6 113.5 %copy-start.5 = (bf16[256,1024]{1,0:T(8,128)(2,1)S(1)}, bf16[256,1024]{1,0:T(8,128)(2,1)}, u32[]{:S(2)}) copy-start(bf16[256,1024]{1,0:T(8,128)(2,1)} %v_ref.3) | copy-start | bytes 1572868
  31.6 113.4 %copy-start.6 = (bf16[256,1024]{1,0:T(8,128)(2,1)S(1)}, bf16[256,1024]{1,0:T(8,128)(2,1)}, u32[]{:S(2)}) copy-start(bf16[256,1024]{1,0:T(8,128)(2,1)} %q_ref.1) | copy-start | bytes 1572868
  31.6 113.4 %copy-start.13 = (f32[1024]{0:T(1024)S(1)}, f32[1024]{0:T(1024)}, u32[]{:S(2)}) copy-start(f32[1024]{0:T(1024)} %param.16) | copy-start | bytes 12292
  146.5 19.3 %collective-permute-start.1 = (bf16[256,1024]{1,0:T(8,128)(2,1)S(1)}, bf16[256,1024]{1,0:T(8,128)(2,1)S(1)}, u32[]{:S(2)}, u32[]{:S(2)}) collective-permute-start(bf16[256,1024]{1,0:T(8,128)(2,1)S(1)} %gate.1.g0), channel_id=1, source_target_pairs={{0,2},{2,0},{1,3},{3,1},{4,6},{6,4},{5,7},{7,5},{8,10},{10,8},{9,1... | collective-permute-start | bytes 1572872 | tf_op jit(solution)/shard_map/ppermute | solution.py:226
  152.5 18.4 %collective-permute-start = (bf16[256,1024]{1,0:T(8,128)(2,1)S(1)}, bf16[256,1024]{1,0:T(8,128)(2,1)S(1)}, u32[]{:S(2)}, u32[]{:S(2)}) collective-permute-start(bf16[256,1024]{1,0:T(8,128)(2,1)S(1)} %gate.1.g0), channel_id=1, source_target_pairs={{0,1},{1,0},{2,3},{3,2},{4,5},{5,4},{6,7},{7,6},{8,9},{9,8},{10,11... | collective-permute-start | bytes 1572872 | tf_op jit(solution)/shard_map/ppermute | solution.py:227
  165.9 6.4 %collective-permute-start.2 = (bf16[256,1024]{1,0:T(8,128)(2,1)S(1)}, bf16[256,1024]{1,0:T(8,128)(2,1)S(1)}, u32[]{:S(2)}, u32[]{:S(2)}) collective-permute-start(bf16[256,1024]{1,0:T(8,128)(2,1)S(1)} %collective-permute-done.1.g2), channel_id=1, source_target_pairs={{0,1},{1,0},{2,3},{3,2},{4,5},{5,4},{6,7},{7,6},{8,9},{9,8},{10,11... | collective-permute-start | bytes 1572872 | tf_op jit(solution)/shard_map/ppermute | solution.py:228
  172.3 3.4 %copy-start = (bf16[64,16,4096]{2,1,0:T(8,128)(2,1)S(1)}, bf16[64,16,4096]{2,1,0:T(8,128)(2,1)}, u32[]{:S(2)}) copy-start(bf16[64,16,4096]{2,1,0:T(8,128)(2,1)} %all-gather.3.cloned.1.call-done) | copy-start | bytes 25165828
Sparse Core Ops, SparseCore 0:
  25.0 101.2 all-gather.2

commit v2 on v1

v2 whole, which is shorter than its diff:
```python
import functools

import numpy as np

import jax
import jax.numpy as jnp
import ml_dtypes
from jax import lax
from jax.experimental import pallas as pl
from jax.experimental.pallas import tpu as pltpu
from jax.sharding import Mesh, PartitionSpec as P

BF, F32 = jnp.bfloat16, jnp.float32
SEQ = ("y", "z", "x")
TOK, NSEQ, CLASSES = 256, 64, 128
FULL = CLASSES * TOK
BIG = 56 << 20
SMALL = 16 << 20
KEPT = 72


def split(table):
    hi = table.astype(ml_dtypes.bfloat16)
    lo = (table - hi.astype(np.float64)).astype(ml_dtypes.bfloat16)
    return hi, lo


def tables():
    classes = np.concatenate([np.arange(0, CLASSES, 2), np.arange(1, CLASSES, 2)])
    blocks, rows = np.arange(NSEQ), np.arange(TOK)
    kept = np.arange(KEPT)
    real = (kept <= CLASSES // 2)[:, None]
    same = (kept[:, None] == classes[None, :]) & real
    other = (CLASSES - kept[:, None] == classes[None, :]) & real & ~same
    fold = np.stack([1.0 * same + other, 1.0 * same - other]).astype(ml_dtypes.bfloat16)
    turn = 2 * np.pi * (kept[:, None] * blocks[None, :] % CLASSES) / CLASSES
    cos, sin = np.cos(turn) * real, np.sin(turn) * real
    fwd_hi, fwd_lo = split(np.concatenate([cos, -sin], 0))
    first = np.concatenate([fwd_hi, fwd_lo], 1)
    last = np.concatenate(split(np.concatenate([cos.T, -sin.T], 1) / FULL), 0)
    turn = 2 * np.pi * (rows[:, None] * rows[None, :] % TOK) / TOK
    row_hi, row_lo = split(np.concatenate([np.cos(turn), np.sin(turn)], 0))
    row = np.concatenate([row_hi, row_hi, row_lo], 0)
    turn = 2 * np.pi * (kept[:, None] * rows[None, :]) / FULL
    return fold, first, last, row, np.stack([np.cos(turn), np.sin(turn)]).astype(np.float32)


def dot(a, b):
    return lax.dot_general(a, b, (((1,), (0,)), ((), ())), preferred_element_type=F32)


def parts(value):
    hi = value.astype(BF)
    return hi, (value - hi.astype(F32)).astype(BF)


def prep_kernel(turned_ref, k_ref, v_ref, s_ref, o_ref):
    conv = k_ref[...].astype(F32) * v_ref[...].astype(F32)
    o_ref[:, :TOK] = conv.T.astype(BF)
    row = lax.broadcasted_iota(jnp.int32, (TOK, TOK), 0)
    col = lax.broadcasted_iota(jnp.int32, (TOK, TOK), 1)
    for e in range(2):
        place = jnp.where(turned_ref[e] == 1, TOK - 1 - row, row)
        order = jnp.where(place == col, 1.0, 0.0).astype(BF)
        for j in (e, 2 + e):
            o_ref[:, TOK * (j + 1) : TOK * (j + 2)] = dot(s_ref[j].T.astype(BF), order).astype(BF)


def prep(turned, key, value, spectra):
    width = key.shape[1]
    blk = 512
    tok = pl.BlockSpec((TOK, blk), lambda i, turned: (0, i))
    return pl.pallas_call(
        prep_kernel,
        grid_spec=pltpu.PrefetchScalarGridSpec(
            num_scalar_prefetch=1,
            grid=(width // blk,),
            in_specs=[tok, tok, pl.BlockSpec((4, TOK, blk), lambda i, turned: (0, 0, i))],
            out_specs=pl.BlockSpec((blk, 5 * TOK), lambda i, turned: (i, 0)),
        ),
        out_shape=jax.ShapeDtypeStruct((width, 5 * TOK), BF),
        compiler_params=pltpu.CompilerParams(vmem_limit_bytes=BIG),
        name="prep",
    )(turned, key, value, spectra)


GROUP = 8


def widen(src, dst, columns):
    def chunk(i, _):
        rows = pl.ds(pl.multiple_of(i * 64, 64), 64)
        for c in range(columns):
            dst[c, rows, :] = src[rows, c * 128 : c * 128 + 128].astype(F32)
        return 0

    lax.fori_loop(0, src.shape[0] // 64, chunk, 0)


def rows_of(ref, h, chans, col):
    rows = pl.ds(h, NSEQ, stride=chans)
    return jnp.concatenate([ref[2 * col, rows, :], ref[2 * col + 1, rows, :]], 1)


def row_section(stacked, row_ref):
    hi = jnp.concatenate([piece for pieces in stacked[0::2] for piece in pieces], 0)
    lo = jnp.concatenate([piece for pieces in stacked[1::2] for piece in pieces], 0)
    return dot(jnp.concatenate([hi, lo, hi], 1), row_ref[...])


def fetch(pairs, sems):
    copies = [pltpu.make_async_copy(src, dst, sems.at[i]) for i, (src, dst) in enumerate(pairs)]
    for copy in copies:
        copy.start()
    return copies


def convolve_kernel(group, r_ref, fold_any, first_any, last_any, row_any, turn_any, o_ref, xs, ys, fold_ref, first_ref, last_ref, row_ref, turn_ref, sems):
    chans = r_ref.shape[0] // NSEQ
    copies = fetch(
        [(fold_any, fold_ref), (first_any, first_ref), (last_any, last_ref), (row_any, row_ref), (turn_any, turn_ref)],
        sems,
    )
    widen(r_ref, xs, 10)
    for copy in copies:
        copy.wait()

    def response(h, part):
        pair = [rows_of(xs, h, chans, 1 + 2 * part + e).astype(BF) for e in range(2)]
        return dot(fold_ref[part], jnp.concatenate(pair, 0))

    def step(g, _):
        tc, ts = turn_ref[0], turn_ref[1]
        stacked = []
        for j in range(group):
            x = rows_of(xs, g * group + j, chans, 0).astype(BF)
            a = dot(first_ref[...], jnp.concatenate([x, x], 0))
            ar, ai = a[:KEPT], a[KEPT:]
            ar, ai = parts(ar * tc + ai * ts), parts(ai * tc - ar * ts)
            stacked += [[jnp.concatenate([ar[n], ai[n]], 1), jnp.concatenate([ai[n], -ar[n]], 1)] for n in (0, 1)]
        freq = row_section(stacked, row_ref)
        stacked = []
        for j in range(group):
            h = g * group + j
            rr, ri = response(h, 0), response(h, 1)
            base = 2 * KEPT * j
            xr, xi = freq[base : base + KEPT], freq[base + KEPT : base + 2 * KEPT]
            pr, pi = parts(rr * xr - ri * xi), parts(rr * xi + ri * xr)
            stacked += [[jnp.concatenate([pr[n], -pi[n]], 1), jnp.concatenate([pi[n], pr[n]], 1)] for n in (0, 1)]
        back = row_section(stacked, row_ref)
        for j in range(group):
            h = g * group + j
            base = 2 * KEPT * j
            br, bi = back[base : base + KEPT], back[base + KEPT : base + 2 * KEPT]
            hi, lo = parts(jnp.concatenate([br * tc - bi * ts, bi * tc + br * ts], 0))
            both = dot(last_ref[...], hi)
            y = both[:NSEQ] + both[NSEQ:] + dot(last_ref[:NSEQ], lo)
            for c in range(2):
                ys[c, pl.ds(h, NSEQ, stride=chans), :] = y[:, c * 128 : c * 128 + 128]
        return 0

    lax.fori_loop(0, chans // group, step, 0)
    for c in range(2):
        o_ref[:, c * 128 : c * 128 + 128] = ys[c].astype(BF)


VMEM = pl.BlockSpec(memory_space=pltpu.VMEM)
ANY = pl.BlockSpec(memory_space=pl.ANY)


def constants():
    return [jnp.asarray(table) for table in tables()]


def held(consts):
    return [pltpu.VMEM(c.shape, c.dtype) for c in consts]


def block(shape):
    return pl.BlockSpec(shape, lambda i: (0,) * len(shape))


def convolve(received, group=GROUP):
    rows = received.shape[0]
    consts = constants()
    return pl.pallas_call(
        functools.partial(convolve_kernel, group),
        grid=(1,),
        in_specs=[block(received.shape)] + [ANY] * len(consts),
        out_specs=block((rows, TOK)),
        out_shape=jax.ShapeDtypeStruct((rows, TOK), BF),
        scratch_shapes=[pltpu.VMEM((10, rows, 128), F32), pltpu.VMEM((2, rows, 128), F32)]
        + held(consts)
        + [pltpu.SemaphoreType.DMA((len(consts),))],
        compiler_params=pltpu.CompilerParams(vmem_limit_bytes=BIG),
        name="convolve",
    )(received, *consts)


def prep_g_kernel(q_ref, k_ref, v_ref, s_ref, qt_ref, ct_ref):
    conv = k_ref[...].astype(F32) * v_ref[...].astype(F32)
    qt_ref[...] = q_ref[...].astype(F32).T.astype(BF)
    ct_ref[...] = (s_ref[...] * conv).T


def prep_g(query, key, value, gain):
    width = key.shape[1]
    blk = 512
    tok = pl.BlockSpec((TOK, blk), lambda i: (0, i))
    chan = pl.BlockSpec((blk, TOK), lambda i: (i, 0))
    return pl.pallas_call(
        prep_g_kernel,
        grid=(width // blk,),
        in_specs=[tok, tok, tok, pl.BlockSpec((1, blk), lambda i: (0, i))],
        out_specs=[chan, chan],
        out_shape=[jax.ShapeDtypeStruct((width, TOK), BF), jax.ShapeDtypeStruct((width, TOK), F32)],
        compiler_params=pltpu.CompilerParams(vmem_limit_bytes=SMALL),
        cost_estimate=pl.CostEstimate(flops=1 << 20, bytes_accessed=4 << 20, transcendentals=0),
        name="prep_g",
    )(query, key, value, gain)


def gate_kernel(y_ref, q_ref, c_ref, o_ref):
    o_ref[...] = (q_ref[...].astype(F32) * (y_ref[...].astype(F32) + c_ref[...])).astype(BF)


def gate(y, query_t, direct_t):
    width = y.shape[0]
    blk = 512
    chan = pl.BlockSpec((blk, TOK), lambda i: (i, 0))
    return pl.pallas_call(
        gate_kernel,
        grid=(width // blk,),
        in_specs=[chan] * 3,
        out_specs=chan,
        out_shape=jax.ShapeDtypeStruct((width, TOK), BF),
        compiler_params=pltpu.CompilerParams(vmem_limit_bytes=SMALL),
        name="gate",
    )(y, query_t, direct_t)


def project_kernel(count, more, final, order_ref, *refs):
    g_refs, w_refs, o_ref = refs[:count], refs[count : 2 * count], refs[-1]
    for y in range(w_refs[0].shape[0]):
        lines = slice(y * 256, y * 256 + 256)
        total = refs[-2][lines] if more else None
        for g_ref, w_ref in zip(g_refs, w_refs):
            w = jnp.concatenate([w_ref[y, x, (order_ref[count] - z) & 3] for z in range(4) for x in range(4)], 0)
            term = dot(w, g_ref[...])
            total = term if total is None else total + term
        if final:
            o_ref[:, lines] = total.T.astype(BF)
        else:
            o_ref[lines] = total


def project(order, pieces, weight, base=None):
    final = base is not None
    width = pieces[0].shape[0]
    count, steps = len(pieces), 2
    lines = 1024 // steps
    more = [base] if final else []
    whole = pl.BlockSpec((width, TOK), lambda i, order: (0, 0))
    sums = pl.BlockSpec((lines, TOK), lambda i, order: (i, 0))
    shape = jax.ShapeDtypeStruct((TOK, 1024) if final else (1024, TOK), BF if final else F32)

    def columns(j):
        shape = (4 // steps,) + weight.shape[1:4] + (width,)
        return pl.BlockSpec(shape, lambda i, order: (i, 0, 0, 0, order[j]))

    return pl.pallas_call(
        functools.partial(project_kernel, count, final, final),
        grid_spec=pltpu.PrefetchScalarGridSpec(
            num_scalar_prefetch=1,
            grid=(steps,),
            in_specs=[whole] * count + [columns(j) for j in range(count)] + [sums] * len(more),
            out_specs=pl.BlockSpec((TOK, lines), lambda i, order: (0, i)) if final else sums,
        ),
        out_shape=shape,
        compiler_params=pltpu.CompilerParams(vmem_limit_bytes=SMALL),
        cost_estimate=pl.CostEstimate(flops=1 << 35, bytes_accessed=6 << 20, transcendentals=0),
        name="project_last" if final else "project_first",
    )(order, *pieces, *([weight] * count), *more)


def gather_weight(weight, after):
    pieces = [weight] + [
        lax.ppermute(weight, "z", [(a, (a + d) % 4) for a in range(4)]) for d in (1, 2, 3)
    ]
    *pieces, after = lax.optimization_barrier((*pieces, after))
    full = lax.all_gather(jnp.stack(pieces)[None], ("y", "x"), axis=0, tiled=True)
    return full.reshape((4, 4, 4) + weight.shape), after


def exchange(send):
    send = send.reshape(NSEQ, -1, send.shape[1])
    got = lax.all_to_all(send, SEQ, split_axis=0, concat_axis=0, tiled=True)
    return got.reshape(-1, got.shape[2])


def local(query, key, value, spectra, gain, weight):
    swap = [(0, 1), (1, 0)]
    index = (lax.axis_index("y") * 4 + lax.axis_index("z")) * 4 + lax.axis_index("x")
    turned = (2 * index + jnp.arange(2) > CLASSES // 2).astype(jnp.int32)
    send = prep(turned, key, value, spectra.reshape((4,) + spectra.shape[2:]))
    full_weight, send = gather_weight(weight, send)
    send, query, key, value, gain = lax.optimization_barrier((send, query, key, value, gain))
    got = exchange(send)
    query_t, direct_t = prep_g(query, key, value, gain[None, :])
    y = exchange(convolve(got))
    gated = gate(y, query_t, direct_t)
    over_k = lax.ppermute(gated, "k", swap)
    gated, over_k = lax.optimization_barrier((gated, over_k))
    over_h = lax.ppermute(gated, "h", swap)
    h, k, z = lax.axis_index("h"), lax.axis_index("k"), lax.axis_index("z")
    near = jnp.stack([h * 2 + k, h * 2 + 1 - k, z]).astype(jnp.int32)
    far = jnp.stack([(1 - h) * 2 + k, (1 - h) * 2 + 1 - k, z]).astype(jnp.int32)
    near, far = lax.optimization_barrier((near, far))
    total = project(near, (gated, over_k), full_weight)
    over_h, total = lax.optimization_barrier((over_h, total))
    over_hk = lax.ppermute(over_h, "k", swap)
    return project(far, (over_h, over_hk), full_weight, total)


def solution(mesh):
    fine = Mesh(mesh.devices.reshape(4, 4, 4, 2, 2), ("y", "z", "x", "h", "k"))
    chan = ("h", "k")
    return jax.shard_map(
        local,
        mesh=fine,
        in_specs=(
            P(SEQ, chan),
            P(SEQ, chan),
            P(SEQ, chan),
            P(None, SEQ, None, chan),
            P(chan),
            P(chan + SEQ, None),
        ),
        out_specs=P(SEQ, chan),
        check_vma=False,
    )
```

time: 191 us -> 176 us (0.921)
  blocking collectives: 93.7 us -> 72.8 us
  waiting for transfers between devices: 23.4 us -> 34.6 us
  Pallas kernels: 28.5 us -> 25.3 us
  local copies, waits for them, and re-layouts: 7.76 us -> 5.3 us
  starting transfers between devices: 18.7 us -> 20.8 us
    all_to_all x2 -> x1, blocking collectives: 93.7 us -> 72.8 us  [exchange(): got = lax.all_to_all(send, SEQ, split_axis=0, concat_axis=0, tiled=True)]
    all_to_all x0 -> x1, waiting for transfers between devices: none -> 15.4 us  [exchange(): got = lax.all_to_all(send, SEQ, split_axis=0, concat_axis=0, tiled=True)]
    ppermute x3, waiting for transfers between devices: 10.9 us -> 3.39 us  [gather_weight(): lax.ppermute(weight, 'z', [(a, (a + d) % 4) for a in range(4)])]
    all_to_all x0 -> x1, starting transfers between devices: none -> 5.52 us  [exchange(): got = lax.all_to_all(send, SEQ, split_axis=0, concat_axis=0, tiled=True)]
    ppermute x1, starting transfers between devices: 4.87 us -> 1.37 us  [local(): over_hk = lax.ppermute(over_h, 'k', swap)]
    pallas_call x4 -> x6, Pallas kernels: 28.5 us -> 25.3 us  [the longest x1 14 us: convolve(): pl.pallas_call(functools.partial(convolve_kernel, group), grid=(1,), in_s...]
    unnamed x28 -> x18, local copies, waits for them, and re-layouts: 7.71 us -> 5.3 us
  transfers between devices with their start and end apart: 7 -> 8, of which waited for: 4 -> 5; matrix products, arithmetic and copies ran while one was open for 0% -> 0% of each run, Pallas kernels for 13% -> 13%
where the time goes in v2:
time: 176 us; the launch traced here: 174 us
  blocking collectives  72.8 us (41%)
  waiting for transfers between devices  34.6 us (20%)
  Pallas kernels  25.3 us (14%)
  starting transfers between devices  20.8 us (12%)
  between operations  13.5 us (8%)
  local copies, waits for them, and re-layouts  5.3 us (3%)
    all_to_all x1, blocking collectives, exchange(): got = lax.all_to_all(send, SEQ, split_axis=0, concat_axis=0, tiled=True)  72.8 us
    all_to_all x1, waiting for transfers between devices, exchange(): got = lax.all_to_all(send, SEQ, split_axis=0, concat_axis=0, tiled=True)  15.4 us
    pallas_call x1, Pallas kernels, convolve(): pl.pallas_call(functools.partial(convolve_kernel, group), grid=(1,), in_s...  14 us
    ppermute x1, waiting for transfers between devices, local(): over_h = lax.ppermute(gated, 'h', swap)  12.8 us
    ppermute x3, starting transfers between devices, gather_weight(): lax.ppermute(weight, 'z', [(a, (a + d) % 4) for a in range(4)])  6.19 us
    all_to_all x1, starting transfers between devices, exchange(): got = lax.all_to_all(send, SEQ, split_axis=0, concat_axis=0, tiled=True)  5.52 us
    pallas_call x2, Pallas kernels, project(): pl.pallas_call(functools.partial(project_kernel, count, final, final), gr...  5.51 us
    ppermute x1, starting transfers between devices, local(): over_h = lax.ppermute(gated, 'h', swap)  5.43 us
  transfers between devices with their start and end apart: 8, of which 5 were waited for; matrix products, arithmetic and copies ran while one was open for 0% of the time, Pallas kernels for 13%

profile of v2, /device:TPU:1, one launch (start us, length us, event | category | flops | bytes accessed | tf_op | source)
XLA Modules:
  0.0 173.9 jit_solution(10851148348479017112)
XLA Ops:
  6.5 0.0 copy-start.8
  6.5 0.0 all-gather.3.cloned.1.call-start
  6.5 2.5 %collective-permute-start = (bf16[16,4096]{1,0:T(8,128)(2,1)}, bf16[16,4096]{1,0:T(8,128)(2,1)S(1)}, u32[]{:S(2)}, u32[]{:S(2)}) collective-permute-start(bf16[16,4096]{1,0:T(8,128)(2,1)} %param.16), channel_id=1, source_target_pairs={{0,16},{16,32},{32,48},{48,0},{1,17},{17,33},{33,49},{49,1},{2,18}... | collective-permute-start | bytes 393224 | tf_op jit(solution)/shard_map/ppermute | solution.py:288
  9.0 3.0 %collective-permute-start.1 = (bf16[16,4096]{1,0:T(8,128)(2,1)}, bf16[16,4096]{1,0:T(8,128)(2,1)S(1)}, u32[]{:S(2)}, u32[]{:S(2)}) collective-permute-start(bf16[16,4096]{1,0:T(8,128)(2,1)} %param.16), channel_id=1, source_target_pairs={{0,32},{16,48},{32,0},{48,16},{1,33},{17,49},{33,1},{49,17},{2,34}... | collective-permute-start | bytes 393224 | tf_op jit(solution)/shard_map/ppermute | solution.py:288
  12.0 0.7 collective-permute-start.2
  12.7 0.5 compare_convert_fusion.turned_ref
  13.2 4.9 %prep.1 = bf16[1024,1280]{1,0:T(8,128)(2,1)} custom-call(s32[2]{0:T(128)} %compare_convert_fusion.turned_ref, bf16[256,1024]{1,0:T(8,128)(2,1)} %k_ref.2, bf16[256,1024]{1,0:T(8,128)(2,1)} %v_ref.2, f32[4,256,1024]{2,1,0:T(8,128)} %bitcast.24), custom_call_target="tpu_custom_call" | custom-call | tf_op jit(solution)/shard_map/prep/pallas_call | solution.py:73
  18.2 0.0 collective-permute-done
  18.2 3.4 %collective-permute-done.1 = bf16[16,4096]{1,0:T(8,128)(2,1)S(1)} collective-permute-done((bf16[16,4096]{1,0:T(8,128)(2,1)}, bf16[16,4096]{1,0:T(8,128)(2,1)S(1)}, u32[]{:S(2)}, u32[]{:S(2)}) %collective-permute-start.1) | collective-permute-done | bytes 131104 | tf_op jit(solution)/shard_map/ppermute | solution.py:288
  21.6 0.0 collective-permute-done.2
  21.6 0.0 copy-done.8
  21.6 0.9 pad_maximum_fusion
  22.4 0.0 all-gather.3.cloned.1.call-update
  22.5 0.0 copy-start
  22.5 0.0 copy-start.1
  22.5 0.0 copy-start.2
  22.5 0.0 copy-start.5
  22.5 72.8 %all_to_all.10 = bf16[64,16,1280]{2,1,0:T(8,128)(2,1)} all-to-all(bf16[64,16,1280]{2,1,0:T(8,128)(2,1)} %bitcast.22), channel_id=1, replica_groups=mesh['y'=4,'z'=4,'x'=4,'h'=2,'k'=2] {'y','z','x'}, dimensions={0} | all-to-all | bytes 5242880 | tf_op jit(solution)/shard_map/all_to_all | solution.py:297
  95.3 14.0 %convolve.1 = bf16[1024,256]{1,0:T(8,128)(2,1)} custom-call(bf16[1024,1280]{1,0:T(8,128)(2,1)} %bitcast.23, bf16[2,72,128]{2,1,0:T(8,128)(2,1)} %constant.37.clone.fold_any, bf16[144,128]{1,0:T(8,128)(2,1)} %constant.38.clone.first_any, bf16[128,144]{1,0:T(8,128)(2,1)} %constant.39.clone.last_any, bf16[1536,256]{1,0:T(8,128)(2,1)} %constant.40.clone.row_any, ...), custom_call_target="tpu_custom_call" | custom-call | tf_op jit(solution)/shard_map/convolve/pallas_call | solution.py:186
  109.3 5.5 %all-to-all-start.1 = ((bf16[64,16,256]{2,1,0:T(8,128)(2,1)}), bf16[64,16,256]{2,1,0:T(8,128)(2,1)S(1)}, u32[]{:S(2)}, u32[]{:S(2)}) async-start(bf16[64,16,256]{2,1,0:T(8,128)(2,1)} %bitcast.25), calls=%async_computation.1 | async-start | bytes 1048576 | tf_op jit(solution)/shard_map/all_to_all | solution.py:297
  114.9 0.0 copy-done
  114.9 0.0 copy-done.1
  114.9 0.0 copy-done.2
  114.9 0.0 copy-done.5
  114.9 0.7 prep_g.1
  115.6 0.0 copy-start.3
  115.6 0.8 copy-done.3
  116.5 15.4 %all-to-all-done.1 = bf16[64,16,256]{2,1,0:T(8,128)(2,1)S(1)} async-done(((bf16[64,16,256]{2,1,0:T(8,128)(2,1)}), bf16[64,16,256]{2,1,0:T(8,128)(2,1)S(1)}, u32[]{:S(2)}, u32[]{:S(2)}) %all-to-all-start.1) | async-done | bytes 524320 | tf_op jit(solution)/shard_map/all_to_all | solution.py:297
  131.9 0.0 copy-start.4
  131.9 1.0 copy-done.4
  133.0 0.2 gate.1.refs_0_
  133.2 2.3 %collective-permute-start.3 = (bf16[1024,256]{1,0:T(8,128)(2,1)S(1)}, bf16[1024,256]{1,0:T(8,128)(2,1)S(1)}, u32[]{:S(2)}, u32[]{:S(2)}) collective-permute-start(bf16[1024,256]{1,0:T(8,128)(2,1)S(1)} %gate.1.refs_0_), channel_id=1, source_target_pairs={{0,1},{1,0},{2,3},{3,2},{4,5},{5,4},{6,7},{7,6},{8,9},{9,8},{10,11... | collective-permute-start | bytes 1572872 | tf_op jit(solution)/shard_map/ppermute | solution.py:312
  135.5 0.1 add_add_fusion
  135.5 1.5 collective-permute-done.3.refs_1_
  137.0 5.4 %collective-permute-start.4 = (bf16[1024,256]{1,0:T(8,128)(2,1)S(1)}, bf16[1024,256]{1,0:T(8,128)(2,1)S(1)}, u32[]{:S(2)}, u32[]{:S(2)}) collective-permute-start(bf16[1024,256]{1,0:T(8,128)(2,1)S(1)} %gate.1.refs_0_), channel_id=1, source_target_pairs={{0,2},{2,0},{1,3},{3,1},{4,6},{6,4},{5,7},{7,5},{8,10},{10,8},{9,1... | collective-permute-start | bytes 1572872 | tf_op jit(solution)/shard_map/ppermute | solution.py:314
  142.4 0.0 all-gather.3.cloned.1.call-done
  142.4 0.0 copy-start.6
  142.4 3.4 %copy-done.6 = bf16[64,16,4096]{2,1,0:T(8,128)(2,1)S(1)} copy-done((bf16[64,16,4096]{2,1,0:T(8,128)(2,1)S(1)}, bf16[64,16,4096]{2,1,0:T(8,128)(2,1)}, u32[]{:S(2)}) %copy-start.6) | copy-done | bytes 8388632
  145.8 0.0 copy-start.7
  145.8 2.3 %project_first.1.refs_4_ = f32[1024,256]{1,0:T(8,128)S(1)} custom-call(s32[3]{0:T(128)S(1)} %get-tuple-element.33.order_ref, bf16[1024,256]{1,0:T(8,128)(2,1)S(1)} %gate.1.refs_0_, bf16[1024,256]{1,0:T(8,128)(2,1)S(1)} %collective-permute-done.3.refs_1_, bf16[4,4,4,16,4096]{4,3,2,1,0:T(8,128)(2,1)S(1)} %bitcast.18, bf16[4,4,4,16,4096]{4,3,2,1,0:T(8,128)(2,1)S(1)} %bitcast.19), custom_call_target="tpu_custom_call" | custom-call | flops 34359738368 | bytes 6291456 | tf_op jit(solution)/shard_map/project_first/pallas_call | solution.py:271
  148.1 12.8 %collective-permute-done.4.refs_0_ = bf16[1024,256]{1,0:T(8,128)(2,1)S(1)} collective-permute-done((bf16[1024,256]{1,0:T(8,128)(2,1)S(1)}, bf16[1024,256]{1,0:T(8,128)(2,1)S(1)}, u32[]{:S(2)}, u32[]{:S(2)}) %collective-permute-start.4) | collective-permute-done | bytes 524320 | tf_op jit(solution)/shard_map/ppermute | solution.py:314
  160.9 1.4 collective-permute-start.5
  162.3 1.5 collective-permute-done.5.refs_1_
  163.8 0.0 copy-done.7
  163.8 3.2 %project_last.1 = bf16[256,1024]{1,0:T(8,128)(2,1)} custom-call(s32[3]{0:T(128)S(1)} %get-tuple-element.23.order_ref, bf16[1024,256]{1,0:T(8,128)(2,1)S(1)} %collective-permute-done.4.refs_0_, bf16[1024,256]{1,0:T(8,128)(2,1)S(1)} %collective-permute-done.5.refs_1_, bf16[4,4,4,16,4096]{4,3,2,1,0:T(8,128)(2,1)S(1)} %bitcast.20, ...), custom_call_target="tpu_custom_call" | custom-call | flops 34359738368 | bytes 6291456 | tf_op jit(solution)/shard_map/project_last/pallas_call | solution.py:271
Async XLA Ops:
  6.5 15.0 %copy-start.8 = (bf16[16,4096]{1,0:T(8,128)(2,1)S(1)}, bf16[16,4096]{1,0:T(8,128)(2,1)}, u32[]{:S(2)}) copy-start(bf16[16,4096]{1,0:T(8,128)(2,1)} %param.16) | copy-start | bytes 393220
  6.5 135.9 %all-gather.3.cloned.1.call-start = ((), (), s32[]{:S(2)}) async-start(), calls=%async_computation.2 | async-start | bytes 8912896 | tf_op jit(solution)/shard_map/all_gather | solution.py:291
  6.5 11.6 %collective-permute-start = (bf16[16,4096]{1,0:T(8,128)(2,1)}, bf16[16,4096]{1,0:T(8,128)(2,1)S(1)}, u32[]{:S(2)}, u32[]{:S(2)}) collective-permute-start(bf16[16,4096]{1,0:T(8,128)(2,1)} %param.16), channel_id=1, source_target_pairs={{0,16},{16,32},{32,48},{48,0},{1,17},{17,33},{33,49},{49,1},{2,18}... | collective-permute-start | bytes 393224 | tf_op jit(solution)/shard_map/ppermute | solution.py:288
  9.0 12.6 %collective-permute-start.1 = (bf16[16,4096]{1,0:T(8,128)(2,1)}, bf16[16,4096]{1,0:T(8,128)(2,1)S(1)}, u32[]{:S(2)}, u32[]{:S(2)}) collective-permute-start(bf16[16,4096]{1,0:T(8,128)(2,1)} %param.16), channel_id=1, source_target_pairs={{0,32},{16,48},{32,0},{48,16},{1,33},{17,49},{33,1},{49,17},{2,34}... | collective-permute-start | bytes 393224 | tf_op jit(solution)/shard_map/ppermute | solution.py:288
  12.0 9.6 %collective-permute-start.2 = (bf16[16,4096]{1,0:T(8,128)(2,1)}, bf16[16,4096]{1,0:T(8,128)(2,1)S(1)}, u32[]{:S(2)}, u32[]{:S(2)}) collective-permute-start(bf16[16,4096]{1,0:T(8,128)(2,1)} %param.16), channel_id=1, source_target_pairs={{0,48},{16,0},{32,16},{48,32},{1,49},{17,1},{33,17},{49,33},{2,50}... | collective-permute-start | bytes 393224 | tf_op jit(solution)/shard_map/ppermute | solution.py:288
  22.5 92.4 %copy-start = (bf16[256,1024]{1,0:T(8,128)(2,1)S(1)}, bf16[256,1024]{1,0:T(8,128)(2,1)}, u32[]{:S(2)}) copy-start(bf16[256,1024]{1,0:T(8,128)(2,1)} %k_ref.2) | copy-start | bytes 1572868
  22.5 92.4 %copy-start.1 = (bf16[256,1024]{1,0:T(8,128)(2,1)S(1)}, bf16[256,1024]{1,0:T(8,128)(2,1)}, u32[]{:S(2)}) copy-start(bf16[256,1024]{1,0:T(8,128)(2,1)} %v_ref.2) | copy-start | bytes 1572868
  22.5 92.4 %copy-start.2 = (bf16[256,1024]{1,0:T(8,128)(2,1)S(1)}, bf16[256,1024]{1,0:T(8,128)(2,1)}, u32[]{:S(2)}) copy-start(bf16[256,1024]{1,0:T(8,128)(2,1)} %q_ref) | copy-start | bytes 1572868
  22.5 92.4 %copy-start.5 = (f32[1024]{0:T(1024)S(1)}, f32[1024]{0:T(1024)}, u32[]{:S(2)}) copy-start(f32[1024]{0:T(1024)} %param.15) | copy-start | bytes 12292
  109.3 22.6 %all-to-all-start.1 = ((bf16[64,16,256]{2,1,0:T(8,128)(2,1)}), bf16[64,16,256]{2,1,0:T(8,128)(2,1)S(1)}, u32[]{:S(2)}, u32[]{:S(2)}) async-start(bf16[64,16,256]{2,1,0:T(8,128)(2,1)} %bitcast.25), calls=%async_computation.1 | async-start | bytes 1048576 | tf_op jit(solution)/shard_map/all_to_all | solution.py:297
  115.6 0.9 copy-start.3
  131.9 1.0 copy-start.4
  133.2 3.8 %collective-permute-start.3 = (bf16[1024,256]{1,0:T(8,128)(2,1)S(1)}, bf16[1024,256]{1,0:T(8,128)(2,1)S(1)}, u32[]{:S(2)}, u32[]{:S(2)}) collective-permute-start(bf16[1024,256]{1,0:T(8,128)(2,1)S(1)} %gate.1.refs_0_), channel_id=1, source_target_pairs={{0,1},{1,0},{2,3},{3,2},{4,5},{5,4},{6,7},{7,6},{8,9},{9,8},{10,11... | collective-permute-start | bytes 1572872 | tf_op jit(solution)/shard_map/ppermute | solution.py:312
  137.0 23.9 %collective-permute-start.4 = (bf16[1024,256]{1,0:T(8,128)(2,1)S(1)}, bf16[1024,256]{1,0:T(8,128)(2,1)S(1)}, u32[]{:S(2)}, u32[]{:S(2)}) collective-permute-start(bf16[1024,256]{1,0:T(8,128)(2,1)S(1)} %gate.1.refs_0_), channel_id=1, source_target_pairs={{0,2},{2,0},{1,3},{3,1},{4,6},{6,4},{5,7},{7,5},{8,10},{10,8},{9,1... | collective-permute-start | bytes 1572872 | tf_op jit(solution)/shard_map/ppermute | solution.py:314
  142.4 3.4 %copy-start.6 = (bf16[64,16,4096]{2,1,0:T(8,128)(2,1)S(1)}, bf16[64,16,4096]{2,1,0:T(8,128)(2,1)}, u32[]{:S(2)}) copy-start(bf16[64,16,4096]{2,1,0:T(8,128)(2,1)} %all-gather.3.cloned.1.call-done) | copy-start | bytes 25165828
  145.8 18.0 %copy-start.7 = (bf16[64,16,4096]{2,1,0:T(8,128)(2,1)S(1)}, bf16[64,16,4096]{2,1,0:T(8,128)(2,1)}, u32[]{:S(2)}) copy-start(bf16[64,16,4096]{2,1,0:T(8,128)(2,1)} %all-gather.3.cloned.1.call-done) | copy-start | bytes 25165828
  160.9 2.9 %collective-permute-start.5 = (bf16[1024,256]{1,0:T(8,128)(2,1)S(1)}, bf16[1024,256]{1,0:T(8,128)(2,1)S(1)}, u32[]{:S(2)}, u32[]{:S(2)}) collective-permute-start(bf16[1024,256]{1,0:T(8,128)(2,1)S(1)} %collective-permute-done.4.refs_0_), channel_id=1, source_target_pairs={{0,1},{1,0},{2,3},{3,2},{4,5},{5,4},{6,7},{7,6},{8,9},{9,8},{10,11... | collective-permute-start | bytes 1572872 | tf_op jit(solution)/shard_map/ppermute | solution.py:321
Sparse Core Ops, SparseCore 0:
  22.6 104.9 all-gather.2

commit v3 on v2

--- a/solution.py
+++ b/solution.py
@@ -193,6 +193,7 @@
         + held(consts)
         + [pltpu.SemaphoreType.DMA((len(consts),))],
         compiler_params=pltpu.CompilerParams(vmem_limit_bytes=BIG),
+        cost_estimate=pl.CostEstimate(flops=16 << 30, bytes_accessed=4 << 20, transcendentals=0),
         name="convolve",
     )(received, *consts)
 
@@ -239,57 +240,95 @@
     )(y, query_t, direct_t)
 
 
-def project_kernel(count, more, final, order_ref, *refs):
-    g_refs, w_refs, o_ref = refs[:count], refs[count : 2 * count], refs[-1]
-    for y in range(w_refs[0].shape[0]):
-        lines = slice(y * 256, y * 256 + 256)
-        total = refs[-2][lines] if more else None
-        for g_ref, w_ref in zip(g_refs, w_refs):
-            w = jnp.concatenate([w_ref[y, x, (order_ref[count] - z) & 3] for z in range(4) for x in range(4)], 0)
-            term = dot(w, g_ref[...])
-            total = term if total is None else total + term
-        if final:
-            o_ref[:, lines] = total.T.astype(BF)
-        else:
-            o_ref[lines] = total
-
-
-def project(order, pieces, weight, base=None):
-    final = base is not None
-    width = pieces[0].shape[0]
-    count, steps = len(pieces), 2
-    lines = 1024 // steps
-    more = [base] if final else []
-    whole = pl.BlockSpec((width, TOK), lambda i, order: (0, 0))
-    sums = pl.BlockSpec((lines, TOK), lambda i, order: (i, 0))
-    shape = jax.ShapeDtypeStruct((TOK, 1024) if final else (1024, TOK), BF if final else F32)
-
-    def columns(j):
-        shape = (4 // steps,) + weight.shape[1:4] + (width,)
-        return pl.BlockSpec(shape, lambda i, order: (i, 0, 0, 0, order[j]))
-
-    return pl.pallas_call(
-        functools.partial(project_kernel, count, final, final),
+def sum_terms(g_refs, w_refs, total):
+    own, left, opp0, opp1, right = w_refs
+    for d, pair in enumerate(((own, own), (left, left), (opp0, opp1), (right, right))):
+        terms = []
+        for c, (g_ref, w_ref) in enumerate(zip(g_refs, pair)):
+            w = w_ref[...] if d == 2 else w_ref[c]
+            terms.append(dot(w.reshape(256, w.shape[-1]), g_ref[...]))
+        total[d * 256 : d * 256 + 256, :] = terms[0] + terms[1]
+
+
+def near_kernel(g0, g1, own, left, opp0, opp1, right, o_ref):
+    sum_terms((g0, g1), (own, left, opp0, opp1, right), o_ref)
+
+
+def far_kernel(place_ref, g0, g1, own, left, opp0, opp1, right, near_ref, o_ref, total):
+    sum_terms((g0, g1), (own, left, opp0, opp1, right), total)
+
+    def line(ref, a, b, c):
+        return ref[pl.ds(pl.multiple_of(((a * 4 + b) * 4 + c) * 16, 16), 16), :]
+
+    for y in range(4):
+        dy, pieces = (place_ref[0] - y) & 3, []
+        for z in range(4):
+            for x in range(4):
+                dz, dx = (place_ref[1] - z) & 3, (place_ref[2] - x) & 3
+                pieces.append(line(near_ref, dx, dy, dz) + line(total, dy, dx, dz))
+        o_ref[:, y * 256 : y * 256 + 256] = jnp.concatenate(pieces, 0).T.astype(BF)
+
+
+def project(place, pieces, weights, near=None):
+    own, left, (opp0, opp1), right = weights
+    args = [*pieces, own, left, opp0, opp1, right] + ([] if near is None else [near])
+
+    def whole(shape):
+        return pl.BlockSpec(shape, lambda i, *_: (0,) * len(shape))
+
+    shape, kind = ((1024, TOK), F32) if near is None else ((TOK, 1024), BF)
+    return pl.pallas_call(
+        near_kernel if near is None else far_kernel,
         grid_spec=pltpu.PrefetchScalarGridSpec(
-            num_scalar_prefetch=1,
-            grid=(steps,),
-            in_specs=[whole] * count + [columns(j) for j in range(count)] + [sums] * len(more),
-            out_specs=pl.BlockSpec((TOK, lines), lambda i, order: (0, i)) if final else sums,
+            num_scalar_prefetch=0 if near is None else 1,
+            grid=(1,),
+            in_specs=[whole(a.shape) for a in args],
+            out_specs=whole(shape),
+            scratch_shapes=[] if near is None else [pltpu.VMEM((1024, TOK), F32)],
         ),
-        out_shape=shape,
-        compiler_params=pltpu.CompilerParams(vmem_limit_bytes=SMALL),
+        out_shape=jax.ShapeDtypeStruct(shape, kind),
+        compiler_params=pltpu.CompilerParams(vmem_limit_bytes=24 << 20),
         cost_estimate=pl.CostEstimate(flops=1 << 35, bytes_accessed=6 << 20, transcendentals=0),
-        name="project_last" if final else "project_first",
-    )(order, *pieces, *([weight] * count), *more)
-
-
-def gather_weight(weight, after):
+        name="near" if near is None else "far",
+    )(*([] if near is None else [place]), *args)
+
+
+def ring(axis, step):
+    return axis, [(a, (a + step) % 4) for a in range(4)]
+
+
+def beside(piece, axis):
+    return lax.ppermute(piece, *ring(axis, 1)), lax.ppermute(piece, *ring(axis, -1))
+
+
+def opposite(left, right, axis):
+    return lax.ppermute(left, *ring(axis, 1)), lax.ppermute(right, *ring(axis, -1))
+
+
+def around(piece, axis):
+    left, right = beside(piece, axis)
+    return piece, left, opposite(left[0], right[1], axis), right
+
+
+def stacked(pieces):
+    own, left, (opp0, opp1), right = pieces
+    return jnp.stack([jnp.stack([own[c], left[c], opp, right[c]]) for c, opp in enumerate((opp0, opp1))])
+
+
+def gather_weight(weight, chan, after):
     pieces = [weight] + [
         lax.ppermute(weight, "z", [(a, (a + d) % 4) for a in range(4)]) for d in (1, 2, 3)
     ]
     *pieces, after = lax.optimization_barrier((*pieces, after))
-    full = lax.all_gather(jnp.stack(pieces)[None], ("y", "x"), axis=0, tiled=True)
-    return full.reshape((4, 4, 4) + weight.shape), after
+    width = weight.shape[1] // 4
+    rows = jnp.stack(pieces)
+    near, far = [
+        jnp.stack([lax.dynamic_slice_in_dim(rows, (chan ^ j) * width, width, 2) for j in pair])
+        for pair in ((0, 1), (2, 3))
+    ]
+    far = stacked(around(far, "x"))
+    near = stacked(around(near, "y"))
+    return (near, *beside(near, "x")), (far, *beside(far, "y")), after
 
 
 def exchange(send):
@@ -303,23 +342,28 @@
     index = (lax.axis_index("y") * 4 + lax.axis_index("z")) * 4 + lax.axis_index("x")
     turned = (2 * index + jnp.arange(2) > CLASSES // 2).astype(jnp.int32)
     send = prep(turned, key, value, spectra.reshape((4,) + spectra.shape[2:]))
-    full_weight, send = gather_weight(weight, send)
+    h, k = lax.axis_index("h"), lax.axis_index("k")
+    (near_own, *near), (far_own, *far), send = gather_weight(weight, h * 2 + k, send)
     send, query, key, value, gain = lax.optimization_barrier((send, query, key, value, gain))
     got = exchange(send)
     query_t, direct_t = prep_g(query, key, value, gain[None, :])
-    y = exchange(convolve(got))
+    y = convolve(got)
+    y, near, far = lax.optimization_barrier((y, near, far))
+    y = exchange(y)
+    opposites = opposite(near[0][0], near[1][1], "x")
+    relay = far[0][0], far[1][1]
+    y, opposites, relay = lax.optimization_barrier((y, opposites, relay))
+    near_weight = near_own, near[0], opposites, near[1]
     gated = gate(y, query_t, direct_t)
     over_k = lax.ppermute(gated, "k", swap)
-    gated, over_k = lax.optimization_barrier((gated, over_k))
     over_h = lax.ppermute(gated, "h", swap)
-    h, k, z = lax.axis_index("h"), lax.axis_index("k"), lax.axis_index("z")
-    near = jnp.stack([h * 2 + k, h * 2 + 1 - k, z]).astype(jnp.int32)
-    far = jnp.stack([(1 - h) * 2 + k, (1 - h) * 2 + 1 - k, z]).astype(jnp.int32)
-    near, far = lax.optimization_barrier((near, far))
-    total = project(near, (gated, over_k), full_weight)
+    over_k, relay = lax.optimization_barrier((over_k, relay))
+    place = jnp.stack([lax.axis_index(axis) for axis in ("y", "z", "x")]).astype(jnp.int32)
+    total = project(place, (gated, over_k), near_weight)
     over_h, total = lax.optimization_barrier((over_h, total))
     over_hk = lax.ppermute(over_h, "k", swap)
-    return project(far, (over_h, over_hk), full_weight, total)
+    far_weight = far_own, far[0], opposite(*relay, "y"), far[1]
+    return project(place, (over_h, over_hk), far_weight, total)
 
 
 def solution(mesh):

time: 176 us -> 168 us (0.955)
  the two profiles are of different devices: /device:TPU:1 before, /device:TPU:65 now
where the time goes in v3:
time: 168 us
  waiting for transfers between devices  82.7 us (49%)
  starting transfers between devices  47.1 us (28%)
  Pallas kernels  27.2 us (16%)
  local copies, waits for them, and re-layouts  8.09 us (5%)
  other arithmetic  2.23 us (1%)
    ppermute x1, waiting for transfers between devices, local(): over_h = lax.ppermute(gated, 'h', swap)  19.3 us
    all_to_all x2, starting transfers between devices, exchange(): got = lax.all_to_all(send, SEQ, split_axis=0, concat_axis=0, tiled=True)  18.1 us
    ppermute x4, waiting for transfers between devices, beside(): lax.ppermute(piece, *ring(axis, -1))  16.2 us
    all_to_all x2, waiting for transfers between devices, exchange(): got = lax.all_to_all(send, SEQ, split_axis=0, concat_axis=0, tiled=True)  14.8 us
    pallas_call x1, Pallas kernels, convolve(): pl.pallas_call(functools.partial(convolve_kernel, group), grid=(1,), in_s...  13.9 us
    ppermute x4, waiting for transfers between devices, opposite(): lax.ppermute(right, *ring(axis, -1))  11.2 us
    ppermute x4, waiting for transfers between devices, beside(): lax.ppermute(piece, *ring(axis, 1))  9.28 us
    ppermute x4, starting transfers between devices, beside(): lax.ppermute(piece, *ring(axis, -1))  7.95 us
  transfers between devices with their start and end apart: 24, of which 10 were waited for; matrix products, arithmetic and copies ran while one was open for 4% of the time, Pallas kernels for 14%

profile of v3, /device:TPU:65, one launch (start us, length us, event | category | flops | bytes accessed | tf_op | source)
XLA Modules:
  0.0 167.7 jit_solution(17522930677030586191)
XLA Ops:
  0.0 1.6 collective-permute-start
  1.6 1.2 collective-permute-start.2
  2.8 0.5 compare_convert_fusion.turned_ref
  3.3 5.0 %prep.1 = bf16[1024,1280]{1,0:T(8,128)(2,1)} custom-call(s32[2]{0:T(128)} %compare_convert_fusion.turned_ref, bf16[256,1024]{1,0:T(8,128)(2,1)} %k_ref.2, bf16[256,1024]{1,0:T(8,128)(2,1)} %v_ref.2, f32[4,256,1024]{2,1,0:T(8,128)} %bitcast.52), custom_call_target="tpu_custom_call" | custom-call | tf_op jit(solution)/shard_map/prep/pallas_call | solution.py:73
  8.3 6.6 %collective-permute-done = bf16[16,4096]{1,0:T(8,128)(2,1)S(1)} collective-permute-done((bf16[16,4096]{1,0:T(8,128)(2,1)}, bf16[16,4096]{1,0:T(8,128)(2,1)S(1)}, u32[]{:S(2)}, u32[]{:S(2)}) %collective-permute-start) | collective-permute-done | bytes 131104 | tf_op jit(solution)/shard_map/ppermute | solution.py:320
  15.0 9.6 %all-to-all-start = ((bf16[64,16,1280]{2,1,0:T(8,128)(2,1)}), bf16[64,16,1280]{2,1,0:T(8,128)(2,1)}, u32[]{:S(2)}, u32[]{:S(2)}) async-start(bf16[64,16,1280]{2,1,0:T(8,128)(2,1)} %bitcast.51), calls=%async_computation | async-start | bytes 5242880 | tf_op jit(solution)/shard_map/all_to_all | solution.py:336
  24.6 0.1 pad_maximum_fusion.2
  24.8 2.7 %collective-permute-start.5 = (bf16[2,4,16,1024]{3,2,1,0:T(8,128)(2,1)S(1)}, bf16[2,4,16,1024]{3,2,1,0:T(8,128)(2,1)S(1)}, u32[]{:S(2)}, u32[]{:S(2)}) collective-permute-start(bf16[2,4,16,1024]{3,2,1,0:T(8,128)(2,1)S(1)} %pad_maximum_fusion.3), channel_id=1, source_target_pairs={{0,192},{64,0},{128,64},{192,128},{1,193},{65,1},{129,65},{193,129... | collective-permute-start | bytes 786440 | tf_op jit(solution)/shard_map/ppermute | solution.py:301
  27.5 2.5 %collective-permute-start.11 = (bf16[2,4,16,1024]{3,2,1,0:T(8,128)(2,1)S(1)}, bf16[2,4,16,1024]{3,2,1,0:T(8,128)(2,1)S(1)}, u32[]{:S(2)}, u32[]{:S(2)}) collective-permute-start(bf16[2,4,16,1024]{3,2,1,0:T(8,128)(2,1)S(1)} %pad_maximum_fusion.4), channel_id=1, source_target_pairs={{0,12},{4,0},{8,4},{12,8},{1,13},{5,1},{9,5},{13,9},{2,14},{6,2},{... | collective-permute-start | bytes 786440 | tf_op jit(solution)/shard_map/ppermute | solution.py:301
  30.0 6.7 %collective-permute-done.5 = bf16[2,4,16,1024]{3,2,1,0:T(8,128)(2,1)S(1)} collective-permute-done((bf16[2,4,16,1024]{3,2,1,0:T(8,128)(2,1)S(1)}, bf16[2,4,16,1024]{3,2,1,0:T(8,128)(2,1)S(1)}, u32[]{:S(2)}, u32[]{:S(2)}) %collective-permute-start.5) | collective-permute-done | bytes 262176 | tf_op jit(solution)/shard_map/ppermute | solution.py:301
  36.7 3.7 %collective-permute-start.6 = (bf16[4,16,1024]{2,1,0:T(8,128)(2,1)S(1)}, bf16[4,16,1024]{2,1,0:T(8,128)(2,1)S(1)}, u32[]{:S(2)}, u32[]{:S(2)}) collective-permute-start(bf16[4,16,1024]{2,1,0:T(8,128)(2,1)S(1)} %get-tuple-element.73), channel_id=1, source_target_pairs={{0,192},{64,0},{128,64},{192,128},{1,193},{65,1},{129,65},{193,129... | collective-permute-start | bytes 393224 | tf_op jit(solution)/shard_map/ppermute | solution.py:305
  40.5 9.5 %collective-permute-done.11 = bf16[2,4,16,1024]{3,2,1,0:T(8,128)(2,1)S(1)} collective-permute-done((bf16[2,4,16,1024]{3,2,1,0:T(8,128)(2,1)S(1)}, bf16[2,4,16,1024]{3,2,1,0:T(8,128)(2,1)S(1)}, u32[]{:S(2)}, u32[]{:S(2)}) %collective-permute-start.11) | collective-permute-done | bytes 262176 | tf_op jit(solution)/shard_map/ppermute | solution.py:301
  50.0 0.1 collective-permute-start.12
  50.2 1.5 collective-permute-start.10
  51.7 9.3 %collective-permute-done.3 = bf16[2,4,16,1024]{3,2,1,0:T(8,128)(2,1)S(1)} collective-permute-done((bf16[2,4,16,1024]{3,2,1,0:T(8,128)(2,1)S(1)}, bf16[2,4,16,1024]{3,2,1,0:T(8,128)(2,1)S(1)}, u32[]{:S(2)}, u32[]{:S(2)}) %collective-permute-start.3) | collective-permute-done | bytes 262176 | tf_op jit(solution)/shard_map/ppermute | solution.py:301
  61.0 0.1 collective-permute-start.4
  61.1 0.1 maximum_bitcast_fusion.3
  61.2 0.1 maximum_bitcast_fusion.2
  61.3 0.1 pad_maximum_fusion.1.own
  61.4 2.7 %collective-permute-start.14 = (bf16[2,4,4,16,1024]{4,3,2,1,0:T(8,128)(2,1)S(1)}, bf16[2,4,4,16,1024]{4,3,2,1,0:T(8,128)(2,1)}, u32[]{:S(2)}, u32[]{:S(2)}) collective-permute-start(bf16[2,4,4,16,1024]{4,3,2,1,0:T(8,128)(2,1)S(1)} %pad_maximum_fusion.1.own), channel_id=1, source_target_pairs={{0,192},{64,0},{128,64},{192,128},{1,193},{65,1},{129,65},{193,129... | collective-permute-start | bytes 3145736 | tf_op jit(solution)/shard_map/ppermute | solution.py:301
  64.2 2.3 %collective-permute-done.4 = bf16[4,16,1024]{2,1,0:T(8,128)(2,1)S(1)} collective-permute-done((bf16[4,16,1024]{2,1,0:T(8,128)(2,1)S(1)}, bf16[4,16,1024]{2,1,0:T(8,128)(2,1)S(1)}, u32[]{:S(2)}, u32[]{:S(2)}) %collective-permute-start.4) | collective-permute-done | bytes 131104 | tf_op jit(solution)/shard_map/ppermute | solution.py:305
  66.6 1.1 pad_maximum_fusion.own
  67.7 1.5 collective-permute-start.7
  69.2 14.8 %all-to-all-done = bf16[64,16,1280]{2,1,0:T(8,128)(2,1)} async-done(((bf16[64,16,1280]{2,1,0:T(8,128)(2,1)}), bf16[64,16,1280]{2,1,0:T(8,128)(2,1)}, u32[]{:S(2)}, u32[]{:S(2)}) %all-to-all-start) | async-done | bytes 2621472 | tf_op jit(solution)/shard_map/all_to_all | solution.py:336
  84.0 13.9 %convolve.1 = bf16[1024,256]{1,0:T(8,128)(2,1)} custom-call(bf16[1024,1280]{1,0:T(8,128)(2,1)} %bitcast.5.r_ref, bf16[2,72,128]{2,1,0:T(8,128)(2,1)} %constant.45.clone.fold_any, bf16[144,128]{1,0:T(8,128)(2,1)} %constant.46.clone.first_any, bf16[128,144]{1,0:T(8,128)(2,1)} %constant.47.clone.last_any, bf16[1536,256]{1,0:T(8,128)(2,1)} %constant.48.clone.row_any, ...), custom_call_target="tpu_custom_call" | custom-call | flops 17179869184 | bytes 4194304 | tf_op jit(solution)/shard_map/convolve/pallas_call | solution.py:186
  98.0 8.5 %all-to-all-start.1 = ((bf16[64,16,256]{2,1,0:T(8,128)(2,1)}), bf16[64,16,256]{2,1,0:T(8,128)(2,1)S(1)}, u32[]{:S(2)}, u32[]{:S(2)}) async-start(bf16[64,16,256]{2,1,0:T(8,128)(2,1)} %bitcast.53), calls=%async_computation.1 | async-start | bytes 1048576 | tf_op jit(solution)/shard_map/all_to_all | solution.py:336
  106.5 1.1 slice_bitcast_fusion.3
  107.6 1.1 slice_bitcast_fusion.2
  108.7 2.5 %collective-permute-start.16 = (bf16[4,4,16,1024]{3,2,1,0:T(8,128)(2,1)S(1)}, bf16[4,4,16,1024]{3,2,1,0:T(8,128)(2,1)S(1)}, u32[]{:S(2)}, u32[]{:S(2)}) collective-permute-start(bf16[4,4,16,1024]{3,2,1,0:T(8,128)(2,1)S(1)} %slice_bitcast_fusion.2), channel_id=1, source_target_pairs={{0,12},{4,0},{8,4},{12,8},{1,13},{5,1},{9,5},{13,9},{2,14},{6,2},{... | collective-permute-start | bytes 1572872 | tf_op jit(solution)/shard_map/ppermute | solution.py:305
  111.2 0.7 prep_g.1
  111.9 1.8 %slice_bitcast_fusion = (bf16[4,4,16,1024]{3,2,1,0:T(8,128)(2,1)S(1)}, bf16[4,4,16,1024]{3,2,1,0:T(8,128)(2,1)S(1)}) fusion(bf16[2,4,4,16,1024]{4,3,2,1,0:T(8,128)(2,1)} %collective-permute-done.14.right, bf16[2,4,4,16,1024]{4,3,2,1,0:T(8,128)(2,1)} %collective-permute-done.13.left), kind=kLoop, calls=%fused_computation.7 | loop fusion | bytes 2097152 | tf_op jit(solution)/shard_map/squeeze | solution.py:354
  113.7 11.2 %collective-permute-done.16.opp1 = bf16[4,4,16,1024]{3,2,1,0:T(8,128)(2,1)S(1)} collective-permute-done((bf16[4,4,16,1024]{3,2,1,0:T(8,128)(2,1)S(1)}, bf16[4,4,16,1024]{3,2,1,0:T(8,128)(2,1)S(1)}, u32[]{:S(2)}, u32[]{:S(2)}) %collective-permute-start.16) | collective-permute-done | bytes 524320 | tf_op jit(solution)/shard_map/ppermute | solution.py:305
  125.0 0.8 copy-done.8
  125.8 1.5 collective-permute-done.15.opp0
  127.3 0.8 copy-done.10
  128.1 1.2 copy-done.3
  129.3 1.0 copy-done.6
  130.3 0.2 gate.1.g0
  130.5 1.9 %collective-permute-start.18 = (bf16[1024,256]{1,0:T(8,128)(2,1)S(1)}, bf16[1024,256]{1,0:T(8,128)(2,1)S(1)}, u32[]{:S(2)}, u32[]{:S(2)}) collective-permute-start(bf16[1024,256]{1,0:T(8,128)(2,1)S(1)} %gate.1.g0), channel_id=1, source_target_pairs={{0,1},{1,0},{2,3},{3,2},{4,5},{5,4},{6,7},{7,6},{8,9},{9,8},{10,11... | collective-permute-start | bytes 1572872 | tf_op jit(solution)/shard_map/ppermute | solution.py:358
  132.4 3.8 %collective-permute-start.17 = (bf16[1024,256]{1,0:T(8,128)(2,1)S(1)}, bf16[1024,256]{1,0:T(8,128)(2,1)S(1)}, u32[]{:S(2)}, u32[]{:S(2)}) collective-permute-start(bf16[1024,256]{1,0:T(8,128)(2,1)S(1)} %gate.1.g0), channel_id=1, source_target_pairs={{0,2},{2,0},{1,3},{3,1},{4,6},{6,4},{5,7},{7,5},{8,10},{10,8},{9,1... | collective-permute-start | bytes 1572872 | tf_op jit(solution)/shard_map/ppermute | solution.py:359
  136.2 1.2 collective-permute-start.20
  137.4 1.5 collective-permute-start.21
  138.9 3.1 %near.1.near_ref = f32[1024,256]{1,0:T(8,128)S(1)} custom-call(bf16[1024,256]{1,0:T(8,128)(2,1)S(1)} %gate.1.g0, bf16[1024,256]{1,0:T(8,128)(2,1)S(1)} %collective-permute-done.18.g1, bf16[2,4,4,16,1024]{4,3,2,1,0:T(8,128)(2,1)} %pad_maximum_fusion.own, bf16[2,4,4,16,1024]{4,3,2,1,0:T(8,128)(2,1)} %collective-permute-done.7.left, ...), custom_call_target="tpu_custom_call" | custom-call | flops 34359738368 | bytes 6291456 | tf_op jit(solution)/shard_map/near/pallas_call | solution.py:280
  142.0 19.3 %collective-permute-done.17.g0 = bf16[1024,256]{1,0:T(8,128)(2,1)S(1)} collective-permute-done((bf16[1024,256]{1,0:T(8,128)(2,1)S(1)}, bf16[1024,256]{1,0:T(8,128)(2,1)S(1)}, u32[]{:S(2)}, u32[]{:S(2)}) %collective-permute-start.17) | collective-permute-done | bytes 524320 | tf_op jit(solution)/shard_map/ppermute | solution.py:359
  161.3 0.4 collective-permute-start.19
  161.8 0.1 pad_add_fusion.place_ref
  161.9 1.5 collective-permute-done.19.g1
  163.3 4.4 %far.1 = bf16[256,1024]{1,0:T(8,128)(2,1)} custom-call(s32[3]{0:T(128)S(1)} %pad_add_fusion.place_ref, bf16[1024,256]{1,0:T(8,128)(2,1)S(1)} %collective-permute-done.17.g0, bf16[1024,256]{1,0:T(8,128)(2,1)S(1)} %collective-permute-done.19.g1, bf16[2,4,4,16,1024]{4,3,2,1,0:T(8,128)(2,1)S(1)} %pad_maximum_fusion.1.own, ...), custom_call_target="tpu_custom_call" | custom-call | flops 34359738368 | bytes 6291456 | tf_op jit(solution)/shard_map/far/pallas_call | solution.py:280
  (51 shorter events, 0.5 us)
Async XLA Ops:
  0.0 8.3 %collective-permute-start.1 = (bf16[16,4096]{1,0:T(8,128)(2,1)}, bf16[16,4096]{1,0:T(8,128)(2,1)S(1)}, u32[]{:S(2)}, u32[]{:S(2)}) collective-permute-start(bf16[16,4096]{1,0:T(8,128)(2,1)} %param.16), channel_id=1, source_target_pairs={{0,32},{16,48},{32,0},{48,16},{1,33},{17,49},{33,1},{49,17},{2,34}... | collective-permute-start | bytes 393224 | tf_op jit(solution)/shard_map/ppermute | solution.py:320
  0.0 15.0 %collective-permute-start = (bf16[16,4096]{1,0:T(8,128)(2,1)}, bf16[16,4096]{1,0:T(8,128)(2,1)S(1)}, u32[]{:S(2)}, u32[]{:S(2)}) collective-permute-start(bf16[16,4096]{1,0:T(8,128)(2,1)} %param.16), channel_id=1, source_target_pairs={{0,16},{16,32},{32,48},{48,0},{1,17},{17,33},{33,49},{49,1},{2,18}... | collective-permute-start | bytes 393224 | tf_op jit(solution)/shard_map/ppermute | solution.py:320
  1.6 13.3 %collective-permute-start.2 = (bf16[16,4096]{1,0:T(8,128)(2,1)}, bf16[16,4096]{1,0:T(8,128)(2,1)S(1)}, u32[]{:S(2)}, u32[]{:S(2)}) collective-permute-start(bf16[16,4096]{1,0:T(8,128)(2,1)} %param.16), channel_id=1, source_target_pairs={{0,48},{16,0},{32,16},{48,32},{1,49},{17,1},{33,17},{49,33},{2,50}... | collective-permute-start | bytes 393224 | tf_op jit(solution)/shard_map/ppermute | solution.py:320
  15.0 9.6 %copy-start.12 = (bf16[16,4096]{1,0:T(8,128)(2,1)S(1)}, bf16[16,4096]{1,0:T(8,128)(2,1)}, u32[]{:S(2)}) copy-start(bf16[16,4096]{1,0:T(8,128)(2,1)} %param.16) | copy-start | bytes 393220
  15.0 69.0 %all-to-all-start = ((bf16[64,16,1280]{2,1,0:T(8,128)(2,1)}), bf16[64,16,1280]{2,1,0:T(8,128)(2,1)}, u32[]{:S(2)}, u32[]{:S(2)}) async-start(bf16[64,16,1280]{2,1,0:T(8,128)(2,1)} %bitcast.51), calls=%async_computation | async-start | bytes 5242880 | tf_op jit(solution)/shard_map/all_to_all | solution.py:336
  24.8 11.9 %collective-permute-start.5 = (bf16[2,4,16,1024]{3,2,1,0:T(8,128)(2,1)S(1)}, bf16[2,4,16,1024]{3,2,1,0:T(8,128)(2,1)S(1)}, u32[]{:S(2)}, u32[]{:S(2)}) collective-permute-start(bf16[2,4,16,1024]{3,2,1,0:T(8,128)(2,1)S(1)} %pad_maximum_fusion.3), channel_id=1, source_target_pairs={{0,192},{64,0},{128,64},{192,128},{1,193},{65,1},{129,65},{193,129... | collective-permute-start | bytes 786440 | tf_op jit(solution)/shard_map/ppermute | solution.py:301
  27.5 22.5 %collective-permute-start.11 = (bf16[2,4,16,1024]{3,2,1,0:T(8,128)(2,1)S(1)}, bf16[2,4,16,1024]{3,2,1,0:T(8,128)(2,1)S(1)}, u32[]{:S(2)}, u32[]{:S(2)}) collective-permute-start(bf16[2,4,16,1024]{3,2,1,0:T(8,128)(2,1)S(1)} %pad_maximum_fusion.4), channel_id=1, source_target_pairs={{0,12},{4,0},{8,4},{12,8},{1,13},{5,1},{9,5},{13,9},{2,14},{6,2},{... | collective-permute-start | bytes 786440 | tf_op jit(solution)/shard_map/ppermute | solution.py:301
  30.0 30.9 %collective-permute-start.3 = (bf16[2,4,16,1024]{3,2,1,0:T(8,128)(2,1)S(1)}, bf16[2,4,16,1024]{3,2,1,0:T(8,128)(2,1)S(1)}, u32[]{:S(2)}, u32[]{:S(2)}) collective-permute-start(bf16[2,4,16,1024]{3,2,1,0:T(8,128)(2,1)S(1)} %pad_maximum_fusion.3), channel_id=1, source_target_pairs={{0,64},{64,128},{128,192},{192,0},{1,65},{65,129},{129,193},{193,1... | collective-permute-start | bytes 786440 | tf_op jit(solution)/shard_map/ppermute | solution.py:301
  30.0 20.1 %collective-permute-start.9 = (bf16[2,4,16,1024]{3,2,1,0:T(8,128)(2,1)S(1)}, bf16[2,4,16,1024]{3,2,1,0:T(8,128)(2,1)S(1)}, u32[]{:S(2)}, u32[]{:S(2)}) collective-permute-start(bf16[2,4,16,1024]{3,2,1,0:T(8,128)(2,1)S(1)} %pad_maximum_fusion.4), channel_id=1, source_target_pairs={{0,4},{4,8},{8,12},{12,0},{1,5},{5,9},{9,13},{13,1},{2,6},{6,10},{... | collective-permute-start | bytes 786440 | tf_op jit(solution)/shard_map/ppermute | solution.py:301
  36.7 27.4 %collective-permute-start.6 = (bf16[4,16,1024]{2,1,0:T(8,128)(2,1)S(1)}, bf16[4,16,1024]{2,1,0:T(8,128)(2,1)S(1)}, u32[]{:S(2)}, u32[]{:S(2)}) collective-permute-start(bf16[4,16,1024]{2,1,0:T(8,128)(2,1)S(1)} %get-tuple-element.73), channel_id=1, source_target_pairs={{0,192},{64,0},{128,64},{192,128},{1,193},{65,1},{129,65},{193,129... | collective-permute-start | bytes 393224 | tf_op jit(solution)/shard_map/ppermute | solution.py:305
  50.0 11.1 %collective-permute-start.12 = (bf16[4,16,1024]{2,1,0:T(8,128)(2,1)S(1)}, bf16[4,16,1024]{2,1,0:T(8,128)(2,1)S(1)}, u32[]{:S(2)}, u32[]{:S(2)}) collective-permute-start(bf16[4,16,1024]{2,1,0:T(8,128)(2,1)S(1)} %get-tuple-element.67), channel_id=1, source_target_pairs={{0,12},{4,0},{8,4},{12,8},{1,13},{5,1},{9,5},{13,9},{2,14},{6,2},{... | collective-permute-start | bytes 393224 | tf_op jit(solution)/shard_map/ppermute | solution.py:305
  50.2 11.0 %collective-permute-start.10 = (bf16[4,16,1024]{2,1,0:T(8,128)(2,1)S(1)}, bf16[4,16,1024]{2,1,0:T(8,128)(2,1)S(1)}, u32[]{:S(2)}, u32[]{:S(2)}) collective-permute-start(bf16[4,16,1024]{2,1,0:T(8,128)(2,1)S(1)} %get-tuple-element.64), channel_id=1, source_target_pairs={{0,4},{4,8},{8,12},{12,0},{1,5},{5,9},{9,13},{13,1},{2,6},{6,10},{... | collective-permute-start | bytes 393224 | tf_op jit(solution)/shard_map/ppermute | solution.py:305
  61.0 5.5 %collective-permute-start.4 = (bf16[4,16,1024]{2,1,0:T(8,128)(2,1)S(1)}, bf16[4,16,1024]{2,1,0:T(8,128)(2,1)S(1)}, u32[]{:S(2)}, u32[]{:S(2)}) collective-permute-start(bf16[4,16,1024]{2,1,0:T(8,128)(2,1)S(1)} %get-tuple-element.70), channel_id=1, source_target_pairs={{0,64},{64,128},{128,192},{192,0},{1,65},{65,129},{129,193},{193,1... | collective-permute-start | bytes 393224 | tf_op jit(solution)/shard_map/ppermute | solution.py:305
  61.4 36.5 %collective-permute-start.14 = (bf16[2,4,4,16,1024]{4,3,2,1,0:T(8,128)(2,1)S(1)}, bf16[2,4,4,16,1024]{4,3,2,1,0:T(8,128)(2,1)}, u32[]{:S(2)}, u32[]{:S(2)}) collective-permute-start(bf16[2,4,4,16,1024]{4,3,2,1,0:T(8,128)(2,1)S(1)} %pad_maximum_fusion.1.own), channel_id=1, source_target_pairs={{0,192},{64,0},{128,64},{192,128},{1,193},{65,1},{129,65},{193,129... | collective-permute-start | bytes 3145736 | tf_op jit(solution)/shard_map/ppermute | solution.py:301
  64.1 33.8 %collective-permute-start.13 = (bf16[2,4,4,16,1024]{4,3,2,1,0:T(8,128)(2,1)S(1)}, bf16[2,4,4,16,1024]{4,3,2,1,0:T(8,128)(2,1)}, u32[]{:S(2)}, u32[]{:S(2)}) collective-permute-start(bf16[2,4,4,16,1024]{4,3,2,1,0:T(8,128)(2,1)S(1)} %pad_maximum_fusion.1.own), channel_id=1, source_target_pairs={{0,64},{64,128},{128,192},{192,0},{1,65},{65,129},{129,193},{193,1... | collective-permute-start | bytes 3145736 | tf_op jit(solution)/shard_map/ppermute | solution.py:301
  67.7 30.2 %collective-permute-start.8 = (bf16[2,4,4,16,1024]{4,3,2,1,0:T(8,128)(2,1)}, bf16[2,4,4,16,1024]{4,3,2,1,0:T(8,128)(2,1)}, u32[]{:S(2)}, u32[]{:S(2)}) collective-permute-start(bf16[2,4,4,16,1024]{4,3,2,1,0:T(8,128)(2,1)} %pad_maximum_fusion.own), channel_id=1, source_target_pairs={{0,12},{4,0},{8,4},{12,8},{1,13},{5,1},{9,5},{13,9},{2,14},{6,2},{... | collective-permute-start | bytes 3145736 | tf_op jit(solution)/shard_map/ppermute | solution.py:301
  67.7 30.2 %collective-permute-start.7 = (bf16[2,4,4,16,1024]{4,3,2,1,0:T(8,128)(2,1)}, bf16[2,4,4,16,1024]{4,3,2,1,0:T(8,128)(2,1)}, u32[]{:S(2)}, u32[]{:S(2)}) collective-permute-start(bf16[2,4,4,16,1024]{4,3,2,1,0:T(8,128)(2,1)} %pad_maximum_fusion.own), channel_id=1, source_target_pairs={{0,4},{4,8},{8,12},{12,0},{1,5},{5,9},{9,13},{13,1},{2,6},{6,10},{... | collective-permute-start | bytes 3145736 | tf_op jit(solution)/shard_map/ppermute | solution.py:301
  97.9 13.3 %copy-start = (bf16[256,1024]{1,0:T(8,128)(2,1)S(1)}, bf16[256,1024]{1,0:T(8,128)(2,1)}, u32[]{:S(2)}) copy-start(bf16[256,1024]{1,0:T(8,128)(2,1)} %k_ref.2) | copy-start | bytes 1572868
  97.9 13.3 %copy-start.1 = (bf16[256,1024]{1,0:T(8,128)(2,1)S(1)}, bf16[256,1024]{1,0:T(8,128)(2,1)}, u32[]{:S(2)}) copy-start(bf16[256,1024]{1,0:T(8,128)(2,1)} %v_ref.2) | copy-start | bytes 1572868
  97.9 13.3 %copy-start.4 = (bf16[256,1024]{1,0:T(8,128)(2,1)S(1)}, bf16[256,1024]{1,0:T(8,128)(2,1)}, u32[]{:S(2)}) copy-start(bf16[256,1024]{1,0:T(8,128)(2,1)} %q_ref) | copy-start | bytes 1572868
  97.9 13.3 %copy-start.7 = (f32[1024]{0:T(1024)S(1)}, f32[1024]{0:T(1024)}, u32[]{:S(2)}) copy-start(f32[1024]{0:T(1024)} %param.15) | copy-start | bytes 12292
  98.0 30.1 %all-to-all-start.1 = ((bf16[64,16,256]{2,1,0:T(8,128)(2,1)}), bf16[64,16,256]{2,1,0:T(8,128)(2,1)S(1)}, u32[]{:S(2)}, u32[]{:S(2)}) async-start(bf16[64,16,256]{2,1,0:T(8,128)(2,1)} %bitcast.53), calls=%async_computation.1 | async-start | bytes 1048576 | tf_op jit(solution)/shard_map/all_to_all | solution.py:336
  108.7 16.3 %collective-permute-start.16 = (bf16[4,4,16,1024]{3,2,1,0:T(8,128)(2,1)S(1)}, bf16[4,4,16,1024]{3,2,1,0:T(8,128)(2,1)S(1)}, u32[]{:S(2)}, u32[]{:S(2)}) collective-permute-start(bf16[4,4,16,1024]{3,2,1,0:T(8,128)(2,1)S(1)} %slice_bitcast_fusion.2), channel_id=1, source_target_pairs={{0,12},{4,0},{8,4},{12,8},{1,13},{5,1},{9,5},{13,9},{2,14},{6,2},{... | collective-permute-start | bytes 1572872 | tf_op jit(solution)/shard_map/ppermute | solution.py:305
  111.1 16.1 %collective-permute-start.15 = (bf16[4,4,16,1024]{3,2,1,0:T(8,128)(2,1)S(1)}, bf16[4,4,16,1024]{3,2,1,0:T(8,128)(2,1)S(1)}, u32[]{:S(2)}, u32[]{:S(2)}) collective-permute-start(bf16[4,4,16,1024]{3,2,1,0:T(8,128)(2,1)S(1)} %slice_bitcast_fusion.3), channel_id=1, source_target_pairs={{0,4},{4,8},{8,12},{12,0},{1,5},{5,9},{9,13},{13,1},{2,6},{6,10},{... | collective-permute-start | bytes 1572872 | tf_op jit(solution)/shard_map/ppermute | solution.py:305
  111.9 13.1 %copy-start.2 = (f32[1024,256]{1,0:T(8,128)}, f32[1024,256]{1,0:T(8,128)S(1)}, u32[]{:S(2)}) copy-start(f32[1024,256]{1,0:T(8,128)S(1)} %get-tuple-element.49.c_ref) | copy-start | bytes 3145732
  111.9 13.1 %copy-start.5 = (bf16[1024,256]{1,0:T(8,128)(2,1)}, bf16[1024,256]{1,0:T(8,128)(2,1)S(1)}, u32[]{:S(2)}) copy-start(bf16[1024,256]{1,0:T(8,128)(2,1)S(1)} %get-tuple-element.48.q_ref) | copy-start | bytes 1572868
  125.0 0.8 copy-start.8
  127.3 0.8 copy-start.10
  128.1 1.2 copy-start.3
  129.3 1.0 copy-start.6
  130.3 8.6 %copy-start.9 = (bf16[4,4,16,1024]{3,2,1,0:T(8,128)(2,1)S(1)}, bf16[4,4,16,1024]{3,2,1,0:T(8,128)(2,1)}, u32[]{:S(2)}) copy-start(bf16[4,4,16,1024]{3,2,1,0:T(8,128)(2,1)} %copy-done.8) | copy-start | bytes 1572868
  130.3 8.6 %copy-start.11 = (bf16[4,4,16,1024]{3,2,1,0:T(8,128)(2,1)S(1)}, bf16[4,4,16,1024]{3,2,1,0:T(8,128)(2,1)}, u32[]{:S(2)}) copy-start(bf16[4,4,16,1024]{3,2,1,0:T(8,128)(2,1)} %copy-done.10) | copy-start | bytes 1572868
  130.5 5.7 %collective-permute-start.18 = (bf16[1024,256]{1,0:T(8,128)(2,1)S(1)}, bf16[1024,256]{1,0:T(8,128)(2,1)S(1)}, u32[]{:S(2)}, u32[]{:S(2)}) collective-permute-start(bf16[1024,256]{1,0:T(8,128)(2,1)S(1)} %gate.1.g0), channel_id=1, source_target_pairs={{0,1},{1,0},{2,3},{3,2},{4,5},{5,4},{6,7},{7,6},{8,9},{9,8},{10,11... | collective-permute-start | bytes 1572872 | tf_op jit(solution)/shard_map/ppermute | solution.py:358
  132.4 28.9 %collective-permute-start.17 = (bf16[1024,256]{1,0:T(8,128)(2,1)S(1)}, bf16[1024,256]{1,0:T(8,128)(2,1)S(1)}, u32[]{:S(2)}, u32[]{:S(2)}) collective-permute-start(bf16[1024,256]{1,0:T(8,128)(2,1)S(1)} %gate.1.g0), channel_id=1, source_target_pairs={{0,2},{2,0},{1,3},{3,1},{4,6},{6,4},{5,7},{7,5},{8,10},{10,8},{9,1... | collective-permute-start | bytes 1572872 | tf_op jit(solution)/shard_map/ppermute | solution.py:359
  136.2 25.7 %collective-permute-start.20 = (bf16[4,4,16,1024]{3,2,1,0:T(8,128)(2,1)S(1)}, bf16[4,4,16,1024]{3,2,1,0:T(8,128)(2,1)S(1)}, u32[]{:S(2)}, u32[]{:S(2)}) collective-permute-start(bf16[4,4,16,1024]{3,2,1,0:T(8,128)(2,1)S(1)} %get-tuple-element.56), channel_id=1, source_target_pairs={{0,64},{64,128},{128,192},{192,0},{1,65},{65,129},{129,193},{193,1... | collective-permute-start | bytes 1572872 | tf_op jit(solution)/shard_map/ppermute | solution.py:305
  137.4 24.4 %collective-permute-start.21 = (bf16[4,4,16,1024]{3,2,1,0:T(8,128)(2,1)S(1)}, bf16[4,4,16,1024]{3,2,1,0:T(8,128)(2,1)S(1)}, u32[]{:S(2)}, u32[]{:S(2)}) collective-permute-start(bf16[4,4,16,1024]{3,2,1,0:T(8,128)(2,1)S(1)} %get-tuple-element.57), channel_id=1, source_target_pairs={{0,192},{64,0},{128,64},{192,128},{1,193},{65,1},{129,65},{193,129... | collective-permute-start | bytes 1572872 | tf_op jit(solution)/shard_map/ppermute | solution.py:305
  161.3 2.0 %collective-permute-start.19 = (bf16[1024,256]{1,0:T(8,128)(2,1)S(1)}, bf16[1024,256]{1,0:T(8,128)(2,1)S(1)}, u32[]{:S(2)}, u32[]{:S(2)}) collective-permute-start(bf16[1024,256]{1,0:T(8,128)(2,1)S(1)} %collective-permute-done.17.g0), channel_id=1, source_target_pairs={{0,1},{1,0},{2,3},{3,2},{4,5},{5,4},{6,7},{7,6},{8,9},{9,8},{10,11... | collective-permute-start | bytes 1572872 | tf_op jit(solution)/shard_map/ppermute | solution.py:364

commit v4 on v3

--- a/solution.py
+++ b/solution.py
@@ -17,6 +17,7 @@
 BIG = 56 << 20
 SMALL = 16 << 20
 KEPT = 72
+GATE = 256
 
 
 def split(table):
@@ -87,11 +88,11 @@
 GROUP = 8
 
 
-def widen(src, dst, columns):
+def widen(src, dst, columns, base):
     def chunk(i, _):
         rows = pl.ds(pl.multiple_of(i * 64, 64), 64)
         for c in range(columns):
-            dst[c, rows, :] = src[rows, c * 128 : c * 128 + 128].astype(F32)
+            dst[base + c, rows, :] = src[rows, c * 128 : c * 128 + 128].astype(F32)
         return 0
 
     lax.fori_loop(0, src.shape[0] // 64, chunk, 0)
@@ -115,43 +116,62 @@
     return copies
 
 
-def convolve_kernel(group, r_ref, fold_any, first_any, last_any, row_any, turn_any, o_ref, xs, ys, fold_ref, first_ref, last_ref, row_ref, turn_ref, sems):
-    chans = r_ref.shape[0] // NSEQ
+def convolve_kernel(r_any, fold_any, first_any, last_any, row_any, turn_any, o_ref, rx, rs, xs, ys, freq, fold_ref, first_ref, last_ref, row_ref, turn_ref, sems):
+    chans = rx.shape[0] // NSEQ
     copies = fetch(
-        [(fold_any, fold_ref), (first_any, first_ref), (last_any, last_ref), (row_any, row_ref), (turn_any, turn_ref)],
+        [
+            (r_any.at[:, pl.ds(0, TOK)], rx),
+            (first_any, first_ref),
+            (turn_any, turn_ref),
+            (row_any, row_ref),
+            (r_any.at[:, pl.ds(TOK, 4 * TOK)], rs),
+            (fold_any, fold_ref),
+            (last_any, last_ref),
+        ],
         sems,
     )
-    widen(r_ref, xs, 10)
-    for copy in copies:
+    copies[0].wait()
+    widen(rx, xs, 2, 0)
+    for copy in copies[1:4]:
         copy.wait()
 
     def response(h, part):
         pair = [rows_of(xs, h, chans, 1 + 2 * part + e).astype(BF) for e in range(2)]
         return dot(fold_ref[part], jnp.concatenate(pair, 0))
 
-    def step(g, _):
+    def ahead(g, _):
         tc, ts = turn_ref[0], turn_ref[1]
         stacked = []
-        for j in range(group):
-            x = rows_of(xs, g * group + j, chans, 0).astype(BF)
+        for j in range(GROUP):
+            x = rows_of(xs, g * GROUP + j, chans, 0).astype(BF)
             a = dot(first_ref[...], jnp.concatenate([x, x], 0))
             ar, ai = a[:KEPT], a[KEPT:]
             ar, ai = parts(ar * tc + ai * ts), parts(ai * tc - ar * ts)
             stacked += [[jnp.concatenate([ar[n], ai[n]], 1), jnp.concatenate([ai[n], -ar[n]], 1)] for n in (0, 1)]
-        freq = row_section(stacked, row_ref)
+        size = GROUP * 2 * KEPT
+        freq[pl.ds(pl.multiple_of(g * size, size), size), :] = row_section(stacked, row_ref)
+        return 0
+
+    lax.fori_loop(0, chans // GROUP, ahead, 0)
+    for copy in copies[4:]:
+        copy.wait()
+    widen(rs, xs, 8, 2)
+
+    def back(g, _):
+        tc, ts = turn_ref[0], turn_ref[1]
         stacked = []
-        for j in range(group):
-            h = g * group + j
+        for j in range(GROUP):
+            h = g * GROUP + j
             rr, ri = response(h, 0), response(h, 1)
-            base = 2 * KEPT * j
-            xr, xi = freq[base : base + KEPT], freq[base + KEPT : base + 2 * KEPT]
+            base = pl.multiple_of(h * 2 * KEPT, 8)
+            xr, xi = freq[pl.ds(base, KEPT), :], freq[pl.ds(base + KEPT, KEPT), :]
             pr, pi = parts(rr * xr - ri * xi), parts(rr * xi + ri * xr)
             stacked += [[jnp.concatenate([pr[n], -pi[n]], 1), jnp.concatenate([pi[n], pr[n]], 1)] for n in (0, 1)]
-        back = row_section(stacked, row_ref)
-        for j in range(group):
-            h = g * group + j
+        rows = row_section(stacked, row_ref)
+        for j in range(GROUP):
+            h = g * GROUP + j
             base = 2 * KEPT * j
-            br, bi = back[base : base + KEPT], back[base + KEPT : base + 2 * KEPT]
+            br, bi = rows[base : base + KEPT], rows[base + KEPT : base + 2 * KEPT]
             hi, lo = parts(jnp.concatenate([br * tc - bi * ts, bi * tc + br * ts], 0))
             both = dot(last_ref[...], hi)
             y = both[:NSEQ] + both[NSEQ:] + dot(last_ref[:NSEQ], lo)
@@ -159,7 +179,7 @@
                 ys[c, pl.ds(h, NSEQ, stride=chans), :] = y[:, c * 128 : c * 128 + 128]
         return 0
 
-    lax.fori_loop(0, chans // group, step, 0)
+    lax.fori_loop(0, chans // GROUP, back, 0)
     for c in range(2):
         o_ref[:, c * 128 : c * 128 + 128] = ys[c].astype(BF)
 
@@ -180,64 +200,50 @@
     return pl.BlockSpec(shape, lambda i: (0,) * len(shape))
 
 
-def convolve(received, group=GROUP):
+def convolve(received):
     rows = received.shape[0]
     consts = constants()
     return pl.pallas_call(
-        functools.partial(convolve_kernel, group),
+        convolve_kernel,
         grid=(1,),
-        in_specs=[block(received.shape)] + [ANY] * len(consts),
+        in_specs=[ANY] * (1 + len(consts)),
         out_specs=block((rows, TOK)),
         out_shape=jax.ShapeDtypeStruct((rows, TOK), BF),
-        scratch_shapes=[pltpu.VMEM((10, rows, 128), F32), pltpu.VMEM((2, rows, 128), F32)]
+        scratch_shapes=[
+            pltpu.VMEM((rows, TOK), BF),
+            pltpu.VMEM((rows, 4 * TOK), BF),
+            pltpu.VMEM((10, rows, 128), F32),
+            pltpu.VMEM((2, rows, 128), F32),
+            pltpu.VMEM((rows // NSEQ * 2 * KEPT, TOK), F32),
+        ]
         + held(consts)
-        + [pltpu.SemaphoreType.DMA((len(consts),))],
+        + [pltpu.SemaphoreType.DMA((2 + len(consts),))],
         compiler_params=pltpu.CompilerParams(vmem_limit_bytes=BIG),
         cost_estimate=pl.CostEstimate(flops=16 << 30, bytes_accessed=4 << 20, transcendentals=0),
         name="convolve",
     )(received, *consts)
 
 
-def prep_g_kernel(q_ref, k_ref, v_ref, s_ref, qt_ref, ct_ref):
+def gate_kernel(y_ref, q_ref, k_ref, v_ref, s_ref, o_ref):
     conv = k_ref[...].astype(F32) * v_ref[...].astype(F32)
-    qt_ref[...] = q_ref[...].astype(F32).T.astype(BF)
-    ct_ref[...] = (s_ref[...] * conv).T
-
-
-def prep_g(query, key, value, gain):
-    width = key.shape[1]
-    blk = 512
+    direct = (s_ref[...] * conv).T
+    o_ref[...] = (q_ref[...].astype(F32).T * (y_ref[...].astype(F32) + direct)).astype(BF)
+
+
+def gate(y, query, key, value, gain):
+    width = y.shape[0]
+    blk = GATE
     tok = pl.BlockSpec((TOK, blk), lambda i: (0, i))
-    chan = pl.BlockSpec((blk, TOK), lambda i: (i, 0))
-    return pl.pallas_call(
-        prep_g_kernel,
-        grid=(width // blk,),
-        in_specs=[tok, tok, tok, pl.BlockSpec((1, blk), lambda i: (0, i))],
-        out_specs=[chan, chan],
-        out_shape=[jax.ShapeDtypeStruct((width, TOK), BF), jax.ShapeDtypeStruct((width, TOK), F32)],
-        compiler_params=pltpu.CompilerParams(vmem_limit_bytes=SMALL),
-        cost_estimate=pl.CostEstimate(flops=1 << 20, bytes_accessed=4 << 20, transcendentals=0),
-        name="prep_g",
-    )(query, key, value, gain)
-
-
-def gate_kernel(y_ref, q_ref, c_ref, o_ref):
-    o_ref[...] = (q_ref[...].astype(F32) * (y_ref[...].astype(F32) + c_ref[...])).astype(BF)
-
-
-def gate(y, query_t, direct_t):
-    width = y.shape[0]
-    blk = 512
     chan = pl.BlockSpec((blk, TOK), lambda i: (i, 0))
     return pl.pallas_call(
         gate_kernel,
         grid=(width // blk,),
-        in_specs=[chan] * 3,
+        in_specs=[chan, tok, tok, tok, pl.BlockSpec((1, blk), lambda i: (0, i))],
         out_specs=chan,
         out_shape=jax.ShapeDtypeStruct((width, TOK), BF),
         compiler_params=pltpu.CompilerParams(vmem_limit_bytes=SMALL),
         name="gate",
-    )(y, query_t, direct_t)
+    )(y, query, key, value, gain)
 
 
 def sum_terms(g_refs, w_refs, total):
@@ -346,18 +352,17 @@
     (near_own, *near), (far_own, *far), send = gather_weight(weight, h * 2 + k, send)
     send, query, key, value, gain = lax.optimization_barrier((send, query, key, value, gain))
     got = exchange(send)
-    query_t, direct_t = prep_g(query, key, value, gain[None, :])
     y = convolve(got)
     y, near, far = lax.optimization_barrier((y, near, far))
     y = exchange(y)
     opposites = opposite(near[0][0], near[1][1], "x")
     relay = far[0][0], far[1][1]
-    y, opposites, relay = lax.optimization_barrier((y, opposites, relay))
-    near_weight = near_own, near[0], opposites, near[1]
-    gated = gate(y, query_t, direct_t)
+    y, relay = lax.optimization_barrier((y, relay))
+    gated = gate(y, query, key, value, gain[None, :])
     over_k = lax.ppermute(gated, "k", swap)
     over_h = lax.ppermute(gated, "h", swap)
-    over_k, relay = lax.optimization_barrier((over_k, relay))
+    over_k, relay, opposites = lax.optimization_barrier((over_k, relay, opposites))
+    near_weight = near_own, near[0], opposites, near[1]
     place = jnp.stack([lax.axis_index(axis) for axis in ("y", "z", "x")]).astype(jnp.int32)
     total = project(place, (gated, over_k), near_weight)
     over_h, total = lax.optimization_barrier((over_h, total))

time: 168 us -> 162 us (0.964)
  the two profiles are of different devices: /device:TPU:65 before, /device:TPU:1 now
where the time goes in v4:
time: 162 us
  waiting for transfers between devices  73.6 us (45%)
  starting transfers between devices  55.7 us (34%)
  Pallas kernels  24.7 us (15%)
  local copies, waits for them, and re-layouts  6.28 us (4%)
    all_to_all x2, waiting for transfers between devices, exchange(): got = lax.all_to_all(send, SEQ, split_axis=0, concat_axis=0, tiled=True)  29.4 us
    all_to_all x2, starting transfers between devices, exchange(): got = lax.all_to_all(send, SEQ, split_axis=0, concat_axis=0, tiled=True)  20.2 us
    ppermute x1, waiting for transfers between devices, local(): over_h = lax.ppermute(gated, 'h', swap)  18.6 us
    ppermute x4, waiting for transfers between devices, beside(): lax.ppermute(piece, *ring(axis, -1))  18.5 us
    pallas_call x1, Pallas kernels, convolve(): pl.pallas_call(convolve_kernel, grid=(1,), in_specs=[ANY] * (1 + len(cons...  11.3 us
    ppermute x4, starting transfers between devices, beside(): lax.ppermute(piece, *ring(axis, -1))  10.7 us
    ppermute x4, starting transfers between devices, opposite(): lax.ppermute(right, *ring(axis, -1))  8.68 us
    pallas_call x2, Pallas kernels, project(): pl.pallas_call(near_kernel if near is None else far_kernel, grid_spec=plt...  7.46 us
  transfers between devices with their start and end apart: 24, of which 8 were waited for; matrix products, arithmetic and copies ran while one was open for 5% of the time, Pallas kernels for 13%

profile of v4, /device:TPU:1, one launch (start us, length us, event | category | flops | bytes accessed | tf_op | source)
XLA Modules:
  0.0 161.7 jit_solution(8877797237569136606)
XLA Ops:
  0.0 3.8 %collective-permute-start.1 = (bf16[16,4096]{1,0:T(8,128)(2,1)}, bf16[16,4096]{1,0:T(8,128)(2,1)S(1)}, u32[]{:S(2)}, u32[]{:S(2)}) collective-permute-start(bf16[16,4096]{1,0:T(8,128)(2,1)} %param.16), channel_id=1, source_target_pairs={{0,32},{16,48},{32,0},{48,16},{1,33},{17,49},{33,1},{49,17},{2,34}... | collective-permute-start | bytes 393224 | tf_op jit(solution)/shard_map/ppermute | solution.py:326
  3.8 1.6 %collective-permute-start = (bf16[16,4096]{1,0:T(8,128)(2,1)}, bf16[16,4096]{1,0:T(8,128)(2,1)S(1)}, u32[]{:S(2)}, u32[]{:S(2)}) collective-permute-start(bf16[16,4096]{1,0:T(8,128)(2,1)} %param.16), channel_id=1, source_target_pairs={{0,16},{16,32},{32,48},{48,0},{1,17},{17,33},{33,49},{49,1},{2,18}... | collective-permute-start | bytes 393224 | tf_op jit(solution)/shard_map/ppermute | solution.py:326
  5.5 1.6 %collective-permute-start.2 = (bf16[16,4096]{1,0:T(8,128)(2,1)}, bf16[16,4096]{1,0:T(8,128)(2,1)S(1)}, u32[]{:S(2)}, u32[]{:S(2)}) collective-permute-start(bf16[16,4096]{1,0:T(8,128)(2,1)} %param.16), channel_id=1, source_target_pairs={{0,48},{16,0},{32,16},{48,32},{1,49},{17,1},{33,17},{49,33},{2,50}... | collective-permute-start | bytes 393224 | tf_op jit(solution)/shard_map/ppermute | solution.py:326
  7.1 0.5 compare_convert_fusion.turned_ref
  7.6 5.0 %prep.1 = bf16[1024,1280]{1,0:T(8,128)(2,1)} custom-call(s32[2]{0:T(128)} %compare_convert_fusion.turned_ref, bf16[256,1024]{1,0:T(8,128)(2,1)} %k_ref.2, bf16[256,1024]{1,0:T(8,128)(2,1)} %v_ref.2, f32[4,256,1024]{2,1,0:T(8,128)} %bitcast.52), custom_call_target="tpu_custom_call" | custom-call | tf_op jit(solution)/shard_map/prep/pallas_call | solution.py:74
  12.6 0.9 collective-permute-done.2
  13.4 13.1 %all-to-all-start = ((bf16[64,16,1280]{2,1,0:T(8,128)(2,1)}), bf16[64,16,1280]{2,1,0:T(8,128)(2,1)}, u32[]{:S(2)}, u32[]{:S(2)}) async-start(bf16[64,16,1280]{2,1,0:T(8,128)(2,1)} %bitcast.51), calls=%async_computation | async-start | bytes 5242880 | tf_op jit(solution)/shard_map/all_to_all | solution.py:342
  26.6 0.1 pad_maximum_fusion.2
  26.7 2.4 %collective-permute-start.5 = (bf16[2,4,16,1024]{3,2,1,0:T(8,128)(2,1)S(1)}, bf16[2,4,16,1024]{3,2,1,0:T(8,128)(2,1)S(1)}, u32[]{:S(2)}, u32[]{:S(2)}) collective-permute-start(bf16[2,4,16,1024]{3,2,1,0:T(8,128)(2,1)S(1)} %pad_maximum_fusion.3), channel_id=1, source_target_pairs={{0,192},{64,0},{128,64},{192,128},{1,193},{65,1},{129,65},{193,129... | collective-permute-start | bytes 786440 | tf_op jit(solution)/shard_map/ppermute | solution.py:307
  29.2 2.5 %collective-permute-start.11 = (bf16[2,4,16,1024]{3,2,1,0:T(8,128)(2,1)S(1)}, bf16[2,4,16,1024]{3,2,1,0:T(8,128)(2,1)S(1)}, u32[]{:S(2)}, u32[]{:S(2)}) collective-permute-start(bf16[2,4,16,1024]{3,2,1,0:T(8,128)(2,1)S(1)} %pad_maximum_fusion.4), channel_id=1, source_target_pairs={{0,12},{4,0},{8,4},{12,8},{1,13},{5,1},{9,5},{13,9},{2,14},{6,2},{... | collective-permute-start | bytes 786440 | tf_op jit(solution)/shard_map/ppermute | solution.py:307
  31.7 18.4 %collective-permute-done.5 = bf16[2,4,16,1024]{3,2,1,0:T(8,128)(2,1)S(1)} collective-permute-done((bf16[2,4,16,1024]{3,2,1,0:T(8,128)(2,1)S(1)}, bf16[2,4,16,1024]{3,2,1,0:T(8,128)(2,1)S(1)}, u32[]{:S(2)}, u32[]{:S(2)}) %collective-permute-start.5) | collective-permute-done | bytes 262176 | tf_op jit(solution)/shard_map/ppermute | solution.py:307
  50.2 0.1 collective-permute-start.6
  50.3 3.7 %collective-permute-start.12 = (bf16[4,16,1024]{2,1,0:T(8,128)(2,1)S(1)}, bf16[4,16,1024]{2,1,0:T(8,128)(2,1)S(1)}, u32[]{:S(2)}, u32[]{:S(2)}) collective-permute-start(bf16[4,16,1024]{2,1,0:T(8,128)(2,1)S(1)} %get-tuple-element.63), channel_id=1, source_target_pairs={{0,12},{4,0},{8,4},{12,8},{1,13},{5,1},{9,5},{13,9},{2,14},{6,2},{... | collective-permute-start | bytes 393224 | tf_op jit(solution)/shard_map/ppermute | solution.py:311
  54.1 1.5 collective-permute-start.10
  55.6 0.1 collective-permute-start.4
  55.7 2.5 %collective-permute-done.12 = bf16[4,16,1024]{2,1,0:T(8,128)(2,1)S(1)} collective-permute-done((bf16[4,16,1024]{2,1,0:T(8,128)(2,1)S(1)}, bf16[4,16,1024]{2,1,0:T(8,128)(2,1)S(1)}, u32[]{:S(2)}, u32[]{:S(2)}) %collective-permute-start.12) | collective-permute-done | bytes 131104 | tf_op jit(solution)/shard_map/ppermute | solution.py:311
  58.2 0.1 maximum_bitcast_fusion.3
  58.2 2.3 %collective-permute-done.10 = bf16[4,16,1024]{2,1,0:T(8,128)(2,1)S(1)} collective-permute-done((bf16[4,16,1024]{2,1,0:T(8,128)(2,1)S(1)}, bf16[4,16,1024]{2,1,0:T(8,128)(2,1)S(1)}, u32[]{:S(2)}, u32[]{:S(2)}) %collective-permute-start.10) | collective-permute-done | bytes 131104 | tf_op jit(solution)/shard_map/ppermute | solution.py:311
  60.5 0.1 maximum_bitcast_fusion.2
  60.6 0.1 pad_maximum_fusion.1.own
  60.7 2.6 %collective-permute-start.14 = (bf16[2,4,4,16,1024]{4,3,2,1,0:T(8,128)(2,1)S(1)}, bf16[2,4,4,16,1024]{4,3,2,1,0:T(8,128)(2,1)}, u32[]{:S(2)}, u32[]{:S(2)}) collective-permute-start(bf16[2,4,4,16,1024]{4,3,2,1,0:T(8,128)(2,1)S(1)} %pad_maximum_fusion.1.own), channel_id=1, source_target_pairs={{0,192},{64,0},{128,64},{192,128},{1,193},{65,1},{129,65},{193,129... | collective-permute-start | bytes 3145736 | tf_op jit(solution)/shard_map/ppermute | solution.py:307
  63.3 0.1 maximum_bitcast_fusion.1
  63.3 0.1 maximum_bitcast_fusion
  63.4 0.1 pad_maximum_fusion.own
  63.5 3.2 %collective-permute-start.8 = (bf16[2,4,4,16,1024]{4,3,2,1,0:T(8,128)(2,1)S(1)}, bf16[2,4,4,16,1024]{4,3,2,1,0:T(8,128)(2,1)}, u32[]{:S(2)}, u32[]{:S(2)}) collective-permute-start(bf16[2,4,4,16,1024]{4,3,2,1,0:T(8,128)(2,1)S(1)} %pad_maximum_fusion.own), channel_id=1, source_target_pairs={{0,12},{4,0},{8,4},{12,8},{1,13},{5,1},{9,5},{13,9},{2,14},{6,2},{... | collective-permute-start | bytes 3145736 | tf_op jit(solution)/shard_map/ppermute | solution.py:307
  66.7 20.6 %all-to-all-done = bf16[64,16,1280]{2,1,0:T(8,128)(2,1)} async-done(((bf16[64,16,1280]{2,1,0:T(8,128)(2,1)}), bf16[64,16,1280]{2,1,0:T(8,128)(2,1)}, u32[]{:S(2)}, u32[]{:S(2)}) %all-to-all-start) | async-done | bytes 2621472 | tf_op jit(solution)/shard_map/all_to_all | solution.py:342
  87.3 11.3 %convolve.1 = bf16[1024,256]{1,0:T(8,128)(2,1)} custom-call(bf16[1024,1280]{1,0:T(8,128)(2,1)} %bitcast.5.r_any, bf16[2,72,128]{2,1,0:T(8,128)(2,1)} %constant.45.clone.fold_any, bf16[144,128]{1,0:T(8,128)(2,1)} %constant.46.clone.first_any, bf16[128,144]{1,0:T(8,128)(2,1)} %constant.47.clone.last_any, bf16[1536,256]{1,0:T(8,128)(2,1)} %constant.48.clone.row_any, ...), custom_call_target="tpu_custom_call" | custom-call | flops 17179869184 | bytes 4194304 | tf_op jit(solution)/shard_map/convolve/pallas_call | solution.py:206
  98.6 0.0 copy-start
  98.6 0.0 copy-start.1
  98.6 0.0 copy-start.4
  98.6 0.0 copy-start.5
  98.6 7.1 %all-to-all-start.1 = ((bf16[64,16,256]{2,1,0:T(8,128)(2,1)}), bf16[64,16,256]{2,1,0:T(8,128)(2,1)S(1)}, u32[]{:S(2)}, u32[]{:S(2)}) async-start(bf16[64,16,256]{2,1,0:T(8,128)(2,1)} %bitcast.53), calls=%async_computation.1 | async-start | bytes 1048576 | tf_op jit(solution)/shard_map/all_to_all | solution.py:342
  105.8 1.9 %slice_bitcast_fusion = bf16[4,4,16,1024]{3,2,1,0:T(8,128)(2,1)} fusion(bf16[2,4,4,16,1024]{4,3,2,1,0:T(8,128)(2,1)} %collective-permute-done.8.right), kind=kLoop, calls=%fused_computation.7 | loop fusion | bytes 1048576 | tf_op jit(solution)/shard_map/squeeze | solution.py:358
  107.7 2.2 %collective-permute-start.18 = (bf16[4,4,16,1024]{3,2,1,0:T(8,128)(2,1)}, bf16[4,4,16,1024]{3,2,1,0:T(8,128)(2,1)}, u32[]{:S(2)}, u32[]{:S(2)}) collective-permute-start(bf16[4,4,16,1024]{3,2,1,0:T(8,128)(2,1)} %slice_bitcast_fusion), channel_id=1, source_target_pairs={{0,12},{4,0},{8,4},{12,8},{1,13},{5,1},{9,5},{13,9},{2,14},{6,2},{... | collective-permute-start | bytes 1572872 | tf_op jit(solution)/shard_map/ppermute | solution.py:311
  109.9 1.9 %slice_bitcast_fusion.1 = bf16[4,4,16,1024]{3,2,1,0:T(8,128)(2,1)} fusion(bf16[2,4,4,16,1024]{4,3,2,1,0:T(8,128)(2,1)} %collective-permute-done.7.left), kind=kLoop, calls=%fused_computation.8 | loop fusion | bytes 1048576 | tf_op jit(solution)/shard_map/squeeze | solution.py:358
  111.8 2.3 %slice_bitcast_fusion.2 = (bf16[4,4,16,1024]{3,2,1,0:T(8,128)(2,1)}, bf16[4,4,16,1024]{3,2,1,0:T(8,128)(2,1)}) fusion(bf16[2,4,4,16,1024]{4,3,2,1,0:T(8,128)(2,1)} %collective-permute-done.14.right, bf16[2,4,4,16,1024]{4,3,2,1,0:T(8,128)(2,1)} %collective-permute-done.13.left), kind=kLoop, calls=%fused_computation.9 | loop fusion | bytes 2097152 | tf_op jit(solution)/shard_map/squeeze | solution.py:359
  114.1 8.8 %all-to-all-done.1 = bf16[64,16,256]{2,1,0:T(8,128)(2,1)S(1)} async-done(((bf16[64,16,256]{2,1,0:T(8,128)(2,1)}), bf16[64,16,256]{2,1,0:T(8,128)(2,1)S(1)}, u32[]{:S(2)}, u32[]{:S(2)}) %all-to-all-start.1) | async-done | bytes 524320 | tf_op jit(solution)/shard_map/all_to_all | solution.py:342
  123.0 1.0 gate.1.g0
  124.0 2.2 %collective-permute-start.16 = (bf16[1024,256]{1,0:T(8,128)(2,1)S(1)}, bf16[1024,256]{1,0:T(8,128)(2,1)S(1)}, u32[]{:S(2)}, u32[]{:S(2)}) collective-permute-start(bf16[1024,256]{1,0:T(8,128)(2,1)S(1)} %gate.1.g0), channel_id=1, source_target_pairs={{0,1},{1,0},{2,3},{3,2},{4,5},{5,4},{6,7},{7,6},{8,9},{9,8},{10,11... | collective-permute-start | bytes 1572872 | tf_op jit(solution)/shard_map/ppermute | solution.py:362
  126.2 4.3 %collective-permute-start.15 = (bf16[1024,256]{1,0:T(8,128)(2,1)S(1)}, bf16[1024,256]{1,0:T(8,128)(2,1)S(1)}, u32[]{:S(2)}, u32[]{:S(2)}) collective-permute-start(bf16[1024,256]{1,0:T(8,128)(2,1)S(1)} %gate.1.g0), channel_id=1, source_target_pairs={{0,2},{2,0},{1,3},{3,1},{4,6},{6,4},{5,7},{7,5},{8,10},{10,8},{9,1... | collective-permute-start | bytes 1572872 | tf_op jit(solution)/shard_map/ppermute | solution.py:363
  130.4 0.1 collective-permute-start.20
  130.5 2.7 %collective-permute-start.21 = (bf16[4,4,16,1024]{3,2,1,0:T(8,128)(2,1)S(1)}, bf16[4,4,16,1024]{3,2,1,0:T(8,128)(2,1)S(1)}, u32[]{:S(2)}, u32[]{:S(2)}) collective-permute-start(bf16[4,4,16,1024]{3,2,1,0:T(8,128)(2,1)S(1)} %copy-done.6), channel_id=1, source_target_pairs={{0,192},{64,0},{128,64},{192,128},{1,193},{65,1},{129,65},{193,129... | collective-permute-start | bytes 1572872 | tf_op jit(solution)/shard_map/ppermute | solution.py:311
  133.2 3.1 %near.1.near_ref = f32[1024,256]{1,0:T(8,128)S(1)} custom-call(bf16[1024,256]{1,0:T(8,128)(2,1)S(1)} %gate.1.g0, bf16[1024,256]{1,0:T(8,128)(2,1)S(1)} %collective-permute-done.16.g1, bf16[2,4,4,16,1024]{4,3,2,1,0:T(8,128)(2,1)S(1)} %copy-done.3, bf16[2,4,4,16,1024]{4,3,2,1,0:T(8,128)(2,1)} %collective-permute-done.7.left, ...), custom_call_target="tpu_custom_call" | custom-call | flops 34359738368 | bytes 6291456 | tf_op jit(solution)/shard_map/near/pallas_call | solution.py:286
  136.3 18.6 %collective-permute-done.15.g0 = bf16[1024,256]{1,0:T(8,128)(2,1)S(1)} collective-permute-done((bf16[1024,256]{1,0:T(8,128)(2,1)S(1)}, bf16[1024,256]{1,0:T(8,128)(2,1)S(1)}, u32[]{:S(2)}, u32[]{:S(2)}) %collective-permute-start.15) | collective-permute-done | bytes 524320 | tf_op jit(solution)/shard_map/ppermute | solution.py:363
  154.9 0.9 collective-permute-start.19
  155.8 0.1 pad_add_fusion.place_ref
  155.9 1.5 collective-permute-done.19.g1
  157.4 4.4 %far.1 = bf16[256,1024]{1,0:T(8,128)(2,1)} custom-call(s32[3]{0:T(128)S(1)} %pad_add_fusion.place_ref, bf16[1024,256]{1,0:T(8,128)(2,1)S(1)} %collective-permute-done.15.g0, bf16[1024,256]{1,0:T(8,128)(2,1)S(1)} %collective-permute-done.19.g1, bf16[2,4,4,16,1024]{4,3,2,1,0:T(8,128)(2,1)S(1)} %pad_maximum_fusion.1.own, ...), custom_call_target="tpu_custom_call" | custom-call | flops 34359738368 | bytes 6291456 | tf_op jit(solution)/shard_map/far/pallas_call | solution.py:286
  (42 shorter events, 0.3 us)
Async XLA Ops:
  0.0 12.6 %collective-permute-start.1 = (bf16[16,4096]{1,0:T(8,128)(2,1)}, bf16[16,4096]{1,0:T(8,128)(2,1)S(1)}, u32[]{:S(2)}, u32[]{:S(2)}) collective-permute-start(bf16[16,4096]{1,0:T(8,128)(2,1)} %param.16), channel_id=1, source_target_pairs={{0,32},{16,48},{32,0},{48,16},{1,33},{17,49},{33,1},{49,17},{2,34}... | collective-permute-start | bytes 393224 | tf_op jit(solution)/shard_map/ppermute | solution.py:326
  3.8 8.8 %collective-permute-start = (bf16[16,4096]{1,0:T(8,128)(2,1)}, bf16[16,4096]{1,0:T(8,128)(2,1)S(1)}, u32[]{:S(2)}, u32[]{:S(2)}) collective-permute-start(bf16[16,4096]{1,0:T(8,128)(2,1)} %param.16), channel_id=1, source_target_pairs={{0,16},{16,32},{32,48},{48,0},{1,17},{17,33},{33,49},{49,1},{2,18}... | collective-permute-start | bytes 393224 | tf_op jit(solution)/shard_map/ppermute | solution.py:326
  5.5 8.0 %collective-permute-start.2 = (bf16[16,4096]{1,0:T(8,128)(2,1)}, bf16[16,4096]{1,0:T(8,128)(2,1)S(1)}, u32[]{:S(2)}, u32[]{:S(2)}) collective-permute-start(bf16[16,4096]{1,0:T(8,128)(2,1)} %param.16), channel_id=1, source_target_pairs={{0,48},{16,0},{32,16},{48,32},{1,49},{17,1},{33,17},{49,33},{2,50}... | collective-permute-start | bytes 393224 | tf_op jit(solution)/shard_map/ppermute | solution.py:326
  13.4 13.1 %copy-start.8 = (bf16[16,4096]{1,0:T(8,128)(2,1)S(1)}, bf16[16,4096]{1,0:T(8,128)(2,1)}, u32[]{:S(2)}) copy-start(bf16[16,4096]{1,0:T(8,128)(2,1)} %param.16) | copy-start | bytes 393220
  13.4 73.8 %all-to-all-start = ((bf16[64,16,1280]{2,1,0:T(8,128)(2,1)}), bf16[64,16,1280]{2,1,0:T(8,128)(2,1)}, u32[]{:S(2)}, u32[]{:S(2)}) async-start(bf16[64,16,1280]{2,1,0:T(8,128)(2,1)} %bitcast.51), calls=%async_computation | async-start | bytes 5242880 | tf_op jit(solution)/shard_map/all_to_all | solution.py:342
  26.7 23.4 %collective-permute-start.5 = (bf16[2,4,16,1024]{3,2,1,0:T(8,128)(2,1)S(1)}, bf16[2,4,16,1024]{3,2,1,0:T(8,128)(2,1)S(1)}, u32[]{:S(2)}, u32[]{:S(2)}) collective-permute-start(bf16[2,4,16,1024]{3,2,1,0:T(8,128)(2,1)S(1)} %pad_maximum_fusion.3), channel_id=1, source_target_pairs={{0,192},{64,0},{128,64},{192,128},{1,193},{65,1},{129,65},{193,129... | collective-permute-start | bytes 786440 | tf_op jit(solution)/shard_map/ppermute | solution.py:307
  29.2 21.1 %collective-permute-start.11 = (bf16[2,4,16,1024]{3,2,1,0:T(8,128)(2,1)S(1)}, bf16[2,4,16,1024]{3,2,1,0:T(8,128)(2,1)S(1)}, u32[]{:S(2)}, u32[]{:S(2)}) collective-permute-start(bf16[2,4,16,1024]{3,2,1,0:T(8,128)(2,1)S(1)} %pad_maximum_fusion.4), channel_id=1, source_target_pairs={{0,12},{4,0},{8,4},{12,8},{1,13},{5,1},{9,5},{13,9},{2,14},{6,2},{... | collective-permute-start | bytes 786440 | tf_op jit(solution)/shard_map/ppermute | solution.py:307
  31.7 23.8 %collective-permute-start.3 = (bf16[2,4,16,1024]{3,2,1,0:T(8,128)(2,1)S(1)}, bf16[2,4,16,1024]{3,2,1,0:T(8,128)(2,1)S(1)}, u32[]{:S(2)}, u32[]{:S(2)}) collective-permute-start(bf16[2,4,16,1024]{3,2,1,0:T(8,128)(2,1)S(1)} %pad_maximum_fusion.3), channel_id=1, source_target_pairs={{0,64},{64,128},{128,192},{192,0},{1,65},{65,129},{129,193},{193,1... | collective-permute-start | bytes 786440 | tf_op jit(solution)/shard_map/ppermute | solution.py:307
  31.7 22.3 %collective-permute-start.9 = (bf16[2,4,16,1024]{3,2,1,0:T(8,128)(2,1)S(1)}, bf16[2,4,16,1024]{3,2,1,0:T(8,128)(2,1)S(1)}, u32[]{:S(2)}, u32[]{:S(2)}) collective-permute-start(bf16[2,4,16,1024]{3,2,1,0:T(8,128)(2,1)S(1)} %pad_maximum_fusion.4), channel_id=1, source_target_pairs={{0,4},{4,8},{8,12},{12,0},{1,5},{5,9},{9,13},{13,1},{2,6},{6,10},{... | collective-permute-start | bytes 786440 | tf_op jit(solution)/shard_map/ppermute | solution.py:307
  50.2 13.1 %collective-permute-start.6 = (bf16[4,16,1024]{2,1,0:T(8,128)(2,1)S(1)}, bf16[4,16,1024]{2,1,0:T(8,128)(2,1)S(1)}, u32[]{:S(2)}, u32[]{:S(2)}) collective-permute-start(bf16[4,16,1024]{2,1,0:T(8,128)(2,1)S(1)} %get-tuple-element.69), channel_id=1, source_target_pairs={{0,192},{64,0},{128,64},{192,128},{1,193},{65,1},{129,65},{193,129... | collective-permute-start | bytes 393224 | tf_op jit(solution)/shard_map/ppermute | solution.py:311
  50.3 7.8 %collective-permute-start.12 = (bf16[4,16,1024]{2,1,0:T(8,128)(2,1)S(1)}, bf16[4,16,1024]{2,1,0:T(8,128)(2,1)S(1)}, u32[]{:S(2)}, u32[]{:S(2)}) collective-permute-start(bf16[4,16,1024]{2,1,0:T(8,128)(2,1)S(1)} %get-tuple-element.63), channel_id=1, source_target_pairs={{0,12},{4,0},{8,4},{12,8},{1,13},{5,1},{9,5},{13,9},{2,14},{6,2},{... | collective-permute-start | bytes 393224 | tf_op jit(solution)/shard_map/ppermute | solution.py:311
  54.1 6.4 %collective-permute-start.10 = (bf16[4,16,1024]{2,1,0:T(8,128)(2,1)S(1)}, bf16[4,16,1024]{2,1,0:T(8,128)(2,1)S(1)}, u32[]{:S(2)}, u32[]{:S(2)}) collective-permute-start(bf16[4,16,1024]{2,1,0:T(8,128)(2,1)S(1)} %get-tuple-element.60), channel_id=1, source_target_pairs={{0,4},{4,8},{8,12},{12,0},{1,5},{5,9},{9,13},{13,1},{2,6},{6,10},{... | collective-permute-start | bytes 393224 | tf_op jit(solution)/shard_map/ppermute | solution.py:311
  55.6 7.7 %collective-permute-start.4 = (bf16[4,16,1024]{2,1,0:T(8,128)(2,1)S(1)}, bf16[4,16,1024]{2,1,0:T(8,128)(2,1)S(1)}, u32[]{:S(2)}, u32[]{:S(2)}) collective-permute-start(bf16[4,16,1024]{2,1,0:T(8,128)(2,1)S(1)} %get-tuple-element.66), channel_id=1, source_target_pairs={{0,64},{64,128},{128,192},{192,0},{1,65},{65,129},{129,193},{193,1... | collective-permute-start | bytes 393224 | tf_op jit(solution)/shard_map/ppermute | solution.py:311
  60.7 37.9 %collective-permute-start.14 = (bf16[2,4,4,16,1024]{4,3,2,1,0:T(8,128)(2,1)S(1)}, bf16[2,4,4,16,1024]{4,3,2,1,0:T(8,128)(2,1)}, u32[]{:S(2)}, u32[]{:S(2)}) collective-permute-start(bf16[2,4,4,16,1024]{4,3,2,1,0:T(8,128)(2,1)S(1)} %pad_maximum_fusion.1.own), channel_id=1, source_target_pairs={{0,192},{64,0},{128,64},{192,128},{1,193},{65,1},{129,65},{193,129... | collective-permute-start | bytes 3145736 | tf_op jit(solution)/shard_map/ppermute | solution.py:307
  63.3 35.3 %collective-permute-start.13 = (bf16[2,4,4,16,1024]{4,3,2,1,0:T(8,128)(2,1)S(1)}, bf16[2,4,4,16,1024]{4,3,2,1,0:T(8,128)(2,1)}, u32[]{:S(2)}, u32[]{:S(2)}) collective-permute-start(bf16[2,4,4,16,1024]{4,3,2,1,0:T(8,128)(2,1)S(1)} %pad_maximum_fusion.1.own), channel_id=1, source_target_pairs={{0,64},{64,128},{128,192},{192,0},{1,65},{65,129},{129,193},{193,1... | collective-permute-start | bytes 3145736 | tf_op jit(solution)/shard_map/ppermute | solution.py:307
  63.5 35.0 %copy-start.2 = (bf16[2,4,4,16,1024]{4,3,2,1,0:T(8,128)(2,1)}, bf16[2,4,4,16,1024]{4,3,2,1,0:T(8,128)(2,1)S(1)}, u32[]{:S(2)}) copy-start(bf16[2,4,4,16,1024]{4,3,2,1,0:T(8,128)(2,1)S(1)} %pad_maximum_fusion.own) | copy-start | bytes 3145732
  63.5 35.0 %collective-permute-start.8 = (bf16[2,4,4,16,1024]{4,3,2,1,0:T(8,128)(2,1)S(1)}, bf16[2,4,4,16,1024]{4,3,2,1,0:T(8,128)(2,1)}, u32[]{:S(2)}, u32[]{:S(2)}) collective-permute-start(bf16[2,4,4,16,1024]{4,3,2,1,0:T(8,128)(2,1)S(1)} %pad_maximum_fusion.own), channel_id=1, source_target_pairs={{0,12},{4,0},{8,4},{12,8},{1,13},{5,1},{9,5},{13,9},{2,14},{6,2},{... | collective-permute-start | bytes 3145736 | tf_op jit(solution)/shard_map/ppermute | solution.py:307
  66.7 31.9 %collective-permute-start.7 = (bf16[2,4,4,16,1024]{4,3,2,1,0:T(8,128)(2,1)S(1)}, bf16[2,4,4,16,1024]{4,3,2,1,0:T(8,128)(2,1)}, u32[]{:S(2)}, u32[]{:S(2)}) collective-permute-start(bf16[2,4,4,16,1024]{4,3,2,1,0:T(8,128)(2,1)S(1)} %pad_maximum_fusion.own), channel_id=1, source_target_pairs={{0,4},{4,8},{8,12},{12,0},{1,5},{5,9},{9,13},{13,1},{2,6},{6,10},{... | collective-permute-start | bytes 3145736 | tf_op jit(solution)/shard_map/ppermute | solution.py:307
  98.6 24.3 %copy-start = (bf16[256,1024]{1,0:T(8,128)(2,1)S(1)}, bf16[256,1024]{1,0:T(8,128)(2,1)}, u32[]{:S(2)}) copy-start(bf16[256,1024]{1,0:T(8,128)(2,1)} %k_ref.2) | copy-start | bytes 1572868
  98.6 24.3 %copy-start.1 = (bf16[256,1024]{1,0:T(8,128)(2,1)S(1)}, bf16[256,1024]{1,0:T(8,128)(2,1)}, u32[]{:S(2)}) copy-start(bf16[256,1024]{1,0:T(8,128)(2,1)} %v_ref.2) | copy-start | bytes 1572868
  98.6 24.3 %copy-start.4 = (bf16[256,1024]{1,0:T(8,128)(2,1)S(1)}, bf16[256,1024]{1,0:T(8,128)(2,1)}, u32[]{:S(2)}) copy-start(bf16[256,1024]{1,0:T(8,128)(2,1)} %q_ref) | copy-start | bytes 1572868
  98.6 24.3 %copy-start.5 = (f32[1024]{0:T(1024)S(1)}, f32[1024]{0:T(1024)}, u32[]{:S(2)}) copy-start(f32[1024]{0:T(1024)} %param.15) | copy-start | bytes 12292
  98.6 24.3 %all-to-all-start.1 = ((bf16[64,16,256]{2,1,0:T(8,128)(2,1)}), bf16[64,16,256]{2,1,0:T(8,128)(2,1)S(1)}, u32[]{:S(2)}, u32[]{:S(2)}) async-start(bf16[64,16,256]{2,1,0:T(8,128)(2,1)} %bitcast.53), calls=%async_computation.1 | async-start | bytes 1048576 | tf_op jit(solution)/shard_map/all_to_all | solution.py:342
  107.7 22.8 %collective-permute-start.18 = (bf16[4,4,16,1024]{3,2,1,0:T(8,128)(2,1)}, bf16[4,4,16,1024]{3,2,1,0:T(8,128)(2,1)}, u32[]{:S(2)}, u32[]{:S(2)}) collective-permute-start(bf16[4,4,16,1024]{3,2,1,0:T(8,128)(2,1)} %slice_bitcast_fusion), channel_id=1, source_target_pairs={{0,12},{4,0},{8,4},{12,8},{1,13},{5,1},{9,5},{13,9},{2,14},{6,2},{... | collective-permute-start | bytes 1572872 | tf_op jit(solution)/shard_map/ppermute | solution.py:311
  111.8 18.6 %collective-permute-start.17 = (bf16[4,4,16,1024]{3,2,1,0:T(8,128)(2,1)}, bf16[4,4,16,1024]{3,2,1,0:T(8,128)(2,1)}, u32[]{:S(2)}, u32[]{:S(2)}) collective-permute-start(bf16[4,4,16,1024]{3,2,1,0:T(8,128)(2,1)} %slice_bitcast_fusion.1), channel_id=1, source_target_pairs={{0,4},{4,8},{8,12},{12,0},{1,5},{5,9},{9,13},{13,1},{2,6},{6,10},{... | collective-permute-start | bytes 1572872 | tf_op jit(solution)/shard_map/ppermute | solution.py:311
  122.9 7.5 %copy-start.7 = (bf16[4,4,16,1024]{3,2,1,0:T(8,128)(2,1)S(1)}, bf16[4,4,16,1024]{3,2,1,0:T(8,128)(2,1)}, u32[]{:S(2)}) copy-start(bf16[4,4,16,1024]{3,2,1,0:T(8,128)(2,1)} %get-tuple-element.52) | copy-start | bytes 1572868
  122.9 7.6 %copy-start.6 = (bf16[4,4,16,1024]{3,2,1,0:T(8,128)(2,1)S(1)}, bf16[4,4,16,1024]{3,2,1,0:T(8,128)(2,1)}, u32[]{:S(2)}) copy-start(bf16[4,4,16,1024]{3,2,1,0:T(8,128)(2,1)} %get-tuple-element.53) | copy-start | bytes 1572868
  122.9 10.3 %copy-start.3 = (bf16[2,4,4,16,1024]{4,3,2,1,0:T(8,128)(2,1)S(1)}, bf16[2,4,4,16,1024]{4,3,2,1,0:T(8,128)(2,1)}, u32[]{:S(2)}) copy-start(bf16[2,4,4,16,1024]{4,3,2,1,0:T(8,128)(2,1)} %copy-done.2) | copy-start | bytes 3145732
  124.0 6.5 %collective-permute-start.16 = (bf16[1024,256]{1,0:T(8,128)(2,1)S(1)}, bf16[1024,256]{1,0:T(8,128)(2,1)S(1)}, u32[]{:S(2)}, u32[]{:S(2)}) collective-permute-start(bf16[1024,256]{1,0:T(8,128)(2,1)S(1)} %gate.1.g0), channel_id=1, source_target_pairs={{0,1},{1,0},{2,3},{3,2},{4,5},{5,4},{6,7},{7,6},{8,9},{9,8},{10,11... | collective-permute-start | bytes 1572872 | tf_op jit(solution)/shard_map/ppermute | solution.py:362
  126.2 28.7 %collective-permute-start.15 = (bf16[1024,256]{1,0:T(8,128)(2,1)S(1)}, bf16[1024,256]{1,0:T(8,128)(2,1)S(1)}, u32[]{:S(2)}, u32[]{:S(2)}) collective-permute-start(bf16[1024,256]{1,0:T(8,128)(2,1)S(1)} %gate.1.g0), channel_id=1, source_target_pairs={{0,2},{2,0},{1,3},{3,1},{4,6},{6,4},{5,7},{7,5},{8,10},{10,8},{9,1... | collective-permute-start | bytes 1572872 | tf_op jit(solution)/shard_map/ppermute | solution.py:363
  130.4 25.5 %collective-permute-start.20 = (bf16[4,4,16,1024]{3,2,1,0:T(8,128)(2,1)S(1)}, bf16[4,4,16,1024]{3,2,1,0:T(8,128)(2,1)S(1)}, u32[]{:S(2)}, u32[]{:S(2)}) collective-permute-start(bf16[4,4,16,1024]{3,2,1,0:T(8,128)(2,1)S(1)} %copy-done.7), channel_id=1, source_target_pairs={{0,64},{64,128},{128,192},{192,0},{1,65},{65,129},{129,193},{193,1... | collective-permute-start | bytes 1572872 | tf_op jit(solution)/shard_map/ppermute | solution.py:311
  130.5 25.4 %collective-permute-start.21 = (bf16[4,4,16,1024]{3,2,1,0:T(8,128)(2,1)S(1)}, bf16[4,4,16,1024]{3,2,1,0:T(8,128)(2,1)S(1)}, u32[]{:S(2)}, u32[]{:S(2)}) collective-permute-start(bf16[4,4,16,1024]{3,2,1,0:T(8,128)(2,1)S(1)} %copy-done.6), channel_id=1, source_target_pairs={{0,192},{64,0},{128,64},{192,128},{1,193},{65,1},{129,65},{193,129... | collective-permute-start | bytes 1572872 | tf_op jit(solution)/shard_map/ppermute | solution.py:311
  154.9 2.5 %collective-permute-start.19 = (bf16[1024,256]{1,0:T(8,128)(2,1)S(1)}, bf16[1024,256]{1,0:T(8,128)(2,1)S(1)}, u32[]{:S(2)}, u32[]{:S(2)}) collective-permute-start(bf16[1024,256]{1,0:T(8,128)(2,1)S(1)} %collective-permute-done.15.g0), channel_id=1, source_target_pairs={{0,1},{1,0},{2,3},{3,2},{4,5},{5,4},{6,7},{7,6},{8,9},{9,8},{10,11... | collective-permute-start | bytes 1572872 | tf_op jit(solution)/shard_map/ppermute | solution.py:369

commit v5 on v4

--- a/solution.py
+++ b/solution.py
@@ -17,7 +17,7 @@
 BIG = 56 << 20
 SMALL = 16 << 20
 KEPT = 72
-GATE = 256
+GATE = 512
 
 
 def split(table):

time: 162 us -> 162 us (level)
  transfers between devices with their start and end apart: 24 -> 24, of which waited for: 8 -> 8; matrix products, arithmetic and copies ran while one was open for 5% -> 5% of each run, Pallas kernels for 13% -> 12%
where the time goes in v5:
time: 162 us; the launch traced here: 161 us
  waiting for transfers between devices  73.6 us (45%)
  starting transfers between devices  55.7 us (34%)
  Pallas kernels  24.4 us (15%)
  local copies, waits for them, and re-layouts  6.28 us (4%)
    all_to_all x2, waiting for transfers between devices, exchange(): got = lax.all_to_all(send, SEQ, split_axis=0, concat_axis=0, tiled=True)  29.4 us
    all_to_all x2, starting transfers between devices, exchange(): got = lax.all_to_all(send, SEQ, split_axis=0, concat_axis=0, tiled=True)  20.2 us
    ppermute x1, waiting for transfers between devices, local(): over_h = lax.ppermute(gated, 'h', swap)  18.6 us
    ppermute x4, waiting for transfers between devices, beside(): lax.ppermute(piece, *ring(axis, -1))  18.5 us
    pallas_call x1, Pallas kernels, convolve(): pl.pallas_call(convolve_kernel, grid=(1,), in_specs=[ANY] * (1 + len(cons...  11.3 us
    ppermute x4, starting transfers between devices, beside(): lax.ppermute(piece, *ring(axis, -1))  10.7 us
    ppermute x4, starting transfers between devices, opposite(): lax.ppermute(right, *ring(axis, -1))  8.68 us
    pallas_call x2, Pallas kernels, project(): pl.pallas_call(near_kernel if near is None else far_kernel, grid_spec=plt...  7.46 us
  transfers between devices with their start and end apart: 24, of which 8 were waited for; matrix products, arithmetic and copies ran while one was open for 5% of the time, Pallas kernels for 12%

profile of v5, /device:TPU:1, one launch (start us, length us, event | category | flops | bytes accessed | tf_op | source)
XLA Modules:
  0.0 161.5 jit_solution(8275888358902848800)
XLA Ops:
  0.0 3.8 %collective-permute-start.1 = (bf16[16,4096]{1,0:T(8,128)(2,1)}, bf16[16,4096]{1,0:T(8,128)(2,1)S(1)}, u32[]{:S(2)}, u32[]{:S(2)}) collective-permute-start(bf16[16,4096]{1,0:T(8,128)(2,1)} %param.16), channel_id=1, source_target_pairs={{0,32},{16,48},{32,0},{48,16},{1,33},{17,49},{33,1},{49,17},{2,34}... | collective-permute-start | bytes 393224 | tf_op jit(solution)/shard_map/ppermute | solution.py:326
  3.8 1.6 %collective-permute-start = (bf16[16,4096]{1,0:T(8,128)(2,1)}, bf16[16,4096]{1,0:T(8,128)(2,1)S(1)}, u32[]{:S(2)}, u32[]{:S(2)}) collective-permute-start(bf16[16,4096]{1,0:T(8,128)(2,1)} %param.16), channel_id=1, source_target_pairs={{0,16},{16,32},{32,48},{48,0},{1,17},{17,33},{33,49},{49,1},{2,18}... | collective-permute-start | bytes 393224 | tf_op jit(solution)/shard_map/ppermute | solution.py:326
  5.5 1.6 %collective-permute-start.2 = (bf16[16,4096]{1,0:T(8,128)(2,1)}, bf16[16,4096]{1,0:T(8,128)(2,1)S(1)}, u32[]{:S(2)}, u32[]{:S(2)}) collective-permute-start(bf16[16,4096]{1,0:T(8,128)(2,1)} %param.16), channel_id=1, source_target_pairs={{0,48},{16,0},{32,16},{48,32},{1,49},{17,1},{33,17},{49,33},{2,50}... | collective-permute-start | bytes 393224 | tf_op jit(solution)/shard_map/ppermute | solution.py:326
  7.1 0.5 compare_convert_fusion.turned_ref
  7.6 5.0 %prep.1 = bf16[1024,1280]{1,0:T(8,128)(2,1)} custom-call(s32[2]{0:T(128)} %compare_convert_fusion.turned_ref, bf16[256,1024]{1,0:T(8,128)(2,1)} %k_ref.2, bf16[256,1024]{1,0:T(8,128)(2,1)} %v_ref.2, f32[4,256,1024]{2,1,0:T(8,128)} %bitcast.52), custom_call_target="tpu_custom_call" | custom-call | tf_op jit(solution)/shard_map/prep/pallas_call | solution.py:74
  12.6 0.9 collective-permute-done.2
  13.4 13.1 %all-to-all-start = ((bf16[64,16,1280]{2,1,0:T(8,128)(2,1)}), bf16[64,16,1280]{2,1,0:T(8,128)(2,1)}, u32[]{:S(2)}, u32[]{:S(2)}) async-start(bf16[64,16,1280]{2,1,0:T(8,128)(2,1)} %bitcast.51), calls=%async_computation | async-start | bytes 5242880 | tf_op jit(solution)/shard_map/all_to_all | solution.py:342
  26.6 0.1 pad_maximum_fusion.2
  26.7 2.4 %collective-permute-start.5 = (bf16[2,4,16,1024]{3,2,1,0:T(8,128)(2,1)S(1)}, bf16[2,4,16,1024]{3,2,1,0:T(8,128)(2,1)S(1)}, u32[]{:S(2)}, u32[]{:S(2)}) collective-permute-start(bf16[2,4,16,1024]{3,2,1,0:T(8,128)(2,1)S(1)} %pad_maximum_fusion.3), channel_id=1, source_target_pairs={{0,192},{64,0},{128,64},{192,128},{1,193},{65,1},{129,65},{193,129... | collective-permute-start | bytes 786440 | tf_op jit(solution)/shard_map/ppermute | solution.py:307
  29.2 2.5 %collective-permute-start.11 = (bf16[2,4,16,1024]{3,2,1,0:T(8,128)(2,1)S(1)}, bf16[2,4,16,1024]{3,2,1,0:T(8,128)(2,1)S(1)}, u32[]{:S(2)}, u32[]{:S(2)}) collective-permute-start(bf16[2,4,16,1024]{3,2,1,0:T(8,128)(2,1)S(1)} %pad_maximum_fusion.4), channel_id=1, source_target_pairs={{0,12},{4,0},{8,4},{12,8},{1,13},{5,1},{9,5},{13,9},{2,14},{6,2},{... | collective-permute-start | bytes 786440 | tf_op jit(solution)/shard_map/ppermute | solution.py:307
  31.7 18.4 %collective-permute-done.5 = bf16[2,4,16,1024]{3,2,1,0:T(8,128)(2,1)S(1)} collective-permute-done((bf16[2,4,16,1024]{3,2,1,0:T(8,128)(2,1)S(1)}, bf16[2,4,16,1024]{3,2,1,0:T(8,128)(2,1)S(1)}, u32[]{:S(2)}, u32[]{:S(2)}) %collective-permute-start.5) | collective-permute-done | bytes 262176 | tf_op jit(solution)/shard_map/ppermute | solution.py:307
  50.2 0.1 collective-permute-start.6
  50.3 3.7 %collective-permute-start.12 = (bf16[4,16,1024]{2,1,0:T(8,128)(2,1)S(1)}, bf16[4,16,1024]{2,1,0:T(8,128)(2,1)S(1)}, u32[]{:S(2)}, u32[]{:S(2)}) collective-permute-start(bf16[4,16,1024]{2,1,0:T(8,128)(2,1)S(1)} %get-tuple-element.63), channel_id=1, source_target_pairs={{0,12},{4,0},{8,4},{12,8},{1,13},{5,1},{9,5},{13,9},{2,14},{6,2},{... | collective-permute-start | bytes 393224 | tf_op jit(solution)/shard_map/ppermute | solution.py:311
  54.1 1.5 collective-permute-start.10
  55.6 0.1 collective-permute-start.4
  55.7 2.5 %collective-permute-done.12 = bf16[4,16,1024]{2,1,0:T(8,128)(2,1)S(1)} collective-permute-done((bf16[4,16,1024]{2,1,0:T(8,128)(2,1)S(1)}, bf16[4,16,1024]{2,1,0:T(8,128)(2,1)S(1)}, u32[]{:S(2)}, u32[]{:S(2)}) %collective-permute-start.12) | collective-permute-done | bytes 131104 | tf_op jit(solution)/shard_map/ppermute | solution.py:311
  58.2 0.1 maximum_bitcast_fusion.3
  58.2 2.3 %collective-permute-done.10 = bf16[4,16,1024]{2,1,0:T(8,128)(2,1)S(1)} collective-permute-done((bf16[4,16,1024]{2,1,0:T(8,128)(2,1)S(1)}, bf16[4,16,1024]{2,1,0:T(8,128)(2,1)S(1)}, u32[]{:S(2)}, u32[]{:S(2)}) %collective-permute-start.10) | collective-permute-done | bytes 131104 | tf_op jit(solution)/shard_map/ppermute | solution.py:311
  60.5 0.1 maximum_bitcast_fusion.2
  60.6 0.1 pad_maximum_fusion.1.own
  60.7 2.6 %collective-permute-start.14 = (bf16[2,4,4,16,1024]{4,3,2,1,0:T(8,128)(2,1)S(1)}, bf16[2,4,4,16,1024]{4,3,2,1,0:T(8,128)(2,1)}, u32[]{:S(2)}, u32[]{:S(2)}) collective-permute-start(bf16[2,4,4,16,1024]{4,3,2,1,0:T(8,128)(2,1)S(1)} %pad_maximum_fusion.1.own), channel_id=1, source_target_pairs={{0,192},{64,0},{128,64},{192,128},{1,193},{65,1},{129,65},{193,129... | collective-permute-start | bytes 3145736 | tf_op jit(solution)/shard_map/ppermute | solution.py:307
  63.3 0.1 maximum_bitcast_fusion.1
  63.3 0.1 maximum_bitcast_fusion
  63.4 0.1 pad_maximum_fusion.own
  63.5 3.2 %collective-permute-start.8 = (bf16[2,4,4,16,1024]{4,3,2,1,0:T(8,128)(2,1)S(1)}, bf16[2,4,4,16,1024]{4,3,2,1,0:T(8,128)(2,1)}, u32[]{:S(2)}, u32[]{:S(2)}) collective-permute-start(bf16[2,4,4,16,1024]{4,3,2,1,0:T(8,128)(2,1)S(1)} %pad_maximum_fusion.own), channel_id=1, source_target_pairs={{0,12},{4,0},{8,4},{12,8},{1,13},{5,1},{9,5},{13,9},{2,14},{6,2},{... | collective-permute-start | bytes 3145736 | tf_op jit(solution)/shard_map/ppermute | solution.py:307
  66.7 20.6 %all-to-all-done = bf16[64,16,1280]{2,1,0:T(8,128)(2,1)} async-done(((bf16[64,16,1280]{2,1,0:T(8,128)(2,1)}), bf16[64,16,1280]{2,1,0:T(8,128)(2,1)}, u32[]{:S(2)}, u32[]{:S(2)}) %all-to-all-start) | async-done | bytes 2621472 | tf_op jit(solution)/shard_map/all_to_all | solution.py:342
  87.3 11.3 %convolve.1 = bf16[1024,256]{1,0:T(8,128)(2,1)} custom-call(bf16[1024,1280]{1,0:T(8,128)(2,1)} %bitcast.5.r_any, bf16[2,72,128]{2,1,0:T(8,128)(2,1)} %constant.45.clone.fold_any, bf16[144,128]{1,0:T(8,128)(2,1)} %constant.46.clone.first_any, bf16[128,144]{1,0:T(8,128)(2,1)} %constant.47.clone.last_any, bf16[1536,256]{1,0:T(8,128)(2,1)} %constant.48.clone.row_any, ...), custom_call_target="tpu_custom_call" | custom-call | flops 17179869184 | bytes 4194304 | tf_op jit(solution)/shard_map/convolve/pallas_call | solution.py:206
  98.6 0.0 copy-start
  98.6 0.0 copy-start.1
  98.6 0.0 copy-start.4
  98.6 0.0 copy-start.5
  98.6 7.1 %all-to-all-start.1 = ((bf16[64,16,256]{2,1,0:T(8,128)(2,1)}), bf16[64,16,256]{2,1,0:T(8,128)(2,1)S(1)}, u32[]{:S(2)}, u32[]{:S(2)}) async-start(bf16[64,16,256]{2,1,0:T(8,128)(2,1)} %bitcast.53), calls=%async_computation.1 | async-start | bytes 1048576 | tf_op jit(solution)/shard_map/all_to_all | solution.py:342
  105.8 1.9 %slice_bitcast_fusion = bf16[4,4,16,1024]{3,2,1,0:T(8,128)(2,1)} fusion(bf16[2,4,4,16,1024]{4,3,2,1,0:T(8,128)(2,1)} %collective-permute-done.8.right), kind=kLoop, calls=%fused_computation.7 | loop fusion | bytes 1048576 | tf_op jit(solution)/shard_map/squeeze | solution.py:358
  107.7 2.2 %collective-permute-start.18 = (bf16[4,4,16,1024]{3,2,1,0:T(8,128)(2,1)}, bf16[4,4,16,1024]{3,2,1,0:T(8,128)(2,1)}, u32[]{:S(2)}, u32[]{:S(2)}) collective-permute-start(bf16[4,4,16,1024]{3,2,1,0:T(8,128)(2,1)} %slice_bitcast_fusion), channel_id=1, source_target_pairs={{0,12},{4,0},{8,4},{12,8},{1,13},{5,1},{9,5},{13,9},{2,14},{6,2},{... | collective-permute-start | bytes 1572872 | tf_op jit(solution)/shard_map/ppermute | solution.py:311
  109.9 1.9 %slice_bitcast_fusion.1 = bf16[4,4,16,1024]{3,2,1,0:T(8,128)(2,1)} fusion(bf16[2,4,4,16,1024]{4,3,2,1,0:T(8,128)(2,1)} %collective-permute-done.7.left), kind=kLoop, calls=%fused_computation.8 | loop fusion | bytes 1048576 | tf_op jit(solution)/shard_map/squeeze | solution.py:358
  111.8 2.3 %slice_bitcast_fusion.2 = (bf16[4,4,16,1024]{3,2,1,0:T(8,128)(2,1)}, bf16[4,4,16,1024]{3,2,1,0:T(8,128)(2,1)}) fusion(bf16[2,4,4,16,1024]{4,3,2,1,0:T(8,128)(2,1)} %collective-permute-done.14.right, bf16[2,4,4,16,1024]{4,3,2,1,0:T(8,128)(2,1)} %collective-permute-done.13.left), kind=kLoop, calls=%fused_computation.9 | loop fusion | bytes 2097152 | tf_op jit(solution)/shard_map/squeeze | solution.py:359
  114.1 8.8 %all-to-all-done.1 = bf16[64,16,256]{2,1,0:T(8,128)(2,1)S(1)} async-done(((bf16[64,16,256]{2,1,0:T(8,128)(2,1)}), bf16[64,16,256]{2,1,0:T(8,128)(2,1)S(1)}, u32[]{:S(2)}, u32[]{:S(2)}) %all-to-all-start.1) | async-done | bytes 524320 | tf_op jit(solution)/shard_map/all_to_all | solution.py:342
  123.0 0.7 gate.1.g0
  123.7 2.2 %collective-permute-start.16 = (bf16[1024,256]{1,0:T(8,128)(2,1)S(1)}, bf16[1024,256]{1,0:T(8,128)(2,1)S(1)}, u32[]{:S(2)}, u32[]{:S(2)}) collective-permute-start(bf16[1024,256]{1,0:T(8,128)(2,1)S(1)} %gate.1.g0), channel_id=1, source_target_pairs={{0,1},{1,0},{2,3},{3,2},{4,5},{5,4},{6,7},{7,6},{8,9},{9,8},{10,11... | collective-permute-start | bytes 1572872 | tf_op jit(solution)/shard_map/ppermute | solution.py:362
  125.9 4.3 %collective-permute-start.15 = (bf16[1024,256]{1,0:T(8,128)(2,1)S(1)}, bf16[1024,256]{1,0:T(8,128)(2,1)S(1)}, u32[]{:S(2)}, u32[]{:S(2)}) collective-permute-start(bf16[1024,256]{1,0:T(8,128)(2,1)S(1)} %gate.1.g0), channel_id=1, source_target_pairs={{0,2},{2,0},{1,3},{3,1},{4,6},{6,4},{5,7},{7,5},{8,10},{10,8},{9,1... | collective-permute-start | bytes 1572872 | tf_op jit(solution)/shard_map/ppermute | solution.py:363
  130.2 0.1 collective-permute-start.20
  130.3 2.7 %collective-permute-start.21 = (bf16[4,4,16,1024]{3,2,1,0:T(8,128)(2,1)S(1)}, bf16[4,4,16,1024]{3,2,1,0:T(8,128)(2,1)S(1)}, u32[]{:S(2)}, u32[]{:S(2)}) collective-permute-start(bf16[4,4,16,1024]{3,2,1,0:T(8,128)(2,1)S(1)} %copy-done.6), channel_id=1, source_target_pairs={{0,192},{64,0},{128,64},{192,128},{1,193},{65,1},{129,65},{193,129... | collective-permute-start | bytes 1572872 | tf_op jit(solution)/shard_map/ppermute | solution.py:311
  132.9 3.1 %near.1.near_ref = f32[1024,256]{1,0:T(8,128)S(1)} custom-call(bf16[1024,256]{1,0:T(8,128)(2,1)S(1)} %gate.1.g0, bf16[1024,256]{1,0:T(8,128)(2,1)S(1)} %collective-permute-done.16.g1, bf16[2,4,4,16,1024]{4,3,2,1,0:T(8,128)(2,1)S(1)} %copy-done.3, bf16[2,4,4,16,1024]{4,3,2,1,0:T(8,128)(2,1)} %collective-permute-done.7.left, ...), custom_call_target="tpu_custom_call" | custom-call | flops 34359738368 | bytes 6291456 | tf_op jit(solution)/shard_map/near/pallas_call | solution.py:286
  136.1 18.6 %collective-permute-done.15.g0 = bf16[1024,256]{1,0:T(8,128)(2,1)S(1)} collective-permute-done((bf16[1024,256]{1,0:T(8,128)(2,1)S(1)}, bf16[1024,256]{1,0:T(8,128)(2,1)S(1)}, u32[]{:S(2)}, u32[]{:S(2)}) %collective-permute-start.15) | collective-permute-done | bytes 524320 | tf_op jit(solution)/shard_map/ppermute | solution.py:363
  154.6 0.9 collective-permute-start.19
  155.6 0.1 pad_add_fusion.place_ref
  155.7 1.5 collective-permute-done.19.g1
  157.1 4.4 %far.1 = bf16[256,1024]{1,0:T(8,128)(2,1)} custom-call(s32[3]{0:T(128)S(1)} %pad_add_fusion.place_ref, bf16[1024,256]{1,0:T(8,128)(2,1)S(1)} %collective-permute-done.15.g0, bf16[1024,256]{1,0:T(8,128)(2,1)S(1)} %collective-permute-done.19.g1, bf16[2,4,4,16,1024]{4,3,2,1,0:T(8,128)(2,1)S(1)} %pad_maximum_fusion.1.own, ...), custom_call_target="tpu_custom_call" | custom-call | flops 34359738368 | bytes 6291456 | tf_op jit(solution)/shard_map/far/pallas_call | solution.py:286
  (42 shorter events, 0.3 us)
Async XLA Ops:
  0.0 12.6 %collective-permute-start.1 = (bf16[16,4096]{1,0:T(8,128)(2,1)}, bf16[16,4096]{1,0:T(8,128)(2,1)S(1)}, u32[]{:S(2)}, u32[]{:S(2)}) collective-permute-start(bf16[16,4096]{1,0:T(8,128)(2,1)} %param.16), channel_id=1, source_target_pairs={{0,32},{16,48},{32,0},{48,16},{1,33},{17,49},{33,1},{49,17},{2,34}... | collective-permute-start | bytes 393224 | tf_op jit(solution)/shard_map/ppermute | solution.py:326
  3.8 8.8 %collective-permute-start = (bf16[16,4096]{1,0:T(8,128)(2,1)}, bf16[16,4096]{1,0:T(8,128)(2,1)S(1)}, u32[]{:S(2)}, u32[]{:S(2)}) collective-permute-start(bf16[16,4096]{1,0:T(8,128)(2,1)} %param.16), channel_id=1, source_target_pairs={{0,16},{16,32},{32,48},{48,0},{1,17},{17,33},{33,49},{49,1},{2,18}... | collective-permute-start | bytes 393224 | tf_op jit(solution)/shard_map/ppermute | solution.py:326
  5.5 8.0 %collective-permute-start.2 = (bf16[16,4096]{1,0:T(8,128)(2,1)}, bf16[16,4096]{1,0:T(8,128)(2,1)S(1)}, u32[]{:S(2)}, u32[]{:S(2)}) collective-permute-start(bf16[16,4096]{1,0:T(8,128)(2,1)} %param.16), channel_id=1, source_target_pairs={{0,48},{16,0},{32,16},{48,32},{1,49},{17,1},{33,17},{49,33},{2,50}... | collective-permute-start | bytes 393224 | tf_op jit(solution)/shard_map/ppermute | solution.py:326
  13.4 13.1 %copy-start.8 = (bf16[16,4096]{1,0:T(8,128)(2,1)S(1)}, bf16[16,4096]{1,0:T(8,128)(2,1)}, u32[]{:S(2)}) copy-start(bf16[16,4096]{1,0:T(8,128)(2,1)} %param.16) | copy-start | bytes 393220
  13.4 73.8 %all-to-all-start = ((bf16[64,16,1280]{2,1,0:T(8,128)(2,1)}), bf16[64,16,1280]{2,1,0:T(8,128)(2,1)}, u32[]{:S(2)}, u32[]{:S(2)}) async-start(bf16[64,16,1280]{2,1,0:T(8,128)(2,1)} %bitcast.51), calls=%async_computation | async-start | bytes 5242880 | tf_op jit(solution)/shard_map/all_to_all | solution.py:342
  26.7 23.4 %collective-permute-start.5 = (bf16[2,4,16,1024]{3,2,1,0:T(8,128)(2,1)S(1)}, bf16[2,4,16,1024]{3,2,1,0:T(8,128)(2,1)S(1)}, u32[]{:S(2)}, u32[]{:S(2)}) collective-permute-start(bf16[2,4,16,1024]{3,2,1,0:T(8,128)(2,1)S(1)} %pad_maximum_fusion.3), channel_id=1, source_target_pairs={{0,192},{64,0},{128,64},{192,128},{1,193},{65,1},{129,65},{193,129... | collective-permute-start | bytes 786440 | tf_op jit(solution)/shard_map/ppermute | solution.py:307
  29.2 21.1 %collective-permute-start.11 = (bf16[2,4,16,1024]{3,2,1,0:T(8,128)(2,1)S(1)}, bf16[2,4,16,1024]{3,2,1,0:T(8,128)(2,1)S(1)}, u32[]{:S(2)}, u32[]{:S(2)}) collective-permute-start(bf16[2,4,16,1024]{3,2,1,0:T(8,128)(2,1)S(1)} %pad_maximum_fusion.4), channel_id=1, source_target_pairs={{0,12},{4,0},{8,4},{12,8},{1,13},{5,1},{9,5},{13,9},{2,14},{6,2},{... | collective-permute-start | bytes 786440 | tf_op jit(solution)/shard_map/ppermute | solution.py:307
  31.7 23.8 %collective-permute-start.3 = (bf16[2,4,16,1024]{3,2,1,0:T(8,128)(2,1)S(1)}, bf16[2,4,16,1024]{3,2,1,0:T(8,128)(2,1)S(1)}, u32[]{:S(2)}, u32[]{:S(2)}) collective-permute-start(bf16[2,4,16,1024]{3,2,1,0:T(8,128)(2,1)S(1)} %pad_maximum_fusion.3), channel_id=1, source_target_pairs={{0,64},{64,128},{128,192},{192,0},{1,65},{65,129},{129,193},{193,1... | collective-permute-start | bytes 786440 | tf_op jit(solution)/shard_map/ppermute | solution.py:307
  31.7 22.3 %collective-permute-start.9 = (bf16[2,4,16,1024]{3,2,1,0:T(8,128)(2,1)S(1)}, bf16[2,4,16,1024]{3,2,1,0:T(8,128)(2,1)S(1)}, u32[]{:S(2)}, u32[]{:S(2)}) collective-permute-start(bf16[2,4,16,1024]{3,2,1,0:T(8,128)(2,1)S(1)} %pad_maximum_fusion.4), channel_id=1, source_target_pairs={{0,4},{4,8},{8,12},{12,0},{1,5},{5,9},{9,13},{13,1},{2,6},{6,10},{... | collective-permute-start | bytes 786440 | tf_op jit(solution)/shard_map/ppermute | solution.py:307
  50.2 13.1 %collective-permute-start.6 = (bf16[4,16,1024]{2,1,0:T(8,128)(2,1)S(1)}, bf16[4,16,1024]{2,1,0:T(8,128)(2,1)S(1)}, u32[]{:S(2)}, u32[]{:S(2)}) collective-permute-start(bf16[4,16,1024]{2,1,0:T(8,128)(2,1)S(1)} %get-tuple-element.69), channel_id=1, source_target_pairs={{0,192},{64,0},{128,64},{192,128},{1,193},{65,1},{129,65},{193,129... | collective-permute-start | bytes 393224 | tf_op jit(solution)/shard_map/ppermute | solution.py:311
  50.3 7.8 %collective-permute-start.12 = (bf16[4,16,1024]{2,1,0:T(8,128)(2,1)S(1)}, bf16[4,16,1024]{2,1,0:T(8,128)(2,1)S(1)}, u32[]{:S(2)}, u32[]{:S(2)}) collective-permute-start(bf16[4,16,1024]{2,1,0:T(8,128)(2,1)S(1)} %get-tuple-element.63), channel_id=1, source_target_pairs={{0,12},{4,0},{8,4},{12,8},{1,13},{5,1},{9,5},{13,9},{2,14},{6,2},{... | collective-permute-start | bytes 393224 | tf_op jit(solution)/shard_map/ppermute | solution.py:311
  54.1 6.4 %collective-permute-start.10 = (bf16[4,16,1024]{2,1,0:T(8,128)(2,1)S(1)}, bf16[4,16,1024]{2,1,0:T(8,128)(2,1)S(1)}, u32[]{:S(2)}, u32[]{:S(2)}) collective-permute-start(bf16[4,16,1024]{2,1,0:T(8,128)(2,1)S(1)} %get-tuple-element.60), channel_id=1, source_target_pairs={{0,4},{4,8},{8,12},{12,0},{1,5},{5,9},{9,13},{13,1},{2,6},{6,10},{... | collective-permute-start | bytes 393224 | tf_op jit(solution)/shard_map/ppermute | solution.py:311
  55.6 7.7 %collective-permute-start.4 = (bf16[4,16,1024]{2,1,0:T(8,128)(2,1)S(1)}, bf16[4,16,1024]{2,1,0:T(8,128)(2,1)S(1)}, u32[]{:S(2)}, u32[]{:S(2)}) collective-permute-start(bf16[4,16,1024]{2,1,0:T(8,128)(2,1)S(1)} %get-tuple-element.66), channel_id=1, source_target_pairs={{0,64},{64,128},{128,192},{192,0},{1,65},{65,129},{129,193},{193,1... | collective-permute-start | bytes 393224 | tf_op jit(solution)/shard_map/ppermute | solution.py:311
  60.7 37.9 %collective-permute-start.14 = (bf16[2,4,4,16,1024]{4,3,2,1,0:T(8,128)(2,1)S(1)}, bf16[2,4,4,16,1024]{4,3,2,1,0:T(8,128)(2,1)}, u32[]{:S(2)}, u32[]{:S(2)}) collective-permute-start(bf16[2,4,4,16,1024]{4,3,2,1,0:T(8,128)(2,1)S(1)} %pad_maximum_fusion.1.own), channel_id=1, source_target_pairs={{0,192},{64,0},{128,64},{192,128},{1,193},{65,1},{129,65},{193,129... | collective-permute-start | bytes 3145736 | tf_op jit(solution)/shard_map/ppermute | solution.py:307
  63.3 35.3 %collective-permute-start.13 = (bf16[2,4,4,16,1024]{4,3,2,1,0:T(8,128)(2,1)S(1)}, bf16[2,4,4,16,1024]{4,3,2,1,0:T(8,128)(2,1)}, u32[]{:S(2)}, u32[]{:S(2)}) collective-permute-start(bf16[2,4,4,16,1024]{4,3,2,1,0:T(8,128)(2,1)S(1)} %pad_maximum_fusion.1.own), channel_id=1, source_target_pairs={{0,64},{64,128},{128,192},{192,0},{1,65},{65,129},{129,193},{193,1... | collective-permute-start | bytes 3145736 | tf_op jit(solution)/shard_map/ppermute | solution.py:307
  63.5 35.0 %copy-start.2 = (bf16[2,4,4,16,1024]{4,3,2,1,0:T(8,128)(2,1)}, bf16[2,4,4,16,1024]{4,3,2,1,0:T(8,128)(2,1)S(1)}, u32[]{:S(2)}) copy-start(bf16[2,4,4,16,1024]{4,3,2,1,0:T(8,128)(2,1)S(1)} %pad_maximum_fusion.own) | copy-start | bytes 3145732
  63.5 35.0 %collective-permute-start.8 = (bf16[2,4,4,16,1024]{4,3,2,1,0:T(8,128)(2,1)S(1)}, bf16[2,4,4,16,1024]{4,3,2,1,0:T(8,128)(2,1)}, u32[]{:S(2)}, u32[]{:S(2)}) collective-permute-start(bf16[2,4,4,16,1024]{4,3,2,1,0:T(8,128)(2,1)S(1)} %pad_maximum_fusion.own), channel_id=1, source_target_pairs={{0,12},{4,0},{8,4},{12,8},{1,13},{5,1},{9,5},{13,9},{2,14},{6,2},{... | collective-permute-start | bytes 3145736 | tf_op jit(solution)/shard_map/ppermute | solution.py:307
  66.7 31.9 %collective-permute-start.7 = (bf16[2,4,4,16,1024]{4,3,2,1,0:T(8,128)(2,1)S(1)}, bf16[2,4,4,16,1024]{4,3,2,1,0:T(8,128)(2,1)}, u32[]{:S(2)}, u32[]{:S(2)}) collective-permute-start(bf16[2,4,4,16,1024]{4,3,2,1,0:T(8,128)(2,1)S(1)} %pad_maximum_fusion.own), channel_id=1, source_target_pairs={{0,4},{4,8},{8,12},{12,0},{1,5},{5,9},{9,13},{13,1},{2,6},{6,10},{... | collective-permute-start | bytes 3145736 | tf_op jit(solution)/shard_map/ppermute | solution.py:307
  98.6 24.3 %copy-start = (bf16[256,1024]{1,0:T(8,128)(2,1)S(1)}, bf16[256,1024]{1,0:T(8,128)(2,1)}, u32[]{:S(2)}) copy-start(bf16[256,1024]{1,0:T(8,128)(2,1)} %k_ref.2) | copy-start | bytes 1572868
  98.6 24.3 %copy-start.1 = (bf16[256,1024]{1,0:T(8,128)(2,1)S(1)}, bf16[256,1024]{1,0:T(8,128)(2,1)}, u32[]{:S(2)}) copy-start(bf16[256,1024]{1,0:T(8,128)(2,1)} %v_ref.2) | copy-start | bytes 1572868
  98.6 24.3 %copy-start.4 = (bf16[256,1024]{1,0:T(8,128)(2,1)S(1)}, bf16[256,1024]{1,0:T(8,128)(2,1)}, u32[]{:S(2)}) copy-start(bf16[256,1024]{1,0:T(8,128)(2,1)} %q_ref) | copy-start | bytes 1572868
  98.6 24.3 %copy-start.5 = (f32[1024]{0:T(1024)S(1)}, f32[1024]{0:T(1024)}, u32[]{:S(2)}) copy-start(f32[1024]{0:T(1024)} %param.15) | copy-start | bytes 12292
  98.6 24.3 %all-to-all-start.1 = ((bf16[64,16,256]{2,1,0:T(8,128)(2,1)}), bf16[64,16,256]{2,1,0:T(8,128)(2,1)S(1)}, u32[]{:S(2)}, u32[]{:S(2)}) async-start(bf16[64,16,256]{2,1,0:T(8,128)(2,1)} %bitcast.53), calls=%async_computation.1 | async-start | bytes 1048576 | tf_op jit(solution)/shard_map/all_to_all | solution.py:342
  107.7 22.5 %collective-permute-start.18 = (bf16[4,4,16,1024]{3,2,1,0:T(8,128)(2,1)}, bf16[4,4,16,1024]{3,2,1,0:T(8,128)(2,1)}, u32[]{:S(2)}, u32[]{:S(2)}) collective-permute-start(bf16[4,4,16,1024]{3,2,1,0:T(8,128)(2,1)} %slice_bitcast_fusion), channel_id=1, source_target_pairs={{0,12},{4,0},{8,4},{12,8},{1,13},{5,1},{9,5},{13,9},{2,14},{6,2},{... | collective-permute-start | bytes 1572872 | tf_op jit(solution)/shard_map/ppermute | solution.py:311
  111.8 18.4 %collective-permute-start.17 = (bf16[4,4,16,1024]{3,2,1,0:T(8,128)(2,1)}, bf16[4,4,16,1024]{3,2,1,0:T(8,128)(2,1)}, u32[]{:S(2)}, u32[]{:S(2)}) collective-permute-start(bf16[4,4,16,1024]{3,2,1,0:T(8,128)(2,1)} %slice_bitcast_fusion.1), channel_id=1, source_target_pairs={{0,4},{4,8},{8,12},{12,0},{1,5},{5,9},{9,13},{13,1},{2,6},{6,10},{... | collective-permute-start | bytes 1572872 | tf_op jit(solution)/shard_map/ppermute | solution.py:311
  122.9 7.3 %copy-start.7 = (bf16[4,4,16,1024]{3,2,1,0:T(8,128)(2,1)S(1)}, bf16[4,4,16,1024]{3,2,1,0:T(8,128)(2,1)}, u32[]{:S(2)}) copy-start(bf16[4,4,16,1024]{3,2,1,0:T(8,128)(2,1)} %get-tuple-element.52) | copy-start | bytes 1572868
  122.9 7.4 %copy-start.6 = (bf16[4,4,16,1024]{3,2,1,0:T(8,128)(2,1)S(1)}, bf16[4,4,16,1024]{3,2,1,0:T(8,128)(2,1)}, u32[]{:S(2)}) copy-start(bf16[4,4,16,1024]{3,2,1,0:T(8,128)(2,1)} %get-tuple-element.53) | copy-start | bytes 1572868
  122.9 10.0 %copy-start.3 = (bf16[2,4,4,16,1024]{4,3,2,1,0:T(8,128)(2,1)S(1)}, bf16[2,4,4,16,1024]{4,3,2,1,0:T(8,128)(2,1)}, u32[]{:S(2)}) copy-start(bf16[2,4,4,16,1024]{4,3,2,1,0:T(8,128)(2,1)} %copy-done.2) | copy-start | bytes 3145732
  123.7 6.5 %collective-permute-start.16 = (bf16[1024,256]{1,0:T(8,128)(2,1)S(1)}, bf16[1024,256]{1,0:T(8,128)(2,1)S(1)}, u32[]{:S(2)}, u32[]{:S(2)}) collective-permute-start(bf16[1024,256]{1,0:T(8,128)(2,1)S(1)} %gate.1.g0), channel_id=1, source_target_pairs={{0,1},{1,0},{2,3},{3,2},{4,5},{5,4},{6,7},{7,6},{8,9},{9,8},{10,11... | collective-permute-start | bytes 1572872 | tf_op jit(solution)/shard_map/ppermute | solution.py:362
  125.9 28.7 %collective-permute-start.15 = (bf16[1024,256]{1,0:T(8,128)(2,1)S(1)}, bf16[1024,256]{1,0:T(8,128)(2,1)S(1)}, u32[]{:S(2)}, u32[]{:S(2)}) collective-permute-start(bf16[1024,256]{1,0:T(8,128)(2,1)S(1)} %gate.1.g0), channel_id=1, source_target_pairs={{0,2},{2,0},{1,3},{3,1},{4,6},{6,4},{5,7},{7,5},{8,10},{10,8},{9,1... | collective-permute-start | bytes 1572872 | tf_op jit(solution)/shard_map/ppermute | solution.py:363
  130.2 25.5 %collective-permute-start.20 = (bf16[4,4,16,1024]{3,2,1,0:T(8,128)(2,1)S(1)}, bf16[4,4,16,1024]{3,2,1,0:T(8,128)(2,1)S(1)}, u32[]{:S(2)}, u32[]{:S(2)}) collective-permute-start(bf16[4,4,16,1024]{3,2,1,0:T(8,128)(2,1)S(1)} %copy-done.7), channel_id=1, source_target_pairs={{0,64},{64,128},{128,192},{192,0},{1,65},{65,129},{129,193},{193,1... | collective-permute-start | bytes 1572872 | tf_op jit(solution)/shard_map/ppermute | solution.py:311
  130.3 25.4 %collective-permute-start.21 = (bf16[4,4,16,1024]{3,2,1,0:T(8,128)(2,1)S(1)}, bf16[4,4,16,1024]{3,2,1,0:T(8,128)(2,1)S(1)}, u32[]{:S(2)}, u32[]{:S(2)}) collective-permute-start(bf16[4,4,16,1024]{3,2,1,0:T(8,128)(2,1)S(1)} %copy-done.6), channel_id=1, source_target_pairs={{0,192},{64,0},{128,64},{192,128},{1,193},{65,1},{129,65},{193,129... | collective-permute-start | bytes 1572872 | tf_op jit(solution)/shard_map/ppermute | solution.py:311
  154.6 2.5 %collective-permute-start.19 = (bf16[1024,256]{1,0:T(8,128)(2,1)S(1)}, bf16[1024,256]{1,0:T(8,128)(2,1)S(1)}, u32[]{:S(2)}, u32[]{:S(2)}) collective-permute-start(bf16[1024,256]{1,0:T(8,128)(2,1)S(1)} %collective-permute-done.15.g0), channel_id=1, source_target_pairs={{0,1},{1,0},{2,3},{3,2},{4,5},{5,4},{6,7},{7,6},{8,9},{9,8},{10,11... | collective-permute-start | bytes 1572872 | tf_op jit(solution)/shard_map/ppermute | solution.py:369
